TPU v7x, 32 devices: a whole 2x2x4 slice. The times are simulated.
32 devices in a mesh: strip: 2 (over y), col: 4 (over z), row: 4 (over x, core).
Axes of the slice: x: 2, y: 2, z: 4, core: 2. Of those that a mesh axis runs over, the one named last changes fastest.
Arguments:
- left_features: bfloat16 [64, 2048, 128], P(('strip', 'row'), 'col'), parts along dimension 0, may hold values from -6 to 6
- right_features: bfloat16 [64, 2048, 128], P(('strip', 'row'), 'col'), parts along dimension 0, may hold values from -6 to 6
- conv_first: bfloat16 [3, 3, 256, 256], replicated, may hold values from -0.125 to 0.125
- conv_second: bfloat16 [3, 3, 256, 256], replicated, may hold values from -0.125 to 0.125
Outputs:
- cost_field: bfloat16 [64, 2048, 256], P(('strip', 'row'), 'col'), parts along dimension 0
There are 2 independent parts, one for each index of `strip`. A program takes and returns all parts, laid end to end along the dimension named above; an argument that names none is the same for every part. Nothing has to cross between parts.
All inputs are finite; a program needn't handle non-finite values.
Results may differ from a plain program's by a relative error of at most 0.0058.
Values may be sent and summed in bfloat16 or wider, within the bound.
No kernel may reach another device: no remote copies, remote signals or barrier semaphores. Data moves between devices by JAX's collectives and lax.ppermute only.
A program may use at most 128 MiB of HBM per device.

v0:
```python
import jax
import jax.numpy as jnp
from jax import lax
from jax.sharding import PartitionSpec as P


def passed_along(value, axis, steps):
    count = lax.axis_size(axis)
    initial, last = (max(0, -steps), min(count, count - steps))
    return lax.ppermute(value, axis, [(source, source + steps) for source in range(initial, last)])


def extended_2(block, sides, width):
    for axis, dim in sides:
        count = lax.axis_size(axis)
        forward = [(i, i + 1) for i in range(count - 1)]
        backward = [(target, source) for source, target in forward]
        low = lax.ppermute(
            lax.slice_in_dim(block, block.shape[dim] - width, None, axis=dim), axis, forward
        )
        high = lax.ppermute(lax.slice_in_dim(block, 0, width, axis=dim), axis, backward)
        block = jnp.concatenate([low, block, high], axis=dim)
    return block


def correlate(left_part, extended, disparities):
    row_count, col_count, chan_count = left_part.shape
    block_count = col_count // disparities
    left_blocks = left_part.reshape(row_count, block_count, disparities, chan_count)
    right_blocks = extended.reshape(row_count, block_count + 1, disparities, chan_count)
    windows = jnp.concatenate((right_blocks[:, :-1], right_blocks[:, 1:]), axis=2)
    scores = jnp.einsum("rjwc,rjvc->rjwv", left_blocks, windows, preferred_element_type=jnp.float32)
    scores = scores * (1.0 / jnp.sqrt(jnp.float32(chan_count)))
    flat_scores = scores.reshape(row_count, block_count, disparities * 2 * disparities)
    flat_scores = jnp.pad(flat_scores, ((0, 0), (0, 0), (0, disparities)))
    skewed = flat_scores.reshape(row_count, block_count, disparities, 2 * disparities + 1)
    banded = skewed[..., 1 : disparities + 1][..., ::-1]
    return banded.reshape(row_count, col_count, disparities).astype(jnp.bfloat16)


def convolve_valid(padded, kernel):
    result = lax.conv_general_dilated(
        padded[None],
        kernel,
        (1, 1),
        "VALID",
        dimension_numbers=("NHWC", "HWIO", "NHWC"),
        preferred_element_type=jnp.float32,
    )
    return result[0]


def local(left_features, right_features, conv_first, conv_second):
    disparities = conv_first.shape[2]
    earlier = passed_along(right_features[:, -disparities:], "col", 1)
    extended = jnp.concatenate((earlier, right_features), axis=1)
    volume = correlate(left_features, extended, disparities)
    padded = extended_2(volume, (("col", 1), ("row", 0)), 1)
    hidden = jax.nn.relu(convolve_valid(padded, conv_first)).astype(jnp.bfloat16)
    padded_hidden = extended_2(hidden, (("col", 1), ("row", 0)), 1)
    result = jax.nn.relu(convolve_valid(padded_hidden, conv_second)).astype(jnp.bfloat16)
    return result


def solution(mesh):
    in_specs = (P(("strip", "row"), "col", None), P(("strip", "row"), "col", None), P(), P())
    out_specs = P(("strip", "row"), "col", None)
    return jax.shard_map(local, mesh=mesh, in_specs=in_specs, out_specs=out_specs, check_vma=False)
```

profile of v0, /device:TPU:1, one launch (start us, length us, event | category | flops | bytes accessed | tf_op | source)
XLA Modules:
  0.0 145.7 jit_solution(355283094916841175)
XLA Ops:
  1.2 4.1 %collective-permute-start = (bf16[8,256,128]{2,1,0:T(8,128)(2,1)S(1)}, bf16[8,256,128]{2,1,0:T(8,128)(2,1)S(1)}, u32[]{:S(2)}, u32[]{:S(2)}) collective-permute-start(bf16[8,256,128]{2,1,0:T(8,128)(2,1)S(1)} %slice.36), channel_id=1, source_target_pairs={{0,4},{4,8},{8,12},{1,5},{5,9},{9,13},{2,6},{6,10},{10,14},{3,7},{... | collective-permute-start | bytes 1572872 | tf_op jit(solution)/shard_map/ppermute | solution.py:10
  5.3 10.5 %collective-permute-done = bf16[8,256,128]{2,1,0:T(8,128)(2,1)S(1)} collective-permute-done((bf16[8,256,128]{2,1,0:T(8,128)(2,1)S(1)}, bf16[8,256,128]{2,1,0:T(8,128)(2,1)S(1)}, u32[]{:S(2)}, u32[]{:S(2)}) %collective-permute-start) | collective-permute-done | bytes 524320 | tf_op jit(solution)/shard_map/ppermute | solution.py:10
  18.4 3.2 %multiply_bitcast_fusion = bf16[8,2,256,512]{2,3,1,0:T(8,128)(2,1)} fusion(bf16[8,2,256,128]{3,2,1,0:T(8,128)(2,1)S(1)} %bitcast.46, bf16[8,2,256,128]{3,2,1,0:T(8,128)(2,1)S(1)} %get-tuple-element.14, bf16[8,2,256,128]{3,2,1,0:T(8,128)(2,1)S(1)} %get-tuple-element.13), kind=kOutput, calls=%fused_computation | convolution fusion | flops 545259520 | bytes 7340032 | tf_op jit(solution)/shard_map/rjwc,rjvc->rjwv/dot_general | solution.py:32
  21.6 6.2 %copy.24 = bf16[8,2,256,512]{3,2,0,1:T(8,128)(2,1)} copy(bf16[8,2,256,512]{2,3,1,0:T(8,128)(2,1)} %multiply_bitcast_fusion) | data formatting | bytes 8388608 | tf_op jit(solution)/shard_map/mul | solution.py:33
  27.8 4.9 %reshape.22 = bf16[8,2,131072]{2,0,1:T(8,128)(2,1)} reshape(bf16[8,2,256,512]{3,2,0,1:T(8,128)(2,1)} %copy.24) | data formatting | bytes 8388608 | tf_op jit(solution)/shard_map/reshape | solution.py:34
  32.7 3.7 %pad.4 = bf16[8,2,131328]{2,0,1:T(8,128)(2,1)} pad(bf16[8,2,131072]{2,0,1:T(8,128)(2,1)} %reshape.22, bf16[]{:T(256)} %constant.10), padding=0_0x0_0x0_256 | pad | bytes 8396802 | tf_op jit(solution)/shard_map/jit(_pad)/pad | solution.py:35
  36.4 13.3 %reshape.23 = bf16[8,2,256,513]{3,2,0,1:T(8,128)(2,1)} reshape(bf16[8,2,131328]{2,0,1:T(8,128)(2,1)} %pad.4) | data formatting | bytes 8404992 | tf_op jit(solution)/shard_map/reshape | solution.py:36
  49.7 2.9 %slice.54 = bf16[8,2,256,256]{3,2,0,1:T(8,128)(2,1)S(1)} slice(bf16[8,2,256,513]{3,2,0,1:T(8,128)(2,1)} %reshape.23), slice={[0:8], [0:2], [0:256], [1:257]} | slice | bytes 4194304 | tf_op jit(solution)/shard_map/slice | solution.py:37
  52.7 22.5 %rev.3 = bf16[8,2,256,256]{3,2,0,1:T(8,128)(2,1)} reverse(bf16[8,2,256,256]{3,2,0,1:T(8,128)(2,1)S(1)} %slice.54), dimensions={3} | reverse | bytes 4194304 | tf_op jit(solution)/shard_map/rev | solution.py:37
  76.9 4.1 %collective-permute-start.1 = (bf16[8,1,256]{2,1,0:T(2,128)(2,1)S(1)}, bf16[8,1,256]{2,1,0:T(2,128)(2,1)S(1)}, u32[]{:S(2)}, u32[]{:S(2)}) collective-permute-start(bf16[8,1,256]{2,1,0:T(2,128)(2,1)S(1)} %get-tuple-element.11), channel_id=1, source_target_pairs={{0,4},{4,8},{8,12},{1,5},{5,9},{9,13},{2,6},{6,10},{10,14},{3,7},{... | collective-permute-start | bytes 12296 | tf_op jit(solution)/shard_map/ppermute | solution.py:18
  82.3 3.1 %collective-permute-done.2 = bf16[8,1,256]{2,1,0:T(2,128)(2,1)S(1)} collective-permute-done((bf16[8,1,256]{2,1,0:T(2,128)(2,1)S(1)}, bf16[8,1,256]{2,1,0:T(2,128)(2,1)S(1)}, u32[]{:S(2)}, u32[]{:S(2)}) %collective-permute-start.2) | collective-permute-done | bytes 4128 | tf_op jit(solution)/shard_map/ppermute | solution.py:21
  85.5 6.0 %collective-permute-start.3 = (bf16[1,514,256]{2,1,0:T(8,128)(2,1)S(1)}, bf16[1,514,256]{2,1,0:T(8,128)(2,1)S(1)}, u32[]{:S(2)}, u32[]{:S(2)}) collective-permute-start(bf16[1,514,256]{2,1,0:T(8,128)(2,1)S(1)} %get-tuple-element.5), channel_id=1, source_target_pairs={{0,1},{1,2},{2,3},{4,5},{5,6},{6,7},{8,9},{9,10},{10,11},{12,13},{... | collective-permute-start | bytes 789512 | tf_op jit(solution)/shard_map/ppermute | solution.py:18
  91.5 2.1 %collective-permute-start.4 = (bf16[1,514,256]{2,1,0:T(8,128)(2,1)S(1)}, bf16[1,514,256]{2,1,0:T(8,128)(2,1)S(1)}, u32[]{:S(2)}, u32[]{:S(2)}) collective-permute-start(bf16[1,514,256]{2,1,0:T(8,128)(2,1)S(1)} %get-tuple-element.6), channel_id=1, source_target_pairs={{1,0},{2,1},{3,2},{5,4},{6,5},{7,6},{9,8},{10,9},{11,10},{13,12},{... | collective-permute-start | bytes 789512 | tf_op jit(solution)/shard_map/ppermute | solution.py:21
  94.9 4.4 %collective-permute-done.4 = bf16[1,514,256]{2,1,0:T(8,128)(2,1)S(1)} collective-permute-done((bf16[1,514,256]{2,1,0:T(8,128)(2,1)S(1)}, bf16[1,514,256]{2,1,0:T(8,128)(2,1)S(1)}, u32[]{:S(2)}, u32[]{:S(2)}) %collective-permute-start.4) | collective-permute-done | bytes 263200 | tf_op jit(solution)/shard_map/ppermute | solution.py:21
  101.8 5.1 %reshape.26 = bf16[10,1,8,65,256]{4,3,2,0,1:T(8,128)(2,1)} reshape(bf16[10,1,520,256]{3,2,0,1:T(8,128)(2,1)} %pad.5) | data formatting | bytes 5324800 | tf_op jit(solution)/shard_map/conv_general_dilated | solution.py:42
  106.9 2.4 %copy.27 = bf16[10,1,8,65,256]{4,2,3,0,1:T(8,128)(2,1)S(1)} copy(bf16[10,1,8,65,256]{4,3,2,0,1:T(8,128)(2,1)} %reshape.26) | data formatting | bytes 5324800 | tf_op jit(solution)/shard_map/conv_general_dilated | solution.py:42
  109.4 5.4 %maximum_convert_fusion.1 = bf16[8,8,65,256]{3,1,2,0:T(8,128)(2,1)S(1)} fusion(pred[8,65]{0,1:T(8,128)(4,1)S(1)} %copy-done.4, bf16[3,3,256,256]{3,2,1,0:T(8,128)(2,1)S(1)} %copy-done, bf16[10,1,7,2,256]{4,2,3,0,1:T(8,128)(2,1)S(1)} %slice.57, bf16[10,1,8,65,256]{4,2,3,0,1:T(8,128)(2,1)S(1)} %copy.27), kind=kOutput, calls=%fused_computation.5 | convolution fusion | flops 4918763520 | bytes 6044168 | tf_op jit(solution)/shard_map/conv_general_dilated | solution.py:42
  115.3 3.2 %collective-permute-start.5 = (bf16[8,1,256]{2,0,1:T(8,128)(2,1)S(1)}, bf16[8,1,256]{2,0,1:T(8,128)(2,1)S(1)}, u32[]{:S(2)}, u32[]{:S(2)}) collective-permute-start(bf16[8,1,256]{2,0,1:T(8,128)(2,1)S(1)} %get-tuple-element.9), channel_id=1, source_target_pairs={{0,4},{4,8},{8,12},{1,5},{5,9},{9,13},{2,6},{6,10},{10,14},{3,7},{... | collective-permute-start | bytes 12296 | tf_op jit(solution)/shard_map/ppermute | solution.py:18
  119.9 3.0 %collective-permute-done.6 = bf16[8,1,256]{2,0,1:T(8,128)(2,1)S(1)} collective-permute-done((bf16[8,1,256]{2,0,1:T(8,128)(2,1)S(1)}, bf16[8,1,256]{2,0,1:T(8,128)(2,1)S(1)}, u32[]{:S(2)}, u32[]{:S(2)}) %collective-permute-start.6) | collective-permute-done | bytes 4128 | tf_op jit(solution)/shard_map/ppermute | solution.py:21
  123.8 1.9 %collective-permute-start.8 = (bf16[1,514,256]{2,1,0:T(8,128)(2,1)S(1)}, bf16[1,514,256]{2,1,0:T(8,128)(2,1)S(1)}, u32[]{:S(2)}, u32[]{:S(2)}) collective-permute-start(bf16[1,514,256]{2,1,0:T(8,128)(2,1)S(1)} %copy.30), channel_id=1, source_target_pairs={{1,0},{2,1},{3,2},{5,4},{6,5},{7,6},{9,8},{10,9},{11,10},{13,12},{... | collective-permute-start | bytes 789512 | tf_op jit(solution)/shard_map/ppermute | solution.py:21
  125.8 3.9 %collective-permute-start.7 = (bf16[1,514,256]{2,1,0:T(8,128)(2,1)S(1)}, bf16[1,514,256]{2,1,0:T(8,128)(2,1)S(1)}, u32[]{:S(2)}, u32[]{:S(2)}) collective-permute-start(bf16[1,514,256]{2,1,0:T(8,128)(2,1)S(1)} %copy.29), channel_id=1, source_target_pairs={{0,1},{1,2},{2,3},{4,5},{5,6},{6,7},{8,9},{9,10},{10,11},{12,13},{... | collective-permute-start | bytes 789512 | tf_op jit(solution)/shard_map/ppermute | solution.py:18
  129.6 1.9 %collective-permute-done.8 = bf16[1,514,256]{2,1,0:T(8,128)(2,1)S(1)} collective-permute-done((bf16[1,514,256]{2,1,0:T(8,128)(2,1)S(1)}, bf16[1,514,256]{2,1,0:T(8,128)(2,1)S(1)}, u32[]{:S(2)}, u32[]{:S(2)}) %collective-permute-start.8) | collective-permute-done | bytes 263200 | tf_op jit(solution)/shard_map/ppermute | solution.py:21
  133.2 3.0 %maximum_bitcast_fusion = bf16[10,1,514,256]{3,0,2,1:T(8,128)(2,1)S(1)} fusion(bf16[1,514,256]{2,0,1:T(2,128)(2,1)S(1)} %copy.32, bf16[8,1,256]{2,0,1:T(8,128)(2,1)S(1)} %collective-permute-done.6, bf16[8,512,256]{2,0,1:T(8,128)(2,1)S(1)} %slice_bitcast_fusion.1, bf16[8,1,256]{2,0,1:T(8,128)(2,1)S(1)} %collective-permute-done.5, bf16[1,514,256]{2,0,1:T(2,128)(2,1)S(1)} %copy.31), kind=kLoop, calls=%fused_computation.6 | loop fusion | flops 13158400 | bytes 5263360 | tf_op jit(solution)/shard_map/broadcast_in_dim | solution.py:43
  138.0 5.4 %maximum_convert_fusion = bf16[8,8,65,256]{3,1,2,0:T(8,128)(2,1)S(1)} fusion(pred[8,65]{0,1:T(8,128)(4,1)S(1)} %copy-done.4, bf16[3,3,256,256]{3,2,1,0:T(8,128)(2,1)S(1)} %copy-done.2, bf16[10,1,7,2,256]{4,2,3,0,1:T(8,128)(2,1)S(1)} %slice.61, bf16[10,1,8,65,256]{4,2,3,0,1:T(8,128)(2,1)S(1)} %copy.35), kind=kOutput, calls=%fused_computation.4 | convolution fusion | flops 4918763520 | bytes 6044168 | tf_op jit(solution)/shard_map/conv_general_dilated | solution.py:42
  (39 shorter events, 19.2 us)
Async XLA Ops:
  0.0 109.3 %copy-start = (bf16[3,3,256,256]{3,2,1,0:T(8,128)(2,1)S(1)}, bf16[3,3,256,256]{3,2,1,0:T(8,128)(2,1)}, u32[]{:S(2)}) copy-start(bf16[3,3,256,256]{3,2,1,0:T(8,128)(2,1)} %param.6) | copy-start | bytes 3538948
  1.2 14.6 %collective-permute-start = (bf16[8,256,128]{2,1,0:T(8,128)(2,1)S(1)}, bf16[8,256,128]{2,1,0:T(8,128)(2,1)S(1)}, u32[]{:S(2)}, u32[]{:S(2)}) collective-permute-start(bf16[8,256,128]{2,1,0:T(8,128)(2,1)S(1)} %slice.36), channel_id=1, source_target_pairs={{0,4},{4,8},{8,12},{1,5},{5,9},{9,13},{2,6},{6,10},{10,14},{3,7},{... | collective-permute-start | bytes 1572872 | tf_op jit(solution)/shard_map/ppermute | solution.py:10
  17.1 1.2 copy-start.3
  76.9 5.4 %collective-permute-start.1 = (bf16[8,1,256]{2,1,0:T(2,128)(2,1)S(1)}, bf16[8,1,256]{2,1,0:T(2,128)(2,1)S(1)}, u32[]{:S(2)}, u32[]{:S(2)}) collective-permute-start(bf16[8,1,256]{2,1,0:T(2,128)(2,1)S(1)} %get-tuple-element.11), channel_id=1, source_target_pairs={{0,4},{4,8},{8,12},{1,5},{5,9},{9,13},{2,6},{6,10},{10,14},{3,7},{... | collective-permute-start | bytes 12296 | tf_op jit(solution)/shard_map/ppermute | solution.py:18
  81.0 4.4 %collective-permute-start.2 = (bf16[8,1,256]{2,1,0:T(2,128)(2,1)S(1)}, bf16[8,1,256]{2,1,0:T(2,128)(2,1)S(1)}, u32[]{:S(2)}, u32[]{:S(2)}) collective-permute-start(bf16[8,1,256]{2,1,0:T(2,128)(2,1)S(1)} %get-tuple-element.12), channel_id=1, source_target_pairs={{4,0},{8,4},{12,8},{5,1},{9,5},{13,9},{6,2},{10,6},{14,10},{7,3},{... | collective-permute-start | bytes 12296 | tf_op jit(solution)/shard_map/ppermute | solution.py:21
  85.5 9.3 %collective-permute-start.3 = (bf16[1,514,256]{2,1,0:T(8,128)(2,1)S(1)}, bf16[1,514,256]{2,1,0:T(8,128)(2,1)S(1)}, u32[]{:S(2)}, u32[]{:S(2)}) collective-permute-start(bf16[1,514,256]{2,1,0:T(8,128)(2,1)S(1)} %get-tuple-element.5), channel_id=1, source_target_pairs={{0,1},{1,2},{2,3},{4,5},{5,6},{6,7},{8,9},{9,10},{10,11},{12,13},{... | collective-permute-start | bytes 789512 | tf_op jit(solution)/shard_map/ppermute | solution.py:18
  91.5 7.7 %collective-permute-start.4 = (bf16[1,514,256]{2,1,0:T(8,128)(2,1)S(1)}, bf16[1,514,256]{2,1,0:T(8,128)(2,1)S(1)}, u32[]{:S(2)}, u32[]{:S(2)}) collective-permute-start(bf16[1,514,256]{2,1,0:T(8,128)(2,1)S(1)} %get-tuple-element.6), channel_id=1, source_target_pairs={{1,0},{2,1},{3,2},{5,4},{6,5},{7,6},{9,8},{10,9},{11,10},{13,12},{... | collective-permute-start | bytes 789512 | tf_op jit(solution)/shard_map/ppermute | solution.py:21
  106.9 2.5 %copy-start.4 = (pred[8,65]{0,1:T(8,128)(4,1)S(1)}, pred[8,65]{0,1:T(8,128)(4,1)}, u32[]{:S(2)}) copy-start(pred[8,65]{0,1:T(8,128)(4,1)} %constant.18) | copy-start | bytes 1564
  115.3 4.5 %collective-permute-start.5 = (bf16[8,1,256]{2,0,1:T(8,128)(2,1)S(1)}, bf16[8,1,256]{2,0,1:T(8,128)(2,1)S(1)}, u32[]{:S(2)}, u32[]{:S(2)}) collective-permute-start(bf16[8,1,256]{2,0,1:T(8,128)(2,1)S(1)} %get-tuple-element.9), channel_id=1, source_target_pairs={{0,4},{4,8},{8,12},{1,5},{5,9},{9,13},{2,6},{6,10},{10,14},{3,7},{... | collective-permute-start | bytes 12296 | tf_op jit(solution)/shard_map/ppermute | solution.py:18
  118.5 4.4 %collective-permute-start.6 = (bf16[8,1,256]{2,0,1:T(8,128)(2,1)S(1)}, bf16[8,1,256]{2,0,1:T(8,128)(2,1)S(1)}, u32[]{:S(2)}, u32[]{:S(2)}) collective-permute-start(bf16[8,1,256]{2,0,1:T(8,128)(2,1)S(1)} %get-tuple-element.10), channel_id=1, source_target_pairs={{4,0},{8,4},{12,8},{5,1},{9,5},{13,9},{6,2},{10,6},{14,10},{7,3},{... | collective-permute-start | bytes 12296 | tf_op jit(solution)/shard_map/ppermute | solution.py:21
  123.8 7.7 %collective-permute-start.8 = (bf16[1,514,256]{2,1,0:T(8,128)(2,1)S(1)}, bf16[1,514,256]{2,1,0:T(8,128)(2,1)S(1)}, u32[]{:S(2)}, u32[]{:S(2)}) collective-permute-start(bf16[1,514,256]{2,1,0:T(8,128)(2,1)S(1)} %copy.30), channel_id=1, source_target_pairs={{1,0},{2,1},{3,2},{5,4},{6,5},{7,6},{9,8},{10,9},{11,10},{13,12},{... | collective-permute-start | bytes 789512 | tf_op jit(solution)/shard_map/ppermute | solution.py:21
  125.8 7.0 %collective-permute-start.7 = (bf16[1,514,256]{2,1,0:T(8,128)(2,1)S(1)}, bf16[1,514,256]{2,1,0:T(8,128)(2,1)S(1)}, u32[]{:S(2)}, u32[]{:S(2)}) collective-permute-start(bf16[1,514,256]{2,1,0:T(8,128)(2,1)S(1)} %copy.29), channel_id=1, source_target_pairs={{0,1},{1,2},{2,3},{4,5},{5,6},{6,7},{8,9},{9,10},{10,11},{12,13},{... | collective-permute-start | bytes 789512 | tf_op jit(solution)/shard_map/ppermute | solution.py:18
  136.7 1.3 copy-start.2
  143.9 1.9 %copy-start.1 = (bf16[3,3,256,256]{3,2,1,0:T(8,128)(2,1)S(1)}, bf16[3,3,256,256]{3,2,1,0:T(8,128)(2,1)}, u32[]{:S(2)}) copy-start(bf16[3,3,256,256]{3,2,1,0:T(8,128)(2,1)} %param.6) | copy-start | bytes 3538948
where the time goes:
time: 147 us; the launch traced here: 146 us
  local copies, waits for them, and re-layouts  72.5 us (49%)
  starting transfers between devices  27.8 us (19%)
  waiting for transfers between devices  25 us (17%)
  matrix products  14 us (10%)
  other arithmetic  6.12 us (4%)
    rev x1, local copies, waits for them, and re-layouts, correlate(): banded = skewed[..., 1:disparities + 1][..., ::-1]  22.5 us
    ppermute x4, starting transfers between devices, extended_2(): lax.ppermute(lax.slice_in_dim(block, block.shape[dim] - width, None, axis...  17.2 us
    reshape x1, local copies, waits for them, and re-layouts, correlate(): flat_scores.reshape(row_count, block_count, disparities, 2 * disparities...  13.3 us
    ppermute x4, waiting for transfers between devices, extended_2(): lax.ppermute(lax.slice_in_dim(block, 0, width, axis=dim), axis, backward)  12.4 us
    conv_general_dilated x2, matrix products, convolve_valid(): lax.conv_general_dilated(padded[None], kernel, (1, 1), 'VALID', dimension...  10.8 us
    ppermute x1, waiting for transfers between devices, passed_along(): lax.ppermute(value, axis, [(source, source + steps) for source in range(i...  10.5 us
    conv_general_dilated x5, local copies, waits for them, and re-layouts, convolve_valid(): lax.conv_general_dilated(padded[None], kernel, (1, 1), 'VALID', dimension...  8.56 us
    ppermute x4, starting transfers between devices, extended_2(): lax.ppermute(lax.slice_in_dim(block, 0, width, axis=dim), axis, backward)  6.61 us
  transfers between devices with their start and end apart: 9, of which 7 were waited for; matrix products, arithmetic and copies ran while one was open for 0% of the time, Pallas kernels for 0%

commit v1 on v0

v1 whole, which is shorter than its diff:
```python
import functools

import jax
import jax.numpy as jnp
from jax import lax
from jax.experimental import pallas as pl
from jax.experimental.pallas import tpu as pltpu
from jax.sharding import PartitionSpec as P

BF = jnp.bfloat16
F32 = jnp.float32
HALO = 16


class Segment:
    def __init__(self, base, outs):
        self.base, self.outs = base, outs
        self.hid = outs + 16
        self.vol = outs + 32


def reversal(size):
    i = lax.broadcasted_iota(jnp.int32, (size, size), 0)
    j = lax.broadcasted_iota(jnp.int32, (size, size), 1)
    return jnp.where(i + j == size - 1, 1.0, 0.0).astype(BF)


def part_kernel(segments, ext, disp, *refs):
    if ext:
        (flags, l_any, r_any, a_any, b_any, zl_any, zr_any, ca_any, cb_any, k1_any, k2_any, _, out_any,
         lbuf, rbuf, rrev, vf, vs, hf, hs, obuf, k1, k2, sems, ksems, osems) = refs
        pad = HALO
        lpad = disp + HALO
    else:
        (flags, l_any, r_any, a_any, b_any, k1_any, k2_any, out_any,
         lbuf, rbuf, rrev, vf, vs, hf, hs, obuf, k1, k2, sems, ksems, osems) = refs
        pad = 0
        lpad = 0
    rows, cols, chans = l_any.shape
    scale = 1.0 / (chans ** 0.5)
    odd = flags[0] == 1

    def copies(group):
        def own():
            lo, n = (0, rows // 2) if group == 1 else (rows // 2, rows - rows // 2)
            src, dst = pl.ds(lo, n), pl.ds(lo + 2, n)
            out = [
                (l_any.at[src], lbuf.at[dst, pl.ds(pad, cols)], sems.at[group]),
                (r_any.at[src], rbuf.at[dst, pl.ds(lpad, cols)], sems.at[group]),
            ]
            if ext:
                out += edges(zl_any.at[src], zr_any.at[src], dst)
            return out

        def edges(zl, zr, dst):
            return [
                (zl.at[:, pl.ds(0, lpad)], rbuf.at[dst, pl.ds(0, lpad)], sems.at[group]),
                (zl.at[:, pl.ds(lpad, pad)], lbuf.at[dst, pl.ds(0, pad)], sems.at[group]),
                (zr.at[:, pl.ds(0, pad)], rbuf.at[dst, pl.ds(lpad + cols, pad)], sems.at[group]),
                (zr.at[:, pl.ds(pad, pad)], lbuf.at[dst, pl.ds(pad + cols, pad)], sems.at[group]),
            ]

        def rim(main, corner):
            dst = pl.ds(0 if group == 0 else rows + 2, 2)
            out = [
                (main.at[:, pl.ds(0, cols)], lbuf.at[dst, pl.ds(pad, cols)], sems.at[group]),
                (main.at[:, pl.ds(cols, cols)], rbuf.at[dst, pl.ds(lpad, cols)], sems.at[group]),
            ]
            if ext:
                out += edges(corner.at[:, pl.ds(0, lpad + pad)], corner.at[:, pl.ds(lpad + pad, 2 * pad)], dst)
            return out

        if group in (1, 2):
            return own(), own()
        first = rim(a_any, ca_any if ext else None)
        second = rim(b_any, cb_any if ext else None)
        return (first, second) if group == 0 else (second, first)

    for group in range(4):
        if_odd, if_even = copies(group)
        if group in (1, 2):
            for c in if_odd:
                pltpu.make_async_copy(*c).start()
        else:
            @pl.when(odd)
            def _():
                for c in if_odd:
                    pltpu.make_async_copy(*c).start()

            @pl.when(jnp.logical_not(odd))
            def _():
                for c in if_even:
                    pltpu.make_async_copy(*c).start()
        if group == 0:
            k1_copy = pltpu.make_async_copy(k1_any, k1, ksems.at[0])
            k1_copy.start()
    k2_copy = pltpu.make_async_copy(k2_any, k2, ksems.at[1])
    k2_copy.start()

    def group_of(row):
        return 0 if row < 2 else 3 if row >= rows + 2 else 1 if row < 2 + rows // 2 else 2

    waited = set()

    def wait_rows(row):
        g = group_of(row)
        if g not in waited:
            waited.add(g)
            for c in copies(g)[0]:
                pltpu.make_async_copy(*c).wait()

    flip = reversal(128)

    def volume_rows(row):
        wait_rows(row)
        wait_rows(row + 1)
        dst_off = 0
        for s, seg in enumerate(segments):
            blocks = -(-seg.vol // 128)
            span = 128 * blocks + disp
            start = seg.base - disp + lpad
            have = seg.vol + disp
            for t in range(-(-have // 128)):
                n = min(128, have - 128 * t)
                both = jnp.concatenate([rbuf[row + q, start + 128 * t:start + 128 * t + n, :] for q in range(2)], axis=1)
                j = flip if n == 128 else reversal(n)
                res = jnp.dot(j, both, preferred_element_type=F32).astype(BF)
                for q in range(2):
                    rrev[s, row % 4 + q, span - 128 * t - n:span - 128 * t, :] = res[:, chans * q:chans * (q + 1)]
            for q in range(2):
                slot = row % 4 + q
                for b in range(blocks):
                    n = min(128, seg.vol - 128 * b)
                    u = 128 * (blocks - 1 - b)
                    left = lbuf[row + q, seg.base + pad + 128 * b:seg.base + pad + 128 * b + n, :]
                    scores = lax.dot_general(left, rrev[s, slot, u:u + 128 + disp, :], (((1,), (1,)), ((), ())),
                                             preferred_element_type=F32) * scale
                    rolled = pltpu.roll(scores, 1, 1, stride=1, stride_axis=0)
                    for h in range(disp // 128):
                        vf[slot, h, dst_off + 128 * b:dst_off + 128 * b + n, :] = rolled[:, 128 * (h + 1):128 * (h + 2)]
            dst_off += seg.vol
        for q in range(2):
            slot = row % 4 + q
            src, dst = 0, 0
            for seg in segments:
                for b in range(3):
                    for h in range(disp // 128):
                        vs[row + q, dst:dst + seg.hid, disp * b + 128 * h:disp * b + 128 * (h + 1)] = (
                            vf[slot, h, pl.ds(src + 14 + b, seg.hid), :].astype(BF))
                src += seg.vol
                dst += seg.hid

    def conv(src, row, kernel, count):
        m, k = src.shape[1], src.shape[2]
        x = jnp.concatenate([src[row + a:row + a + count].reshape(count * m, k) for a in range(3)], axis=1)
        return jnp.maximum(jnp.dot(x, kernel[...], preferred_element_type=F32), 0.0)

    m_hid = sum(seg.hid for seg in segments)
    m_out = sum(seg.outs for seg in segments)

    def hidden_rows(row, count):
        res = conv(vs, row, k1, count)
        for q in range(count):
            slot = (row + q) % 4
            one = res[q * m_hid:(q + 1) * m_hid]
            if row + q == 0:
                one = one * flags[1].astype(F32)
            if row + q == rows + 1:
                one = one * flags[2].astype(F32)
            for h in range(disp // 128):
                hf[slot, h] = one[:, 128 * h:128 * (h + 1)]
            src, dst = 0, 0
            for seg in segments:
                for edge, flag in ((-1, flags[3]), (cols, flags[4])):
                    pos = edge - (seg.base + 15)
                    if 0 <= pos < seg.outs + 2:
                        at = src + pos // 8 * 8
                        keep = lax.broadcasted_iota(jnp.int32, (8, 128), 0) != pos % 8
                        keep = jnp.where(keep, 1.0, flag.astype(F32))
                        for h in range(disp // 128):
                            hf[slot, h, at:at + 8, :] = hf[slot, h, at:at + 8, :] * keep
                for b in range(3):
                    for h in range(disp // 128):
                        hs[row + q, dst:dst + seg.outs, disp * b + 128 * h:disp * b + 128 * (h + 1)] = (
                            hf[slot, h, pl.ds(src + b, seg.outs), :].astype(BF))
                src += seg.hid
                dst += seg.outs

    pending = []

    def out_rows(row, count):
        res = conv(hs, row, k2, count).astype(BF)
        obuf[row:row + count] = res.reshape(count, m_out, disp)
        src = 0
        for s, seg in enumerate(segments):
            c = pltpu.make_async_copy(
                obuf.at[pl.ds(row, count), pl.ds(src, seg.outs)],
                out_any.at[pl.ds(row, count), pl.ds(seg.base + 16, seg.outs)], osems.at[row, s])
            c.start()
            pending.append(c)
            src += seg.outs

    volume_rows(0)
    volume_rows(2)
    k1_copy.wait()
    step = 2
    for row in range(0, rows + 2, step):
        if row + 4 < rows + 4:
            volume_rows(row + 4)
        hidden_rows(row, step)
        if row == 2:
            k2_copy.wait()
        if row >= 4:
            out_rows(row - 4, step)
    out_rows(rows - 2, step)
    for c in pending:
        c.wait()


def part_call(segments, ext, disp, rows, cols, chans, out_shape, operands):
    m_vol = sum(s.vol for s in segments)
    m_hid = sum(s.hid for s in segments)
    m_out = sum(s.outs for s in segments)
    pad = HALO if ext else 0
    span = max(128 * -(-s.vol // 128) + disp for s in segments)
    scratch = [
        pltpu.VMEM((rows + 4, cols + 2 * pad, chans), BF),
        pltpu.VMEM((rows + 4, cols + 2 * pad + (disp if ext else 0), chans), BF),
        pltpu.VMEM((len(segments), 4, span, chans), BF),
        pltpu.VMEM((4, disp // 128, m_vol, 128), F32),
        pltpu.VMEM((rows + 4, m_hid, 3 * disp), BF),
        pltpu.VMEM((4, disp // 128, m_hid, 128), F32),
        pltpu.VMEM((rows + 2, m_out, 3 * disp), BF),
        pltpu.VMEM((rows, m_out, disp), BF),
        pltpu.VMEM((9 * disp, disp), BF),
        pltpu.VMEM((9 * disp, disp), BF),
        pltpu.SemaphoreType.DMA((4,)),
        pltpu.SemaphoreType.DMA((2,)),
        pltpu.SemaphoreType.DMA((rows, len(segments))),
    ]
    flops = 2 * 9 * disp * disp * ((rows + 2) * m_hid + rows * m_out)
    return pl.pallas_call(
        functools.partial(part_kernel, segments, ext, disp),
        out_shape=out_shape,
        in_specs=[pl.BlockSpec(memory_space=pltpu.SMEM)] + [pl.BlockSpec(memory_space=pl.ANY)] * (len(operands) - 1),
        out_specs=pl.BlockSpec(memory_space=pl.ANY),
        scratch_shapes=scratch,
        input_output_aliases={len(operands) - 1: 0} if ext else {},
        compiler_params=pltpu.CompilerParams(vmem_limit_bytes=44 << 20),
        cost_estimate=pl.CostEstimate(flops=flops, bytes_accessed=6 << 20, transcendentals=0),
    )(*operands)


def pair_permute(x, axis, first):
    n = lax.axis_size(axis)
    perm = []
    for i in range(first, n - 1, 2):
        perm += [(i, i + 1), (i + 1, i)]
    return lax.ppermute(x, axis, perm)


def local(left, right, conv_first, conv_second):
    rows, cols, chans = left.shape
    disp = conv_first.shape[2]
    n_row, n_col = lax.axis_size("row"), lax.axis_size("col")
    ri, ci = lax.axis_index("row"), lax.axis_index("col")
    odd = ri % 2
    flags = jnp.stack([odd, (ri > 0).astype(jnp.int32), (ri < n_row - 1).astype(jnp.int32),
                       (ci > 0).astype(jnp.int32), (ci < n_col - 1).astype(jnp.int32)]).astype(jnp.int32)
    k1 = conv_first.reshape(9 * disp, disp)
    k2 = conv_second.reshape(9 * disp, disp)

    zl_msg = jnp.concatenate([right[:, cols - disp - HALO:], left[:, cols - HALO:]], axis=1)
    zl = lax.ppermute(zl_msg, "col", [(i, i + 1) for i in range(n_col - 1)])

    a_at = jnp.where(odd == 1, 0, rows - 2)
    b_at = jnp.where(odd == 1, rows - 2, 0)

    def facing(at, arrays):
        return jnp.concatenate([lax.dynamic_slice_in_dim(x, at, 2, 0) for x in arrays], axis=1)

    b = pair_permute(facing(b_at, (left, right)), "row", 1)
    a = pair_permute(facing(a_at, (left, right)), "row", 0)
    zr_msg = jnp.concatenate([right[:, :HALO], left[:, :HALO]], axis=1)
    zr = lax.ppermute(zr_msg, "col", [(i + 1, i) for i in range(n_col - 1)])

    out_shape = jax.ShapeDtypeStruct((rows, cols, disp), BF)
    mid = [Segment(disp, cols - disp - 2 * HALO)]
    out = part_call(mid, False, disp, rows, cols, chans, out_shape, (flags, left, right, a, b, k1, k2))

    cb = pair_permute(facing(b_at, (zl, zr)), "row", 1)
    ca = pair_permute(facing(a_at, (zl, zr)), "row", 0)
    rest = [Segment(-HALO, disp + HALO), Segment(cols - 2 * HALO, HALO)]
    return part_call(rest, True, disp, rows, cols, chans, out_shape,
                     (flags, left, right, a, b, zl, zr, ca, cb, k1, k2, out))


def solution(mesh):
    spec = P(("strip", "row"), "col", None)
    return jax.shard_map(local, mesh=mesh, in_specs=(spec, spec, P(), P()), out_specs=spec, check_vma=False)
```

time: 147 us -> 54.5 us (0.37)
  local copies, waits for them, and re-layouts: 72.5 us -> 3.57 us
  Pallas kernels: 0 us -> 29.8 us
  waiting for transfers between devices: 25 us -> 4.02 us
  matrix products: 14 us -> 0 us
  starting transfers between devices: 27.8 us -> 13.9 us
  other arithmetic: 6.12 us -> 2.58 us
    pallas_call x0 -> x2, Pallas kernels: none -> 29.8 us  [part_call(): pl.pallas_call(functools.partial(part_kernel, segments, ext, disp), out_s...]
    rev x1 -> x0, local copies, waits for them, and re-layouts: 22.5 us -> none  [correlate(): banded = skewed[..., 1:disparities + 1][..., ::-1]]
    ppermute x9 -> x6, waiting for transfers between devices: 25 us -> 4.02 us  [the longest x1 4.01 us: local(): zl = lax.ppermute(zl_msg, 'col', [(i, i + 1) for i in range(n_col - 1)])]
    reshape x2 -> x0, local copies, waits for them, and re-layouts: 18.2 us -> none  [the longest x1 13.3 us: correlate(): flat_scores.reshape(row_count, block_count, disparities, 2 * disparities...]
    ppermute x9 -> x6, starting transfers between devices: 27.8 us -> 13.9 us  [the longest x4 8.59 us: pair_permute(): return lax.ppermute(x, axis, perm)]
    conv_general_dilated x2 -> x0, matrix products: 10.8 us -> none  [convolve_valid(): lax.conv_general_dilated(padded[None], kernel, (1, 1), 'VALID', dimension...]
    conv_general_dilated x5 -> x0, local copies, waits for them, and re-layouts: 8.56 us -> none  [convolve_valid(): lax.conv_general_dilated(padded[None], kernel, (1, 1), 'VALID', dimension...]
    mul x1 -> x0, local copies, waits for them, and re-layouts: 6.22 us -> none  [correlate(): scores = scores * (1.0 / jnp.sqrt(jnp.float32(chan_count)))]
  transfers between devices with their start and end apart: 9 -> 6, of which waited for: 7 -> 1; matrix products, arithmetic and copies ran while one was open for 0% -> 5% of each run, Pallas kernels for 0% -> 24%
where the time goes in v1:
time: 54.5 us; the launch traced here: 54.3 us
  Pallas kernels  29.8 us (55%)
  starting transfers between devices  13.9 us (26%)
  waiting for transfers between devices  4.02 us (7%)
  local copies, waits for them, and re-layouts  3.57 us (7%)
  other arithmetic  2.58 us (5%)
    pallas_call x2, Pallas kernels, part_call(): pl.pallas_call(functools.partial(part_kernel, segments, ext, disp), out_s...  29.8 us
    ppermute x4, starting transfers between devices, pair_permute(): return lax.ppermute(x, axis, perm)  8.59 us
    ppermute x1, starting transfers between devices, local(): zl = lax.ppermute(zl_msg, 'col', [(i, i + 1) for i in range(n_col - 1)])  4.05 us
    ppermute x1, waiting for transfers between devices, local(): zl = lax.ppermute(zl_msg, 'col', [(i, i + 1) for i in range(n_col - 1)])  4.01 us
    concatenate x4, other arithmetic, facing(): jnp.concatenate([lax.dynamic_slice_in_dim(x, at, 2, 0) for x in arrays],...  1.72 us
    ppermute x1, starting transfers between devices, local(): zr = lax.ppermute(zr_msg, 'col', [(i + 1, i) for i in range(n_col - 1)])  1.29 us
    unnamed x8, local copies, waits for them, and re-layouts  1.28 us
    dynamic_slice x3, local copies, waits for them, and re-layouts, facing(): lax.dynamic_slice_in_dim(x, at, 2, 0)  1.13 us
  transfers between devices with their start and end apart: 6, of which 1 were waited for; matrix products, arithmetic and copies ran while one was open for 5% of the time, Pallas kernels for 24%

profile of v1, /device:TPU:1, one launch (start us, length us, event | category | flops | bytes accessed | tf_op | source)
XLA Modules:
  0.0 54.3 jit_solution(12849766524105409031)
XLA Ops:
  0.0 0.8 %fusion = (bf16[8,16,128]{2,1,0:T(8,128)(2,1)S(1)}, bf16[8,16,128]{2,1,0:T(8,128)(2,1)S(1)}) fusion(bf16[8,512,128]{2,1,0:T(8,128)(2,1)} %refs_1_.3), kind=kLoop, calls=%fused_computation.14 | loop fusion | bytes 131072 | tf_op jit(solution)/shard_map/slice | solution.py:284
  0.9 0.2 slice-done
  1.1 0.9 %pad_maximum_fusion = bf16[8,288,128]{2,1,0:T(8,128)(2,1)} fusion(bf16[8,16,128]{2,1,0:T(8,128)(2,1)S(1)} %get-tuple-element.6, bf16[8,272,128]{2,1,0:T(8,128)(2,1)S(1)} %slice-done), kind=kLoop, calls=%fused_computation | loop fusion | flops 1179648 | bytes 1179648 | tf_op jit(solution)/shard_map/concatenate | solution.py:273
  1.9 4.1 %collective-permute-start.2 = (bf16[8,288,128]{2,1,0:T(8,128)(2,1)}, bf16[8,288,128]{2,1,0:T(8,128)(2,1)S(1)}, u32[]{:S(2)}, u32[]{:S(2)}) collective-permute-start(bf16[8,288,128]{2,1,0:T(8,128)(2,1)} %pad_maximum_fusion), channel_id=1, source_target_pairs={{0,4},{4,8},{8,12},{1,5},{5,9},{9,13},{2,6},{6,10},{10,14},{3,7},{... | collective-permute-start | bytes 1769480 | tf_op jit(solution)/shard_map/ppermute | solution.py:274
  6.0 1.3 %collective-permute-start.3 = (bf16[8,32,128]{2,1,0:T(8,128)(2,1)S(1)}, bf16[8,32,128]{2,1,0:T(8,128)(2,1)S(1)}, u32[]{:S(2)}, u32[]{:S(2)}) collective-permute-start(bf16[8,32,128]{2,1,0:T(8,128)(2,1)S(1)} %pad_maximum_fusion.5), channel_id=1, source_target_pairs={{4,0},{8,4},{12,8},{5,1},{9,5},{13,9},{6,2},{10,6},{14,10},{7,3},{... | collective-permute-start | bytes 196616 | tf_op jit(solution)/shard_map/ppermute | solution.py:285
  7.4 1.1 %constant_dynamic-slice_fusion.4 = (bf16[2,512,128]{2,1,0:T(8,128)(2,1)S(1)}, bf16[2,512,128]{2,1,0:T(8,128)(2,1)S(1)}, bf16[2,512,128]{2,1,0:T(8,128)(2,1)S(1)}, bf16[2,512,128]{2,1,0:T(8,128)(2,1)S(1)}) fusion(bf16[8,512,128]{2,1,0:T(8,128)(2,1)S(1)} %copy-done, s32[]{:T(128)S(6)} %select_n.24, s32[]{:T(128)S(6)} %select_n.23, bf16[8,512,128]{2,1,0:T(8,128)(2,1)} %refs_1_.3), kind=kLoop, calls=%fused_computation.10 | loop fusion | bytes 2097160 | tf_op jit(solution)/shard_map/dynamic_slice | solution.py:280
  8.5 0.8 %pad_maximum_fusion.1 = bf16[2,1024,128]{2,1,0:T(8,128)(2,1)} fusion(bf16[2,512,128]{2,1,0:T(8,128)(2,1)S(1)} %get-tuple-element.10, bf16[2,512,128]{2,1,0:T(8,128)(2,1)S(1)} %get-tuple-element.15), kind=kLoop, calls=%fused_computation.1 | loop fusion | flops 1048576 | bytes 1048576 | tf_op jit(solution)/shard_map/concatenate | solution.py:280
  9.3 1.0 %collective-permute-start = (bf16[2,1024,128]{2,1,0:T(8,128)(2,1)}, bf16[2,1024,128]{2,1,0:T(8,128)(2,1)}, u32[]{:S(2)}, u32[]{:S(2)}) collective-permute-start(bf16[2,1024,128]{2,1,0:T(8,128)(2,1)} %pad_maximum_fusion.1), channel_id=1, source_target_pairs={{0,1},{1,0},{2,3},{3,2},{4,5},{5,4},{6,7},{7,6},{8,9},{9,8},{10,11... | collective-permute-start | bytes 1572872 | tf_op jit(solution)/shard_map/ppermute | solution.py:259
  10.3 0.9 %pad_maximum_fusion.2 = bf16[2,1024,128]{2,1,0:T(8,128)(2,1)} fusion(bf16[2,512,128]{2,1,0:T(8,128)(2,1)S(1)} %get-tuple-element.9, bf16[2,512,128]{2,1,0:T(8,128)(2,1)S(1)} %get-tuple-element.16), kind=kLoop, calls=%fused_computation.2 | loop fusion | flops 1048576 | bytes 1048576 | tf_op jit(solution)/shard_map/concatenate | solution.py:280
  11.1 3.0 %collective-permute-start.1 = (bf16[2,1024,128]{2,1,0:T(8,128)(2,1)}, bf16[2,1024,128]{2,1,0:T(8,128)(2,1)}, u32[]{:S(2)}, u32[]{:S(2)}) collective-permute-start(bf16[2,1024,128]{2,1,0:T(8,128)(2,1)} %pad_maximum_fusion.2), channel_id=1, source_target_pairs={{1,2},{2,1},{5,6},{6,5},{9,10},{10,9},{13,14},{14,13},{17,18},{18,... | collective-permute-start | bytes 1572872 | tf_op jit(solution)/shard_map/ppermute | solution.py:259
  14.1 0.1 stack.39.refs_0_
  14.2 0.0 collective-permute-done.3.refs_6_
  14.2 4.0 %collective-permute-done.2.refs_5_ = bf16[8,288,128]{2,1,0:T(8,128)(2,1)S(1)} collective-permute-done((bf16[8,288,128]{2,1,0:T(8,128)(2,1)}, bf16[8,288,128]{2,1,0:T(8,128)(2,1)S(1)}, u32[]{:S(2)}, u32[]{:S(2)}) %collective-permute-start.2) | collective-permute-done | bytes 589856 | tf_op jit(solution)/shard_map/ppermute | solution.py:274
  18.3 1.6 %collective-permute-start.4 = (bf16[2,320,128]{2,1,0:T(8,128)(2,1)S(1)}, bf16[2,320,128]{2,1,0:T(8,128)(2,1)S(1)}, u32[]{:S(2)}, u32[]{:S(2)}) collective-permute-start(bf16[2,320,128]{2,1,0:T(8,128)(2,1)S(1)} %pad_maximum_fusion.3), channel_id=1, source_target_pairs={{0,1},{1,0},{2,3},{3,2},{4,5},{5,4},{6,7},{7,6},{8,9},{9,8},{10,11... | collective-permute-start | bytes 491528 | tf_op jit(solution)/shard_map/ppermute | solution.py:259
  19.9 3.0 %collective-permute-start.5 = (bf16[2,320,128]{2,1,0:T(8,128)(2,1)S(1)}, bf16[2,320,128]{2,1,0:T(8,128)(2,1)S(1)}, u32[]{:S(2)}, u32[]{:S(2)}) collective-permute-start(bf16[2,320,128]{2,1,0:T(8,128)(2,1)S(1)} %pad_maximum_fusion.4), channel_id=1, source_target_pairs={{1,2},{2,1},{5,6},{6,5},{9,10},{10,9},{13,14},{14,13},{17,18},{18,... | collective-permute-start | bytes 491528 | tf_op jit(solution)/shard_map/ppermute | solution.py:259
  23.0 0.0 collective-permute-done.refs_3_
  23.0 0.0 collective-permute-done.1.refs_4_
  23.0 0.0 copy-done.1
  23.0 0.0 copy-start.3
  23.0 1.3 %copy-done.3 = bf16[3,3,256,256]{3,2,1,0:T(8,128)(2,1)S(1)} copy-done((bf16[3,3,256,256]{3,2,1,0:T(8,128)(2,1)S(1)}, bf16[3,3,256,256]{3,2,1,0:T(8,128)(2,1)}, u32[]{:S(2)}) %copy-start.3) | copy-done | bytes 1179672
  24.3 12.8 %shard_map.46.refs_11_ = bf16[8,512,256]{2,1,0:T(8,128)(2,1)} custom-call(s32[5]{0:T(128)S(1)} %stack.39.refs_0_, bf16[8,512,128]{2,1,0:T(8,128)(2,1)S(1)} %copy-done.1, bf16[8,512,128]{2,1,0:T(8,128)(2,1)S(1)} %copy-done, bf16[2,1024,128]{2,1,0:T(8,128)(2,1)} %collective-permute-done.refs_3_, bf16[2,1024,128]{2,1,0:T(8,128)(2,1)} %collective-permute-done.1.refs_4_, ...), custom_call_target="tpu_custom_call" | custom-call | flops 4945084416 | bytes 6291456 | tf_op jit(solution)/shard_map/pallas_call | solution.py:242
  37.0 0.0 collective-permute-done.4.refs_7_
  37.1 0.0 collective-permute-done.5.refs_8_
  37.1 17.0 %shard_map.47 = bf16[8,512,256]{2,1,0:T(8,128)(2,1)} custom-call(s32[5]{0:T(128)S(1)} %stack.39.refs_0_, bf16[8,512,128]{2,1,0:T(8,128)(2,1)S(1)} %copy-done.1, bf16[8,512,128]{2,1,0:T(8,128)(2,1)S(1)} %copy-done, bf16[2,1024,128]{2,1,0:T(8,128)(2,1)} %collective-permute-done.refs_3_, ...), custom_call_target="tpu_custom_call", output_to_operand_aliasing={{}: (11, {})} | custom-call | flops 6492782592 | bytes 6291456 | tf_op jit(solution)/shard_map/pallas_call | solution.py:242
  (13 shorter events, 0.1 us)
Async XLA Ops:
  0.0 1.1 %slice-start = ((bf16[8,512,128]{2,1,0:T(8,128)(2,1)}), bf16[8,272,128]{2,1,0:T(8,128)(2,1)S(1)}, s32[]{:S(2)}) async-start(bf16[8,512,128]{2,1,0:T(8,128)(2,1)} %refs_2_.3), calls=%async_computation | async-start | bytes 1114112 | tf_op jit(solution)/shard_map/slice | solution.py:273
  0.8 5.2 %slice-start.1 = ((bf16[8,512,128]{2,1,0:T(8,128)(2,1)}), bf16[8,16,128]{2,1,0:T(8,128)(2,1)S(1)}, s32[]{:S(2)}) async-start(bf16[8,512,128]{2,1,0:T(8,128)(2,1)} %refs_2_.3), calls=%async_computation.1 | async-start | bytes 65536 | tf_op jit(solution)/shard_map/slice | solution.py:284
  0.8 6.5 %copy-start = (bf16[8,512,128]{2,1,0:T(8,128)(2,1)S(1)}, bf16[8,512,128]{2,1,0:T(8,128)(2,1)}, u32[]{:S(2)}) copy-start(bf16[8,512,128]{2,1,0:T(8,128)(2,1)} %refs_2_.3) | copy-start | bytes 3145732
  1.9 16.3 %collective-permute-start.2 = (bf16[8,288,128]{2,1,0:T(8,128)(2,1)}, bf16[8,288,128]{2,1,0:T(8,128)(2,1)S(1)}, u32[]{:S(2)}, u32[]{:S(2)}) collective-permute-start(bf16[8,288,128]{2,1,0:T(8,128)(2,1)} %pad_maximum_fusion), channel_id=1, source_target_pairs={{0,4},{4,8},{8,12},{1,5},{5,9},{9,13},{2,6},{6,10},{10,14},{3,7},{... | collective-permute-start | bytes 1769480 | tf_op jit(solution)/shard_map/ppermute | solution.py:274
  6.0 8.2 %collective-permute-start.3 = (bf16[8,32,128]{2,1,0:T(8,128)(2,1)S(1)}, bf16[8,32,128]{2,1,0:T(8,128)(2,1)S(1)}, u32[]{:S(2)}, u32[]{:S(2)}) collective-permute-start(bf16[8,32,128]{2,1,0:T(8,128)(2,1)S(1)} %pad_maximum_fusion.5), channel_id=1, source_target_pairs={{4,0},{8,4},{12,8},{5,1},{9,5},{13,9},{6,2},{10,6},{14,10},{7,3},{... | collective-permute-start | bytes 196616 | tf_op jit(solution)/shard_map/ppermute | solution.py:285
  9.3 13.7 %collective-permute-start = (bf16[2,1024,128]{2,1,0:T(8,128)(2,1)}, bf16[2,1024,128]{2,1,0:T(8,128)(2,1)}, u32[]{:S(2)}, u32[]{:S(2)}) collective-permute-start(bf16[2,1024,128]{2,1,0:T(8,128)(2,1)} %pad_maximum_fusion.1), channel_id=1, source_target_pairs={{0,1},{1,0},{2,3},{3,2},{4,5},{5,4},{6,7},{7,6},{8,9},{9,8},{10,11... | collective-permute-start | bytes 1572872 | tf_op jit(solution)/shard_map/ppermute | solution.py:259
  10.3 12.7 %copy-start.1 = (bf16[8,512,128]{2,1,0:T(8,128)(2,1)S(1)}, bf16[8,512,128]{2,1,0:T(8,128)(2,1)}, u32[]{:S(2)}) copy-start(bf16[8,512,128]{2,1,0:T(8,128)(2,1)} %refs_1_.3) | copy-start | bytes 3145732
  11.1 11.8 %collective-permute-start.1 = (bf16[2,1024,128]{2,1,0:T(8,128)(2,1)}, bf16[2,1024,128]{2,1,0:T(8,128)(2,1)}, u32[]{:S(2)}, u32[]{:S(2)}) collective-permute-start(bf16[2,1024,128]{2,1,0:T(8,128)(2,1)} %pad_maximum_fusion.2), channel_id=1, source_target_pairs={{1,2},{2,1},{5,6},{6,5},{9,10},{10,9},{13,14},{14,13},{17,18},{18,... | collective-permute-start | bytes 1572872 | tf_op jit(solution)/shard_map/ppermute | solution.py:259
  14.2 8.8 %copy-start.2 = (bf16[3,3,256,256]{3,2,1,0:T(8,128)(2,1)S(1)}, bf16[3,3,256,256]{3,2,1,0:T(8,128)(2,1)}, u32[]{:S(2)}) copy-start(bf16[3,3,256,256]{3,2,1,0:T(8,128)(2,1)} %param.6) | copy-start | bytes 3538948
  18.3 18.7 %collective-permute-start.4 = (bf16[2,320,128]{2,1,0:T(8,128)(2,1)S(1)}, bf16[2,320,128]{2,1,0:T(8,128)(2,1)S(1)}, u32[]{:S(2)}, u32[]{:S(2)}) collective-permute-start(bf16[2,320,128]{2,1,0:T(8,128)(2,1)S(1)} %pad_maximum_fusion.3), channel_id=1, source_target_pairs={{0,1},{1,0},{2,3},{3,2},{4,5},{5,4},{6,7},{7,6},{8,9},{9,8},{10,11... | collective-permute-start | bytes 491528 | tf_op jit(solution)/shard_map/ppermute | solution.py:259
  19.9 17.1 %collective-permute-start.5 = (bf16[2,320,128]{2,1,0:T(8,128)(2,1)S(1)}, bf16[2,320,128]{2,1,0:T(8,128)(2,1)S(1)}, u32[]{:S(2)}, u32[]{:S(2)}) collective-permute-start(bf16[2,320,128]{2,1,0:T(8,128)(2,1)S(1)} %pad_maximum_fusion.4), channel_id=1, source_target_pairs={{1,2},{2,1},{5,6},{6,5},{9,10},{10,9},{13,14},{14,13},{17,18},{18,... | collective-permute-start | bytes 491528 | tf_op jit(solution)/shard_map/ppermute | solution.py:259
  23.0 1.3 %copy-start.3 = (bf16[3,3,256,256]{3,2,1,0:T(8,128)(2,1)S(1)}, bf16[3,3,256,256]{3,2,1,0:T(8,128)(2,1)}, u32[]{:S(2)}) copy-start(bf16[3,3,256,256]{3,2,1,0:T(8,128)(2,1)} %param.7) | copy-start | bytes 3538948

commit v2 on v0

v2 whole, which is shorter than its diff:
```python
import functools

import jax
import jax.numpy as jnp
from jax import lax
from jax.experimental import pallas as pl
from jax.experimental.pallas import tpu as pltpu
from jax.sharding import PartitionSpec as P

BF = jnp.bfloat16
F32 = jnp.float32
HALO = 16
LAG = 0


class Segment:
    def __init__(self, base, outs):
        self.base, self.outs = base, outs
        self.hid = outs + 16
        self.vol = outs + 32


def part_kernel(segments, ext, disp, *refs):
    refs = list(refs)
    flags, l_own, r_own, a_any, b_any = refs[:5]
    zl, zr, ca_any, cb_any = refs[5:9] if ext else (None,) * 4
    k1_any, k2_any = refs[9:11] if ext else refs[5:7]
    out_any, lrim, rrim, rrev, vf, vs, hf, hs, obuf, k1, k2, sems, osems = refs[-13:]
    rows, cols, chans = l_own.shape
    pad = HALO if ext else 0
    lpad = disp + HALO if ext else 0
    scale = 1.0 / (chans ** 0.5)
    odd = flags[0] == 1
    if not ext:
        out_any, done = refs[7:9]
        done[0] = flags[5]
        done[1] = flags[6]

    def rim(side, main, corner):
        dst = pl.ds(2 * side, 2)
        out = [
            (main.at[:, pl.ds(0, cols)], lrim.at[dst, pl.ds(pad, cols)], sems.at[side]),
            (main.at[:, pl.ds(cols, cols)], rrim.at[dst, pl.ds(lpad, cols)], sems.at[side]),
        ]
        if ext:
            wide = lpad + pad
            out += [
                (corner.at[:, pl.ds(0, lpad)], rrim.at[dst, pl.ds(0, lpad)], sems.at[side]),
                (corner.at[:, pl.ds(lpad, pad)], lrim.at[dst, pl.ds(0, pad)], sems.at[side]),
                (corner.at[:, pl.ds(wide, pad)], rrim.at[dst, pl.ds(lpad + cols, pad)], sems.at[side]),
                (corner.at[:, pl.ds(wide + pad, pad)], lrim.at[dst, pl.ds(pad + cols, pad)], sems.at[side]),
            ]
        return out

    @pl.when(odd)
    def _():
        for c in rim(0, a_any, ca_any) + rim(1, b_any, cb_any):
            pltpu.make_async_copy(*c).start()

    @pl.when(jnp.logical_not(odd))
    def _():
        for c in rim(0, b_any, cb_any) + rim(1, a_any, ca_any):
            pltpu.make_async_copy(*c).start()

    k1_copy = pltpu.make_async_copy(k1_any, k1, sems.at[2])
    k2_copy = pltpu.make_async_copy(k2_any, k2, sems.at[3])
    k1_copy.start()
    k2_copy.start()
    waited = set()

    def wait_rows(row):
        side = 0 if row < 2 else 1 if row >= rows + 2 else None
        if side is not None and side not in waited:
            waited.add(side)
            for c in rim(side, a_any, ca_any):
                pltpu.make_async_copy(*c).wait()

    def pieces(row, lo, n, right):
        if row < 2 or row >= rows + 2:
            at = row if row < 2 else row - rows
            ref, off = (rrim, lpad) if right else (lrim, pad)
            return [ref[at, lo + off:lo + off + n, :]]
        row -= 2
        out = []
        if lo < 0:
            m = min(n, -lo)
            at = lo + lpad if right else lo + lpad + pad
            out.append(zl[row, at:at + m, :])
            lo, n = lo + m, n - m
        if n and lo < cols:
            m = min(n, cols - lo)
            out.append((r_own if right else l_own)[row, lo:lo + m, :])
            lo, n = lo + m, n - m
        if n:
            at = lo - cols + (0 if right else pad)
            out.append(zr[row, at:at + n, :])
        return out

    def columns(row, lo, n, right):
        parts = pieces(row, lo, n, right)
        return parts[0] if len(parts) == 1 else jnp.concatenate(parts, axis=0)

    mirror = 7 - lax.broadcasted_iota(jnp.int32, (8, 128), 0)

    def flip(row):
        def unit(s, seg, t):
            span = 128 * -(-seg.vol // 128) + disp
            start = seg.base - disp + 128 * t
            n = min(128, seg.vol + disp - 128 * t)
            both = jnp.concatenate([columns(row + q, start, n, True) for q in range(2)], axis=1)
            wide = both.astype(F32)
            res = jnp.concatenate([jnp.concatenate([
                jnp.take_along_axis(wide[n - 8 * (i + 1):n - 8 * i, chans * q:chans * (q + 1)], mirror, axis=0,
                                    mode="promise_in_bounds") for q in range(2)], axis=1)
                for i in range(n // 8)], axis=0).astype(BF)
            for q in range(2):
                rrev[s, row + q, span - 128 * t - n:span - 128 * t, :] = res[:, chans * q:chans * (q + 1)]

        if row < rows + 4:
            wait_rows(row)
            wait_rows(row + 1)
            for s, seg in enumerate(segments):
                for t in range(-(-(seg.vol + disp) // 128)):
                    unit(s, seg, t)

    def volume(row, scores_now):
        slot = row

        def score(s, seg, dst, b):
            n = min(128, seg.vol - 128 * b)
            u = 128 * (-(-seg.vol // 128) - 1 - b)
            left = columns(row, seg.base + 128 * b, n, False)
            scores = lax.dot_general(left, rrev[s, slot, u:u + 128 + disp, :], (((1,), (1,)), ((), ())),
                                     preferred_element_type=F32) * scale
            rolled = pltpu.roll(scores, 1, 1, stride=1, stride_axis=0)
            for h in range(disp // 128):
                vf[slot, h, dst + 128 * b:dst + 128 * b + n, :] = rolled[:, 128 * (h + 1):128 * (h + 2)]

        def spread(b):
            src, dst = 0, 0
            for seg in segments:
                for h in range(disp // 128):
                    vs[row, dst:dst + seg.hid, disp * b + 128 * h:disp * b + 128 * (h + 1)] = (
                        vf[slot, h, pl.ds(src + 14 + b, seg.hid), :].astype(BF))
                src += seg.vol
                dst += seg.hid

        dst = 0
        if scores_now:
            for s, seg in enumerate(segments):
                for b in range(-(-seg.vol // 128)):
                    score(s, seg, dst, b)
                dst += seg.vol
        else:
            for b in range(3):
                spread(b)

    def conv(src, row, count, kernel):
        x = jnp.concatenate([src[row + a:row + a + count].reshape(count * src.shape[1], src.shape[2])
                             for a in range(3)], axis=1)
        res = jnp.maximum(jnp.dot(x, kernel[...], preferred_element_type=F32), 0.0)
        return [res[q * src.shape[1]:(q + 1) * src.shape[1]] for q in range(count)]

    m_hid = sum(seg.hid for seg in segments)
    m_out = sum(seg.outs for seg in segments)

    def hidden(row, count):
        for q, one in enumerate(conv(vs, row, count, k1)):
            if row + q == 0:
                one = one * flags[1].astype(F32)
            if row + q == rows + 1:
                one = one * flags[2].astype(F32)
            for h in range(disp // 128):
                hf[row + q, h] = one[:, 128 * h:128 * (h + 1)]

    def hidden_spreads(row):
        slot = row

        def spread(b):
            src, dst = 0, 0
            for seg in segments:
                for edge, flag in ((-1, flags[3]), (cols, flags[4])):
                    pos = edge - (seg.base + 15)
                    if b == 0 and 0 <= pos < seg.outs + 2:
                        at = src + pos // 8 * 8
                        keep = lax.broadcasted_iota(jnp.int32, (8, 128), 0) != pos % 8
                        keep = jnp.where(keep, 1.0, flag.astype(F32))
                        for h in range(disp // 128):
                            hf[slot, h, at:at + 8, :] = hf[slot, h, at:at + 8, :] * keep
                for h in range(disp // 128):
                    hs[row, dst:dst + seg.outs, disp * b + 128 * h:disp * b + 128 * (h + 1)] = (
                        hf[slot, h, pl.ds(src + b, seg.outs), :].astype(BF))
                src += seg.hid
                dst += seg.outs

        for b in range(3):
            spread(b)

    pending = []

    def out(row, count):
        for q, one in enumerate(conv(hs, row, count, k2)):
            obuf[row + q] = one.astype(BF)
        src = 0
        for s, seg in enumerate(segments):
            c = pltpu.make_async_copy(
                obuf.at[pl.ds(row, count), pl.ds(src, seg.outs)],
                out_any.at[pl.ds(row, count), pl.ds(seg.base + 16, seg.outs)], osems.at[row, s])
            c.start()
            pending.append(c)
            src += seg.outs

    def both(row, end, f, *args):
        if 0 <= row < end:
            f(row, *args)
            f(row + 1, *args)

    flip(2)
    flip(4)
    both(2, rows + 4, volume, True)
    flip(0)
    both(0, rows + 4, volume, True)
    both(2, rows + 4, volume, False)
    both(0, rows + 4, volume, False)
    k1_copy.wait()
    for row in range(0, rows + 6, 2):
        if row == 6:
            k2_copy.wait()
        both(row + 4, rows + 4, volume, True)
        if row < rows + 2:
            hidden(row, 2)
        if 6 <= row < rows + 6:
            out(row - 6, 2)
        flip(row + 6)
        both(row + 4, rows + 4, volume, False)
        both(row - 2 + LAG, rows + 2, hidden_spreads)
    for c in pending:
        c.wait()


def part_call(segments, ext, disp, rows, cols, chans, out_shape, operands):
    m_vol = sum(s.vol for s in segments)
    m_hid = sum(s.hid for s in segments)
    m_out = sum(s.outs for s in segments)
    pad = HALO if ext else 0
    span = max(128 * -(-s.vol // 128) + disp for s in segments)
    scratch = [
        pltpu.VMEM((4, cols + 2 * pad, chans), BF),
        pltpu.VMEM((4, cols + 2 * pad + (disp if ext else 0), chans), BF),
        pltpu.VMEM((len(segments), rows + 4, span, chans), BF),
        pltpu.VMEM((rows + 4, disp // 128, m_vol, 128), F32),
        pltpu.VMEM((rows + 4, m_hid, 3 * disp), BF),
        pltpu.VMEM((rows + 2, disp // 128, m_hid, 128), F32),
        pltpu.VMEM((rows + 2, m_out, 3 * disp), BF),
        pltpu.VMEM((rows, m_out, disp), BF),
        pltpu.VMEM((9 * disp, disp), BF),
        pltpu.VMEM((9 * disp, disp), BF),
        pltpu.SemaphoreType.DMA((4,)),
        pltpu.SemaphoreType.DMA((rows, len(segments))),
    ]
    vmem, anywhere = pl.BlockSpec(memory_space=pltpu.VMEM), pl.BlockSpec(memory_space=pltpu.HBM)
    smem = pl.BlockSpec(memory_space=pltpu.SMEM)
    flops = 2 * 9 * disp * disp * ((rows + 2) * m_hid + rows * m_out)
    return pl.pallas_call(
        functools.partial(part_kernel, segments, ext, disp),
        out_shape=out_shape if ext else [out_shape, jax.ShapeDtypeStruct((2,), jnp.int32)],
        in_specs=([smem, vmem, vmem, anywhere, anywhere] + ([vmem, vmem, anywhere, anywhere] if ext else [])
                  + [anywhere, anywhere] + ([anywhere] if ext else [])),
        out_specs=anywhere if ext else [anywhere, smem],
        scratch_shapes=scratch,
        input_output_aliases={len(operands) - 1: 0} if ext else {},
        compiler_params=pltpu.CompilerParams(vmem_limit_bytes=54 << 20),
        cost_estimate=pl.CostEstimate(flops=flops if ext else 1 << 20, bytes_accessed=1 << 20, transcendentals=0),
    )(*operands)


def pair_permute(x, axis, first):
    n = lax.axis_size(axis)
    perm = []
    for i in range(first, n - 1, 2):
        perm += [(i, i + 1), (i + 1, i)]
    return lax.ppermute(x, axis, perm)


def copy_all(copies, sems):
    copies = [pltpu.make_async_copy(src, dst, sems.at[i]) for i, (src, dst) in enumerate(copies)]
    for c in copies:
        c.start()
    for c in copies:
        c.wait()


def pack_columns(l_any, r_any, zl, sems):
    rows, cols, _ = l_any.shape
    wide = zl.shape[1] - HALO
    copies = [(r_any.at[q, pl.ds(cols - wide, wide)], zl.at[q, pl.ds(0, wide)]) for q in range(rows)]
    copies.append((l_any.at[:, pl.ds(cols - HALO, HALO)], zl.at[:, pl.ds(wide, HALO)]))
    copy_all(copies, sems)


def pack_rims(flags, l_any, r_any, a, b, zr, sems):
    cols = l_any.shape[1]
    copies = []
    for msg, at in ((b, flags[6]), (a, flags[5])):
        copies.append((l_any.at[pl.ds(at, 2)], msg.at[:, pl.ds(0, cols)]))
        copies.append((r_any.at[pl.ds(at, 2)], msg.at[:, pl.ds(cols, cols)]))
    copies.append((r_any.at[:, pl.ds(0, HALO)], zr.at[:, pl.ds(0, HALO)]))
    copies.append((l_any.at[:, pl.ds(0, HALO)], zr.at[:, pl.ds(HALO, HALO)]))
    copy_all(copies, sems)


def pack(flags, left, right, disp):
    rows, cols, chans = left.shape
    anywhere = pl.BlockSpec(memory_space=pl.ANY)
    zl = pl.pallas_call(
        pack_columns,
        out_shape=jax.ShapeDtypeStruct((rows, disp + 2 * HALO, chans), BF),
        in_specs=[pl.BlockSpec(memory_space=pltpu.HBM)] * 2,
        out_specs=anywhere,
        scratch_shapes=[pltpu.SemaphoreType.DMA((rows + 1,))],
        compiler_params=pltpu.CompilerParams(vmem_limit_bytes=1 << 20),
        cost_estimate=pl.CostEstimate(flops=0, bytes_accessed=1 << 20, transcendentals=0),
    )(left, right)
    shapes = [(2, 2 * cols, chans), (2, 2 * cols, chans), (rows, 2 * HALO, chans)]
    return [zl] + list(pl.pallas_call(
        pack_rims,
        out_shape=[jax.ShapeDtypeStruct(s, BF) for s in shapes],
        in_specs=[pl.BlockSpec(memory_space=pltpu.SMEM)] + [pl.BlockSpec(memory_space=pltpu.HBM)] * 2,
        out_specs=[anywhere] * 3,
        scratch_shapes=[pltpu.SemaphoreType.DMA((6,))],
        compiler_params=pltpu.CompilerParams(vmem_limit_bytes=1 << 20),
        cost_estimate=pl.CostEstimate(flops=20 << 30, bytes_accessed=1 << 20, transcendentals=0),
    )(flags, left, right))


def local(left, right, conv_first, conv_second):
    rows, cols, chans = left.shape
    disp = conv_first.shape[2]
    n_row, n_col = lax.axis_size("row"), lax.axis_size("col")
    ri, ci = lax.axis_index("row"), lax.axis_index("col")
    odd = ri % 2
    a_at = jnp.where(odd == 1, 0, rows - 2)
    b_at = jnp.where(odd == 1, rows - 2, 0)
    flags = jnp.stack([odd, ri > 0, ri < n_row - 1, ci > 0, ci < n_col - 1, a_at, b_at]).astype(jnp.int32)
    k1 = conv_first.reshape(9 * disp, disp)
    k2 = conv_second.reshape(9 * disp, disp)

    zl_msg, a_msg, b_msg, zr_msg = pack(flags, left, right, disp)
    zl = lax.ppermute(zl_msg, "col", [(i, i + 1) for i in range(n_col - 1)])
    b = pair_permute(b_msg, "row", 1)
    a = pair_permute(a_msg, "row", 0)
    zr = lax.ppermute(zr_msg, "col", [(i + 1, i) for i in range(n_col - 1)])

    out_shape = jax.ShapeDtypeStruct((rows, cols, disp), BF)
    mid = [Segment(disp, cols - disp - 2 * HALO)]
    out, done = part_call(mid, False, disp, rows, cols, chans, out_shape, (flags, left, right, a, b, k1, k2))

    def facing(at):
        return jnp.concatenate([lax.dynamic_slice_in_dim(x, at, 2, 0) for x in (zl, zr)], axis=1)

    cb = pair_permute(facing(done[1]), "row", 1)
    ca = pair_permute(facing(done[0]), "row", 0)
    rest = [Segment(-HALO, disp + HALO), Segment(cols - 2 * HALO, HALO)]
    return part_call(rest, True, disp, rows, cols, chans, out_shape,
                     (flags, left, right, a, b, zl, zr, ca, cb, k1, k2, out))


def solution(mesh):
    spec = P(("strip", "row"), "col", None)
    return jax.shard_map(local, mesh=mesh, in_specs=(spec, spec, P(), P()), out_specs=spec, check_vma=False)
```

time: 147 us -> 56 us (0.38)
  local copies, waits for them, and re-layouts: 72.5 us -> 5.42 us
  Pallas kernels: 0 us -> 28.3 us
  waiting for transfers between devices: 25 us -> 4.74 us
  starting transfers between devices: 27.8 us -> 12.8 us
  matrix products: 14 us -> 0 us
  other arithmetic: 6.12 us -> 0.03 us
  between operations: 0.31 us -> 4.28 us
    pallas_call x0 -> x4, Pallas kernels: none -> 28.3 us  [the longest x2 26.8 us: part_call(): pl.pallas_call(functools.partial(part_kernel, segments, ext, disp), out_s...]
    rev x1 -> x0, local copies, waits for them, and re-layouts: 22.5 us -> none  [correlate(): banded = skewed[..., 1:disparities + 1][..., ::-1]]
    ppermute x9 -> x6, waiting for transfers between devices: 25 us -> 4.74 us  [the longest x4 4.74 us: pair_permute(): return lax.ppermute(x, axis, perm)]
    reshape x2 -> x0, local copies, waits for them, and re-layouts: 18.2 us -> none  [the longest x1 13.3 us: correlate(): flat_scores.reshape(row_count, block_count, disparities, 2 * disparities...]
    ppermute x9 -> x6, starting transfers between devices: 27.8 us -> 12.8 us  [the longest x4 8.27 us: pair_permute(): return lax.ppermute(x, axis, perm)]
    conv_general_dilated x2 -> x0, matrix products: 10.8 us -> none  [convolve_valid(): lax.conv_general_dilated(padded[None], kernel, (1, 1), 'VALID', dimension...]
    conv_general_dilated x5 -> x0, local copies, waits for them, and re-layouts: 8.56 us -> none  [convolve_valid(): lax.conv_general_dilated(padded[None], kernel, (1, 1), 'VALID', dimension...]
    mul x1 -> x0, local copies, waits for them, and re-layouts: 6.22 us -> none  [correlate(): scores = scores * (1.0 / jnp.sqrt(jnp.float32(chan_count)))]
  transfers between devices with their start and end apart: 9 -> 6, of which waited for: 7 -> 2; matrix products, arithmetic and copies ran while one was open for 0% -> 2% of each run, Pallas kernels for 0% -> 23%
where the time goes in v2:
time: 56 us; the launch traced here: 55.6 us
  Pallas kernels  28.3 us (51%)
  starting transfers between devices  12.8 us (23%)
  local copies, waits for them, and re-layouts  5.42 us (10%)
  waiting for transfers between devices  4.74 us (8%)
  between operations  4.28 us (8%)
    pallas_call x2, Pallas kernels, part_call(): pl.pallas_call(functools.partial(part_kernel, segments, ext, disp), out_s...  26.8 us
    ppermute x4, starting transfers between devices, pair_permute(): return lax.ppermute(x, axis, perm)  8.27 us
    ppermute x4, waiting for transfers between devices, pair_permute(): return lax.ppermute(x, axis, perm)  4.74 us
    unnamed x22, local copies, waits for them, and re-layouts  3.93 us
    ppermute x1, starting transfers between devices, local(): zl = lax.ppermute(zl_msg, 'col', [(i, i + 1) for i in range(n_col - 1)])  3.24 us
    slice x1, local copies, waits for them, and re-layouts, local(): cb = pair_permute(facing(done[1]), 'row', 1)  1.36 us
    ppermute x1, starting transfers between devices, local(): zr = lax.ppermute(zr_msg, 'col', [(i + 1, i) for i in range(n_col - 1)])  1.29 us
  transfers between devices with their start and end apart: 6, of which 2 were waited for; matrix products, arithmetic and copies ran while one was open for 2% of the time, Pallas kernels for 23%

profile of v2, /device:TPU:1, one launch (start us, length us, event | category | flops | bytes accessed | tf_op | source)
XLA Modules:
  0.0 55.6 jit_solution(15542455863093331641)
XLA Ops:
  0.0 0.1 stack.47.flags.refs_0_
  0.1 1.2 %copy-done = bf16[8,512,128]{2,1,0:T(8,128)(2,1)S(1)} copy-done((bf16[8,512,128]{2,1,0:T(8,128)(2,1)S(1)}, bf16[8,512,128]{2,1,0:T(8,128)(2,1)}, u32[]{:S(2)}) %copy-start) | copy-done | bytes 1048600
  1.3 1.2 %copy-done.2 = bf16[8,512,128]{2,1,0:T(8,128)(2,1)S(1)} copy-done((bf16[8,512,128]{2,1,0:T(8,128)(2,1)S(1)}, bf16[8,512,128]{2,1,0:T(8,128)(2,1)}, u32[]{:S(2)}) %copy-start.2) | copy-done | bytes 1048600
  2.5 0.7 %shard_map.46 = (bf16[2,1024,128]{2,1,0:T(8,128)(2,1)S(1)}, bf16[2,1024,128]{2,1,0:T(8,128)(2,1)S(1)}, bf16[8,32,128]{2,1,0:T(8,128)(2,1)S(1)}) custom-call(s32[7]{0:T(128)S(1)} %stack.47.flags.refs_0_, bf16[8,512,128]{2,1,0:T(8,128)(2,1)S(1)} %copy-done, bf16[8,512,128]{2,1,0:T(8,128)(2,1)S(1)} %copy-done.2), custom_call_target="tpu_custom_call" | custom-call | flops 21474836480 | bytes 1048576 | tf_op jit(solution)/shard_map/pallas_call | solution.py:325
  3.3 0.1 collective-permute-start
  3.4 4.5 %collective-permute-start.1 = (bf16[2,1024,128]{2,1,0:T(8,128)(2,1)S(1)}, bf16[2,1024,128]{2,1,0:T(8,128)(2,1)S(1)}, u32[]{:S(2)}, u32[]{:S(2)}) collective-permute-start(bf16[2,1024,128]{2,1,0:T(8,128)(2,1)S(1)} %get-tuple-element.11), channel_id=1, source_target_pairs={{1,2},{2,1},{5,6},{6,5},{9,10},{10,9},{13,14},{14,13},{17,18},{18,... | collective-permute-start | bytes 1572872 | tf_op jit(solution)/shard_map/ppermute | solution.py:282
  7.9 0.0 copy-done.1
  7.9 0.0 copy-done.3
  7.9 0.8 %shard_map.47 = bf16[8,288,128]{2,1,0:T(8,128)(2,1)S(1)} custom-call(bf16[8,512,128]{2,1,0:T(8,128)(2,1)S(1)} %copy-done.1, bf16[8,512,128]{2,1,0:T(8,128)(2,1)S(1)} %copy-done.3), custom_call_target="tpu_custom_call" | custom-call | bytes 1048576 | tf_op jit(solution)/shard_map/pallas_call | solution.py:315
  8.7 3.2 %collective-permute-start.2 = (bf16[8,288,128]{2,1,0:T(8,128)(2,1)S(1)}, bf16[8,288,128]{2,1,0:T(8,128)(2,1)S(1)}, u32[]{:S(2)}, u32[]{:S(2)}) collective-permute-start(bf16[8,288,128]{2,1,0:T(8,128)(2,1)S(1)} %shard_map.47), channel_id=1, source_target_pairs={{0,4},{4,8},{8,12},{1,5},{5,9},{9,13},{2,6},{6,10},{10,14},{3,7},{... | collective-permute-start | bytes 1769480 | tf_op jit(solution)/shard_map/ppermute | solution.py:349
  11.9 1.3 %collective-permute-start.3 = (bf16[8,32,128]{2,1,0:T(8,128)(2,1)S(1)}, bf16[8,32,128]{2,1,0:T(8,128)(2,1)S(1)}, u32[]{:S(2)}, u32[]{:S(2)}) collective-permute-start(bf16[8,32,128]{2,1,0:T(8,128)(2,1)S(1)} %get-tuple-element.12), channel_id=1, source_target_pairs={{4,0},{8,4},{12,8},{5,1},{9,5},{13,9},{6,2},{10,6},{14,10},{7,3},{... | collective-permute-start | bytes 196616 | tf_op jit(solution)/shard_map/ppermute | solution.py:352
  13.2 0.0 collective-permute-done.refs_3_
  13.3 1.7 %collective-permute-done.1.refs_4_ = bf16[2,1024,128]{2,1,0:T(8,128)(2,1)S(1)} collective-permute-done((bf16[2,1024,128]{2,1,0:T(8,128)(2,1)S(1)}, bf16[2,1024,128]{2,1,0:T(8,128)(2,1)S(1)}, u32[]{:S(2)}, u32[]{:S(2)}) %collective-permute-start.1) | collective-permute-done | bytes 524320 | tf_op jit(solution)/shard_map/ppermute | solution.py:282
  15.0 0.8 %copy-done.6 = bf16[2,1024,128]{2,1,0:T(8,128)(2,1)} copy-done((bf16[2,1024,128]{2,1,0:T(8,128)(2,1)}, bf16[2,1024,128]{2,1,0:T(8,128)(2,1)S(1)}, u32[]{:S(2)}) %copy-start.6) | copy-done | bytes 524312
  15.8 12.0 %shard_map.48 = (bf16[8,512,256]{2,1,0:T(8,128)(2,1)}, s32[2]{0:T(128)}) custom-call(s32[7]{0:T(128)} %copy-done.4, bf16[8,512,128]{2,1,0:T(8,128)(2,1)} %refs_1_.3, bf16[8,512,128]{2,1,0:T(8,128)(2,1)} %refs_2_.3, bf16[2,1024,128]{2,1,0:T(8,128)(2,1)} %copy-done.5, bf16[2,1024,128]{2,1,0:T(8,128)(2,1)} %copy-done.6, bf16[2304,256]{1,0:T(8,128)(2,1)} %bitcast.11, ...), custom_call_target="tpu_custom_call" | custom-call | flops 1048576 | bytes 1048576 | tf_op jit(solution)/shard_map/pallas_call | solution.py:264
  27.8 1.4 %fusion = (s32[1]{0:T(128)}, s32[1]{0:T(128)}) fusion(s32[2]{0:T(128)} %get-tuple-element.13), kind=kLoop, calls=%fused_computation.6 | loop fusion | bytes 16 | tf_op jit(solution)/shard_map/slice | solution.py:361
  33.1 0.0 collective-permute-done.3.refs_6_
  33.2 0.0 collective-permute-done.2.refs_5_
  33.3 0.1 collective-permute-start.4
  33.4 3.6 %collective-permute-start.5 = (bf16[2,320,128]{2,1,0:T(8,128)(2,1)S(1)}, bf16[2,320,128]{2,1,0:T(8,128)(2,1)S(1)}, u32[]{:S(2)}, u32[]{:S(2)}) collective-permute-start(bf16[2,320,128]{2,1,0:T(8,128)(2,1)S(1)} %pad_maximum_fusion.1), channel_id=1, source_target_pairs={{1,2},{2,1},{5,6},{6,5},{9,10},{10,9},{13,14},{14,13},{17,18},{18,... | collective-permute-start | bytes 491528 | tf_op jit(solution)/shard_map/ppermute | solution.py:282
  37.0 0.0 collective-permute-done.4.refs_7_
  37.0 3.0 %collective-permute-done.5.refs_8_ = bf16[2,320,128]{2,1,0:T(8,128)(2,1)S(1)} collective-permute-done((bf16[2,320,128]{2,1,0:T(8,128)(2,1)S(1)}, bf16[2,320,128]{2,1,0:T(8,128)(2,1)S(1)}, u32[]{:S(2)}, u32[]{:S(2)}) %collective-permute-start.5) | collective-permute-done | bytes 163872 | tf_op jit(solution)/shard_map/ppermute | solution.py:282
  40.0 0.7 %copy-done.10 = bf16[2,320,128]{2,1,0:T(8,128)(2,1)} copy-done((bf16[2,320,128]{2,1,0:T(8,128)(2,1)}, bf16[2,320,128]{2,1,0:T(8,128)(2,1)S(1)}, u32[]{:S(2)}) %copy-start.10) | copy-done | bytes 163864
  40.7 14.8 %shard_map.49 = bf16[8,512,256]{2,1,0:T(8,128)(2,1)} custom-call(s32[7]{0:T(128)} %copy-done.4, bf16[8,512,128]{2,1,0:T(8,128)(2,1)} %refs_1_.3, bf16[8,512,128]{2,1,0:T(8,128)(2,1)} %refs_2_.3, bf16[2,1024,128]{2,1,0:T(8,128)(2,1)} %copy-done.5, bf16[2,1024,128]{2,1,0:T(8,128)(2,1)} %copy-done.6, ...), custom_call_target="tpu_custom_call", output_to_operand_aliasing={{}: (11, {})} | custom-call | flops 6492782592 | bytes 1048576 | tf_op jit(solution)/shard_map/pallas_call | solution.py:264
  (20 shorter events, 0.1 us)
Async XLA Ops:
  0.1 1.2 %copy-start = (bf16[8,512,128]{2,1,0:T(8,128)(2,1)S(1)}, bf16[8,512,128]{2,1,0:T(8,128)(2,1)}, u32[]{:S(2)}) copy-start(bf16[8,512,128]{2,1,0:T(8,128)(2,1)} %refs_1_.3) | copy-start | bytes 3145732
  1.3 1.2 %copy-start.2 = (bf16[8,512,128]{2,1,0:T(8,128)(2,1)S(1)}, bf16[8,512,128]{2,1,0:T(8,128)(2,1)}, u32[]{:S(2)}) copy-start(bf16[8,512,128]{2,1,0:T(8,128)(2,1)} %refs_2_.3) | copy-start | bytes 3145732
  2.5 0.7 %copy-start.4 = (s32[7]{0:T(128)}, s32[7]{0:T(128)S(1)}, u32[]{:S(2)}) copy-start(s32[7]{0:T(128)S(1)} %stack.47.flags.refs_0_) | copy-start | bytes 88
  2.5 5.3 %copy-start.1 = (bf16[8,512,128]{2,1,0:T(8,128)(2,1)S(1)}, bf16[8,512,128]{2,1,0:T(8,128)(2,1)}, u32[]{:S(2)}) copy-start(bf16[8,512,128]{2,1,0:T(8,128)(2,1)} %refs_1_.3) | copy-start | bytes 3145732
  2.5 5.3 %copy-start.3 = (bf16[8,512,128]{2,1,0:T(8,128)(2,1)S(1)}, bf16[8,512,128]{2,1,0:T(8,128)(2,1)}, u32[]{:S(2)}) copy-start(bf16[8,512,128]{2,1,0:T(8,128)(2,1)} %refs_2_.3) | copy-start | bytes 3145732
  3.3 10.0 %collective-permute-start = (bf16[2,1024,128]{2,1,0:T(8,128)(2,1)S(1)}, bf16[2,1024,128]{2,1,0:T(8,128)(2,1)S(1)}, u32[]{:S(2)}, u32[]{:S(2)}) collective-permute-start(bf16[2,1024,128]{2,1,0:T(8,128)(2,1)S(1)} %get-tuple-element.10), channel_id=1, source_target_pairs={{0,1},{1,0},{2,3},{3,2},{4,5},{5,4},{6,7},{7,6},{8,9},{9,8},{10,11... | collective-permute-start | bytes 1572872 | tf_op jit(solution)/shard_map/ppermute | solution.py:282
  3.4 11.6 %collective-permute-start.1 = (bf16[2,1024,128]{2,1,0:T(8,128)(2,1)S(1)}, bf16[2,1024,128]{2,1,0:T(8,128)(2,1)S(1)}, u32[]{:S(2)}, u32[]{:S(2)}) collective-permute-start(bf16[2,1024,128]{2,1,0:T(8,128)(2,1)S(1)} %get-tuple-element.11), channel_id=1, source_target_pairs={{1,2},{2,1},{5,6},{6,5},{9,10},{10,9},{13,14},{14,13},{17,18},{18,... | collective-permute-start | bytes 1572872 | tf_op jit(solution)/shard_map/ppermute | solution.py:282
  8.7 24.5 %collective-permute-start.2 = (bf16[8,288,128]{2,1,0:T(8,128)(2,1)S(1)}, bf16[8,288,128]{2,1,0:T(8,128)(2,1)S(1)}, u32[]{:S(2)}, u32[]{:S(2)}) collective-permute-start(bf16[8,288,128]{2,1,0:T(8,128)(2,1)S(1)} %shard_map.47), channel_id=1, source_target_pairs={{0,4},{4,8},{8,12},{1,5},{5,9},{9,13},{2,6},{6,10},{10,14},{3,7},{... | collective-permute-start | bytes 1769480 | tf_op jit(solution)/shard_map/ppermute | solution.py:349
  11.9 21.2 %collective-permute-start.3 = (bf16[8,32,128]{2,1,0:T(8,128)(2,1)S(1)}, bf16[8,32,128]{2,1,0:T(8,128)(2,1)S(1)}, u32[]{:S(2)}, u32[]{:S(2)}) collective-permute-start(bf16[8,32,128]{2,1,0:T(8,128)(2,1)S(1)} %get-tuple-element.12), channel_id=1, source_target_pairs={{4,0},{8,4},{12,8},{5,1},{9,5},{13,9},{6,2},{10,6},{14,10},{7,3},{... | collective-permute-start | bytes 196616 | tf_op jit(solution)/shard_map/ppermute | solution.py:352
  13.3 1.7 %copy-start.5 = (bf16[2,1024,128]{2,1,0:T(8,128)(2,1)}, bf16[2,1024,128]{2,1,0:T(8,128)(2,1)S(1)}, u32[]{:S(2)}) copy-start(bf16[2,1024,128]{2,1,0:T(8,128)(2,1)S(1)} %collective-permute-done.refs_3_) | copy-start | bytes 1572868
  15.0 0.8 %copy-start.6 = (bf16[2,1024,128]{2,1,0:T(8,128)(2,1)}, bf16[2,1024,128]{2,1,0:T(8,128)(2,1)S(1)}, u32[]{:S(2)}) copy-start(bf16[2,1024,128]{2,1,0:T(8,128)(2,1)S(1)} %collective-permute-done.1.refs_4_) | copy-start | bytes 1572868
  33.1 6.9 %copy-start.8 = (bf16[8,32,128]{2,1,0:T(8,128)(2,1)}, bf16[8,32,128]{2,1,0:T(8,128)(2,1)S(1)}, u32[]{:S(2)}) copy-start(bf16[8,32,128]{2,1,0:T(8,128)(2,1)S(1)} %collective-permute-done.3.refs_6_) | copy-start | bytes 196612
  33.2 6.8 %copy-start.7 = (bf16[8,288,128]{2,1,0:T(8,128)(2,1)}, bf16[8,288,128]{2,1,0:T(8,128)(2,1)S(1)}, u32[]{:S(2)}) copy-start(bf16[8,288,128]{2,1,0:T(8,128)(2,1)S(1)} %collective-permute-done.2.refs_5_) | copy-start | bytes 1769476
  33.3 3.7 %collective-permute-start.4 = (bf16[2,320,128]{2,1,0:T(8,128)(2,1)S(1)}, bf16[2,320,128]{2,1,0:T(8,128)(2,1)S(1)}, u32[]{:S(2)}, u32[]{:S(2)}) collective-permute-start(bf16[2,320,128]{2,1,0:T(8,128)(2,1)S(1)} %pad_maximum_fusion), channel_id=1, source_target_pairs={{0,1},{1,0},{2,3},{3,2},{4,5},{5,4},{6,7},{7,6},{8,9},{9,8},{10,11... | collective-permute-start | bytes 491528 | tf_op jit(solution)/shard_map/ppermute | solution.py:282
  33.4 6.6 %collective-permute-start.5 = (bf16[2,320,128]{2,1,0:T(8,128)(2,1)S(1)}, bf16[2,320,128]{2,1,0:T(8,128)(2,1)S(1)}, u32[]{:S(2)}, u32[]{:S(2)}) collective-permute-start(bf16[2,320,128]{2,1,0:T(8,128)(2,1)S(1)} %pad_maximum_fusion.1), channel_id=1, source_target_pairs={{1,2},{2,1},{5,6},{6,5},{9,10},{10,9},{13,14},{14,13},{17,18},{18,... | collective-permute-start | bytes 491528 | tf_op jit(solution)/shard_map/ppermute | solution.py:282
  37.0 3.0 %copy-start.9 = (bf16[2,320,128]{2,1,0:T(8,128)(2,1)}, bf16[2,320,128]{2,1,0:T(8,128)(2,1)S(1)}, u32[]{:S(2)}) copy-start(bf16[2,320,128]{2,1,0:T(8,128)(2,1)S(1)} %collective-permute-done.4.refs_7_) | copy-start | bytes 491524
  40.0 0.7 %copy-start.10 = (bf16[2,320,128]{2,1,0:T(8,128)(2,1)}, bf16[2,320,128]{2,1,0:T(8,128)(2,1)S(1)}, u32[]{:S(2)}) copy-start(bf16[2,320,128]{2,1,0:T(8,128)(2,1)S(1)} %collective-permute-done.5.refs_8_) | copy-start | bytes 491524

commit v3 on v2

--- a/solution.py
+++ b/solution.py
@@ -10,7 +10,7 @@
 BF = jnp.bfloat16
 F32 = jnp.float32
 HALO = 16
-LAG = 0
+PACK = 60
 
 
 class Segment:
@@ -24,17 +24,15 @@
     refs = list(refs)
     flags, l_own, r_own, a_any, b_any = refs[:5]
     zl, zr, ca_any, cb_any = refs[5:9] if ext else (None,) * 4
-    k1_any, k2_any = refs[9:11] if ext else refs[5:7]
-    out_any, lrim, rrim, rrev, vf, vs, hf, hs, obuf, k1, k2, sems, osems = refs[-13:]
+    k1, k2 = refs[9:11] if ext else refs[5:7]
+    out_any, lrim, rrim, rrev, vf, vs, hf, hs, obuf, sems, osems = refs[-11:]
     rows, cols, chans = l_own.shape
     pad = HALO if ext else 0
     lpad = disp + HALO if ext else 0
     scale = 1.0 / (chans ** 0.5)
     odd = flags[0] == 1
     if not ext:
-        out_any, done = refs[7:9]
-        done[0] = flags[5]
-        done[1] = flags[6]
+        out_any = refs[7]
 
     def rim(side, main, corner):
         dst = pl.ds(2 * side, 2)
@@ -62,10 +60,6 @@
         for c in rim(0, b_any, cb_any) + rim(1, a_any, ca_any):
             pltpu.make_async_copy(*c).start()
 
-    k1_copy = pltpu.make_async_copy(k1_any, k1, sems.at[2])
-    k2_copy = pltpu.make_async_copy(k2_any, k2, sems.at[3])
-    k1_copy.start()
-    k2_copy.start()
     waited = set()
 
     def wait_rows(row):
@@ -222,10 +216,7 @@
     both(0, rows + 4, volume, True)
     both(2, rows + 4, volume, False)
     both(0, rows + 4, volume, False)
-    k1_copy.wait()
     for row in range(0, rows + 6, 2):
-        if row == 6:
-            k2_copy.wait()
         both(row + 4, rows + 4, volume, True)
         if row < rows + 2:
             hidden(row, 2)
@@ -233,7 +224,7 @@
             out(row - 6, 2)
         flip(row + 6)
         both(row + 4, rows + 4, volume, False)
-        both(row - 2 + LAG, rows + 2, hidden_spreads)
+        both(row - 2, rows + 2, hidden_spreads)
     for c in pending:
         c.wait()
 
@@ -253,24 +244,22 @@
         pltpu.VMEM((rows + 2, disp // 128, m_hid, 128), F32),
         pltpu.VMEM((rows + 2, m_out, 3 * disp), BF),
         pltpu.VMEM((rows, m_out, disp), BF),
-        pltpu.VMEM((9 * disp, disp), BF),
-        pltpu.VMEM((9 * disp, disp), BF),
-        pltpu.SemaphoreType.DMA((4,)),
+        pltpu.SemaphoreType.DMA((2,)),
         pltpu.SemaphoreType.DMA((rows, len(segments))),
     ]
-    vmem, anywhere = pl.BlockSpec(memory_space=pltpu.VMEM), pl.BlockSpec(memory_space=pltpu.HBM)
+    vmem, anywhere = pl.BlockSpec(memory_space=pltpu.VMEM), pl.BlockSpec(memory_space=pl.ANY)
     smem = pl.BlockSpec(memory_space=pltpu.SMEM)
     flops = 2 * 9 * disp * disp * ((rows + 2) * m_hid + rows * m_out)
     return pl.pallas_call(
         functools.partial(part_kernel, segments, ext, disp),
-        out_shape=out_shape if ext else [out_shape, jax.ShapeDtypeStruct((2,), jnp.int32)],
+        out_shape=out_shape if ext else [out_shape, jax.ShapeDtypeStruct((16, 128), BF)],
         in_specs=([smem, vmem, vmem, anywhere, anywhere] + ([vmem, vmem, anywhere, anywhere] if ext else [])
-                  + [anywhere, anywhere] + ([anywhere] if ext else [])),
-        out_specs=anywhere if ext else [anywhere, smem],
+                  + [vmem, vmem] + ([anywhere] if ext else [])),
+        out_specs=anywhere if ext else [anywhere, anywhere],
         scratch_shapes=scratch,
         input_output_aliases={len(operands) - 1: 0} if ext else {},
-        compiler_params=pltpu.CompilerParams(vmem_limit_bytes=54 << 20),
-        cost_estimate=pl.CostEstimate(flops=flops if ext else 1 << 20, bytes_accessed=1 << 20, transcendentals=0),
+        compiler_params=pltpu.CompilerParams(vmem_limit_bytes=44 << 20),
+        cost_estimate=pl.CostEstimate(flops=flops, bytes_accessed=6 << 20, transcendentals=0),
     )(*operands)
 
 
@@ -315,22 +304,45 @@
     zl = pl.pallas_call(
         pack_columns,
         out_shape=jax.ShapeDtypeStruct((rows, disp + 2 * HALO, chans), BF),
-        in_specs=[pl.BlockSpec(memory_space=pltpu.HBM)] * 2,
+        in_specs=[pl.BlockSpec(memory_space=pl.ANY)] * 2,
         out_specs=anywhere,
         scratch_shapes=[pltpu.SemaphoreType.DMA((rows + 1,))],
-        compiler_params=pltpu.CompilerParams(vmem_limit_bytes=1 << 20),
-        cost_estimate=pl.CostEstimate(flops=0, bytes_accessed=1 << 20, transcendentals=0),
+        compiler_params=pltpu.CompilerParams(vmem_limit_bytes=PACK << 20),
+        cost_estimate=pl.CostEstimate(flops=0, bytes_accessed=1 << 10, transcendentals=0),
     )(left, right)
     shapes = [(2, 2 * cols, chans), (2, 2 * cols, chans), (rows, 2 * HALO, chans)]
     return [zl] + list(pl.pallas_call(
         pack_rims,
         out_shape=[jax.ShapeDtypeStruct(s, BF) for s in shapes],
-        in_specs=[pl.BlockSpec(memory_space=pltpu.SMEM)] + [pl.BlockSpec(memory_space=pltpu.HBM)] * 2,
+        in_specs=[pl.BlockSpec(memory_space=pltpu.SMEM)] + [pl.BlockSpec(memory_space=pl.ANY)] * 2,
         out_specs=[anywhere] * 3,
         scratch_shapes=[pltpu.SemaphoreType.DMA((6,))],
+        compiler_params=pltpu.CompilerParams(vmem_limit_bytes=PACK << 20),
+        cost_estimate=pl.CostEstimate(flops=0, bytes_accessed=1 << 10, transcendentals=0),
+    )(flags, left, right))
+
+
+def pack_corners_kernel(flags, zl, zr, _, ca, cb, sems):
+    wide = zl.shape[1]
+    copies = []
+    for msg, at in ((cb, flags[6]), (ca, flags[5])):
+        copies.append((zl.at[pl.ds(at, 2)], msg.at[:, pl.ds(0, wide)]))
+        copies.append((zr.at[pl.ds(at, 2)], msg.at[:, pl.ds(wide, 2 * HALO)]))
+    copy_all(copies, sems)
+
+
+def pack_corners(flags, zl, zr, after):
+    anywhere = pl.BlockSpec(memory_space=pl.ANY)
+    shape = jax.ShapeDtypeStruct((2, zl.shape[1] + zr.shape[1], zl.shape[2]), BF)
+    return pl.pallas_call(
+        pack_corners_kernel,
+        out_shape=[shape, shape],
+        in_specs=[pl.BlockSpec(memory_space=pltpu.SMEM)] + [anywhere] * 3,
+        out_specs=[anywhere] * 2,
+        scratch_shapes=[pltpu.SemaphoreType.DMA((4,))],
         compiler_params=pltpu.CompilerParams(vmem_limit_bytes=1 << 20),
-        cost_estimate=pl.CostEstimate(flops=20 << 30, bytes_accessed=1 << 20, transcendentals=0),
-    )(flags, left, right))
+        cost_estimate=pl.CostEstimate(flops=0, bytes_accessed=1 << 10, transcendentals=0),
+    )(flags, zl, zr, after)
 
 
 def local(left, right, conv_first, conv_second):
@@ -353,13 +365,11 @@
 
     out_shape = jax.ShapeDtypeStruct((rows, cols, disp), BF)
     mid = [Segment(disp, cols - disp - 2 * HALO)]
-    out, done = part_call(mid, False, disp, rows, cols, chans, out_shape, (flags, left, right, a, b, k1, k2))
-
-    def facing(at):
-        return jnp.concatenate([lax.dynamic_slice_in_dim(x, at, 2, 0) for x in (zl, zr)], axis=1)
-
-    cb = pair_permute(facing(done[1]), "row", 1)
-    ca = pair_permute(facing(done[0]), "row", 0)
+    out, after = part_call(mid, False, disp, rows, cols, chans, out_shape, (flags, left, right, a, b, k1, k2))
+
+    ca_msg, cb_msg = pack_corners(flags, zl, zr, after)
+    cb = pair_permute(cb_msg, "row", 1)
+    ca = pair_permute(ca_msg, "row", 0)
     rest = [Segment(-HALO, disp + HALO), Segment(cols - 2 * HALO, HALO)]
     return part_call(rest, True, disp, rows, cols, chans, out_shape,
                      (flags, left, right, a, b, zl, zr, ca, cb, k1, k2, out))

time: 56 us -> 96.1 us (1.72)
  Pallas kernels: 28.3 us -> 77.1 us
  between operations: 4.28 us -> 0.33 us
  local copies, waits for them, and re-layouts: 5.42 us -> 1.95 us
    pallas_call x1, Pallas kernels: 0.69 us -> 35.7 us  [pack(): pl.pallas_call(pack_rims, out_shape=[jax.ShapeDtypeStruct(s, BF) for s in...]
    pallas_call x1, Pallas kernels: 0.82 us -> 19.1 us  [pack(): pl.pallas_call(pack_columns, out_shape=jax.ShapeDtypeStruct((rows, disp +...]
    pallas_call x2, Pallas kernels: 26.8 us -> 21.6 us  [part_call(): pl.pallas_call(functools.partial(part_kernel, segments, ext, disp), out_s...]
    unnamed x22 -> x12, local copies, waits for them, and re-layouts: 3.93 us -> 1.28 us
    slice x1 -> x0, local copies, waits for them, and re-layouts: 1.36 us -> none  [local(): cb = pair_permute(facing(done[1]), 'row', 1)]
    ppermute x4, waiting for transfers between devices: 4.74 us -> 3.71 us  [pair_permute(): return lax.ppermute(x, axis, perm)]
  transfers between devices with their start and end apart: 6 -> 6, of which waited for: 2 -> 2; matrix products, arithmetic and copies ran while one was open for 2% -> 0% of each run, Pallas kernels for 23% -> 29%
where the time goes in v3:
time: 96.1 us; the launch traced here: 95.8 us
  Pallas kernels  77.1 us (80%)
  starting transfers between devices  12.1 us (13%)
  waiting for transfers between devices  4.28 us (4%)
  local copies, waits for them, and re-layouts  1.95 us (2%)
    pallas_call x1, Pallas kernels, pack(): pl.pallas_call(pack_rims, out_shape=[jax.ShapeDtypeStruct(s, BF) for s in...  35.7 us
    pallas_call x2, Pallas kernels, part_call(): pl.pallas_call(functools.partial(part_kernel, segments, ext, disp), out_s...  21.6 us
    pallas_call x1, Pallas kernels, pack(): pl.pallas_call(pack_columns, out_shape=jax.ShapeDtypeStruct((rows, disp +...  19.1 us
    ppermute x4, starting transfers between devices, pair_permute(): return lax.ppermute(x, axis, perm)  7.57 us
    ppermute x4, waiting for transfers between devices, pair_permute(): return lax.ppermute(x, axis, perm)  3.71 us
    ppermute x1, starting transfers between devices, local(): zl = lax.ppermute(zl_msg, 'col', [(i, i + 1) for i in range(n_col - 1)])  3.24 us
  transfers between devices with their start and end apart: 6, of which 2 were waited for; matrix products, arithmetic and copies ran while one was open for 0% of the time, Pallas kernels for 29%

profile of v3, /device:TPU:1, one launch (start us, length us, event | category | flops | bytes accessed | tf_op | source)
XLA Modules:
  0.0 95.8 jit_solution(2811779709709001876)
XLA Ops:
  0.0 0.7 stack.47.flags.refs_0_
  0.7 35.7 %shard_map.46 = (bf16[2,1024,128]{2,1,0:T(8,128)(2,1)}, bf16[2,1024,128]{2,1,0:T(8,128)(2,1)}, bf16[8,32,128]{2,1,0:T(8,128)(2,1)}) custom-call(s32[7]{0:T(128)} %stack.47.flags.refs_0_, bf16[8,512,128]{2,1,0:T(8,128)(2,1)} %refs_1_.3, bf16[8,512,128]{2,1,0:T(8,128)(2,1)} %refs_2_.3), custom_call_target="tpu_custom_call" | custom-call | bytes 1024 | tf_op jit(solution)/shard_map/pallas_call | solution.py:314
  36.4 0.1 collective-permute-start
  36.5 4.5 %collective-permute-start.1 = (bf16[2,1024,128]{2,1,0:T(8,128)(2,1)}, bf16[2,1024,128]{2,1,0:T(8,128)(2,1)}, u32[]{:S(2)}, u32[]{:S(2)}) collective-permute-start(bf16[2,1024,128]{2,1,0:T(8,128)(2,1)} %get-tuple-element.13), channel_id=1, source_target_pairs={{1,2},{2,1},{5,6},{6,5},{9,10},{10,9},{13,14},{14,13},{17,18},{18,... | collective-permute-start | bytes 1572872 | tf_op jit(solution)/shard_map/ppermute | solution.py:271
  41.0 19.1 %shard_map.47 = bf16[8,288,128]{2,1,0:T(8,128)(2,1)} custom-call(bf16[8,512,128]{2,1,0:T(8,128)(2,1)} %refs_1_.3, bf16[8,512,128]{2,1,0:T(8,128)(2,1)} %refs_2_.3), custom_call_target="tpu_custom_call" | custom-call | bytes 1024 | tf_op jit(solution)/shard_map/pallas_call | solution.py:304
  60.1 3.2 %collective-permute-start.2 = (bf16[8,288,128]{2,1,0:T(8,128)(2,1)}, bf16[8,288,128]{2,1,0:T(8,128)(2,1)S(1)}, u32[]{:S(2)}, u32[]{:S(2)}) collective-permute-start(bf16[8,288,128]{2,1,0:T(8,128)(2,1)} %shard_map.47), channel_id=1, source_target_pairs={{0,4},{4,8},{8,12},{1,5},{5,9},{9,13},{2,6},{6,10},{10,14},{3,7},{... | collective-permute-start | bytes 1769480 | tf_op jit(solution)/shard_map/ppermute | solution.py:361
  63.3 1.3 %collective-permute-start.3 = (bf16[8,32,128]{2,1,0:T(8,128)(2,1)S(1)}, bf16[8,32,128]{2,1,0:T(8,128)(2,1)S(1)}, u32[]{:S(2)}, u32[]{:S(2)}) collective-permute-start(bf16[8,32,128]{2,1,0:T(8,128)(2,1)S(1)} %copy-done.5), channel_id=1, source_target_pairs={{4,0},{8,4},{12,8},{5,1},{9,5},{13,9},{6,2},{10,6},{14,10},{7,3},{... | collective-permute-start | bytes 196616 | tf_op jit(solution)/shard_map/ppermute | solution.py:364
  64.6 0.0 collective-permute-done.refs_3_
  64.6 0.0 collective-permute-done.1.refs_4_
  64.6 0.0 copy-done
  64.6 0.0 copy-done.1
  64.7 0.0 copy-done.2
  64.7 0.0 copy-done.3
  64.7 0.0 copy-start.4
  64.7 1.3 %copy-done.4 = bf16[3,3,256,256]{3,2,1,0:T(8,128)(2,1)S(1)} copy-done((bf16[3,3,256,256]{3,2,1,0:T(8,128)(2,1)S(1)}, bf16[3,3,256,256]{3,2,1,0:T(8,128)(2,1)}, u32[]{:S(2)}) %copy-start.4) | copy-done | bytes 1179672
  65.9 9.1 %shard_map.48 = (bf16[8,512,256]{2,1,0:T(8,128)(2,1)}, bf16[16,128]{1,0:T(8,128)(2,1)S(1)}) custom-call(s32[7]{0:T(128)S(1)} %copy-done.2, bf16[8,512,128]{2,1,0:T(8,128)(2,1)S(1)} %copy-done, bf16[8,512,128]{2,1,0:T(8,128)(2,1)S(1)} %copy-done.1, bf16[2,1024,128]{2,1,0:T(8,128)(2,1)S(1)} %collective-permute-done.refs_3_, ...), custom_call_target="tpu_custom_call" | custom-call | flops 4945084416 | bytes 6291456 | tf_op jit(solution)/shard_map/pallas_call | solution.py:253
  75.1 0.0 collective-permute-done.3.zr.refs_6_
  75.1 0.6 collective-permute-done.2.zl.refs_5_
  75.6 0.8 shard_map.49
  76.4 0.1 collective-permute-start.4
  76.5 2.9 %collective-permute-start.5 = (bf16[2,320,128]{2,1,0:T(8,128)(2,1)S(1)}, bf16[2,320,128]{2,1,0:T(8,128)(2,1)S(1)}, u32[]{:S(2)}, u32[]{:S(2)}) collective-permute-start(bf16[2,320,128]{2,1,0:T(8,128)(2,1)S(1)} %get-tuple-element.17), channel_id=1, source_target_pairs={{1,2},{2,1},{5,6},{6,5},{9,10},{10,9},{13,14},{14,13},{17,18},{18,... | collective-permute-start | bytes 491528 | tf_op jit(solution)/shard_map/ppermute | solution.py:271
  79.4 0.0 collective-permute-done.4.refs_7_
  79.4 3.7 %collective-permute-done.5.refs_8_ = bf16[2,320,128]{2,1,0:T(8,128)(2,1)S(1)} collective-permute-done((bf16[2,320,128]{2,1,0:T(8,128)(2,1)S(1)}, bf16[2,320,128]{2,1,0:T(8,128)(2,1)S(1)}, u32[]{:S(2)}, u32[]{:S(2)}) %collective-permute-start.5) | collective-permute-done | bytes 163872 | tf_op jit(solution)/shard_map/ppermute | solution.py:271
  83.1 12.5 %shard_map.50 = bf16[8,512,256]{2,1,0:T(8,128)(2,1)} custom-call(s32[7]{0:T(128)S(1)} %copy-done.2, bf16[8,512,128]{2,1,0:T(8,128)(2,1)S(1)} %copy-done, bf16[8,512,128]{2,1,0:T(8,128)(2,1)S(1)} %copy-done.1, bf16[2,1024,128]{2,1,0:T(8,128)(2,1)S(1)} %collective-permute-done.refs_3_, ...), custom_call_target="tpu_custom_call", output_to_operand_aliasing={{}: (11, {})} | custom-call | flops 6492782592 | bytes 6291456 | tf_op jit(solution)/shard_map/pallas_call | solution.py:253
  (6 shorter events, 0.0 us)
Async XLA Ops:
  0.7 64.0 %copy-start = (bf16[8,512,128]{2,1,0:T(8,128)(2,1)S(1)}, bf16[8,512,128]{2,1,0:T(8,128)(2,1)}, u32[]{:S(2)}) copy-start(bf16[8,512,128]{2,1,0:T(8,128)(2,1)} %refs_1_.3) | copy-start | bytes 3145732
  0.7 64.0 %copy-start.1 = (bf16[8,512,128]{2,1,0:T(8,128)(2,1)S(1)}, bf16[8,512,128]{2,1,0:T(8,128)(2,1)}, u32[]{:S(2)}) copy-start(bf16[8,512,128]{2,1,0:T(8,128)(2,1)} %refs_2_.3) | copy-start | bytes 3145732
  0.7 64.0 %copy-start.2 = (s32[7]{0:T(128)S(1)}, s32[7]{0:T(128)}, u32[]{:S(2)}) copy-start(s32[7]{0:T(128)} %stack.47.flags.refs_0_) | copy-start | bytes 88
  0.7 64.0 %copy-start.3 = (bf16[3,3,256,256]{3,2,1,0:T(8,128)(2,1)S(1)}, bf16[3,3,256,256]{3,2,1,0:T(8,128)(2,1)}, u32[]{:S(2)}) copy-start(bf16[3,3,256,256]{3,2,1,0:T(8,128)(2,1)} %param.6) | copy-start | bytes 3538948
  36.4 26.9 %copy-start.5 = (bf16[8,32,128]{2,1,0:T(8,128)(2,1)S(1)}, bf16[8,32,128]{2,1,0:T(8,128)(2,1)}, u32[]{:S(2)}) copy-start(bf16[8,32,128]{2,1,0:T(8,128)(2,1)} %get-tuple-element.14) | copy-start | bytes 196612
  36.4 28.2 %collective-permute-start = (bf16[2,1024,128]{2,1,0:T(8,128)(2,1)}, bf16[2,1024,128]{2,1,0:T(8,128)(2,1)S(1)}, u32[]{:S(2)}, u32[]{:S(2)}) collective-permute-start(bf16[2,1024,128]{2,1,0:T(8,128)(2,1)} %get-tuple-element.12), channel_id=1, source_target_pairs={{0,1},{1,0},{2,3},{3,2},{4,5},{5,4},{6,7},{7,6},{8,9},{9,8},{10,11... | collective-permute-start | bytes 1572872 | tf_op jit(solution)/shard_map/ppermute | solution.py:271
  36.5 28.1 %collective-permute-start.1 = (bf16[2,1024,128]{2,1,0:T(8,128)(2,1)}, bf16[2,1024,128]{2,1,0:T(8,128)(2,1)}, u32[]{:S(2)}, u32[]{:S(2)}) collective-permute-start(bf16[2,1024,128]{2,1,0:T(8,128)(2,1)} %get-tuple-element.13), channel_id=1, source_target_pairs={{1,2},{2,1},{5,6},{6,5},{9,10},{10,9},{13,14},{14,13},{17,18},{18,... | collective-permute-start | bytes 1572872 | tf_op jit(solution)/shard_map/ppermute | solution.py:271
  60.1 15.6 %collective-permute-start.2 = (bf16[8,288,128]{2,1,0:T(8,128)(2,1)}, bf16[8,288,128]{2,1,0:T(8,128)(2,1)S(1)}, u32[]{:S(2)}, u32[]{:S(2)}) collective-permute-start(bf16[8,288,128]{2,1,0:T(8,128)(2,1)} %shard_map.47), channel_id=1, source_target_pairs={{0,4},{4,8},{8,12},{1,5},{5,9},{9,13},{2,6},{6,10},{10,14},{3,7},{... | collective-permute-start | bytes 1769480 | tf_op jit(solution)/shard_map/ppermute | solution.py:361
  63.3 11.7 %collective-permute-start.3 = (bf16[8,32,128]{2,1,0:T(8,128)(2,1)S(1)}, bf16[8,32,128]{2,1,0:T(8,128)(2,1)S(1)}, u32[]{:S(2)}, u32[]{:S(2)}) collective-permute-start(bf16[8,32,128]{2,1,0:T(8,128)(2,1)S(1)} %copy-done.5), channel_id=1, source_target_pairs={{4,0},{8,4},{12,8},{5,1},{9,5},{13,9},{6,2},{10,6},{14,10},{7,3},{... | collective-permute-start | bytes 196616 | tf_op jit(solution)/shard_map/ppermute | solution.py:364
  64.7 1.3 %copy-start.4 = (bf16[3,3,256,256]{3,2,1,0:T(8,128)(2,1)S(1)}, bf16[3,3,256,256]{3,2,1,0:T(8,128)(2,1)}, u32[]{:S(2)}) copy-start(bf16[3,3,256,256]{3,2,1,0:T(8,128)(2,1)} %param.7) | copy-start | bytes 3538948
  76.4 3.0 %collective-permute-start.4 = (bf16[2,320,128]{2,1,0:T(8,128)(2,1)S(1)}, bf16[2,320,128]{2,1,0:T(8,128)(2,1)S(1)}, u32[]{:S(2)}, u32[]{:S(2)}) collective-permute-start(bf16[2,320,128]{2,1,0:T(8,128)(2,1)S(1)} %get-tuple-element.16), channel_id=1, source_target_pairs={{0,1},{1,0},{2,3},{3,2},{4,5},{5,4},{6,7},{7,6},{8,9},{9,8},{10,11... | collective-permute-start | bytes 491528 | tf_op jit(solution)/shard_map/ppermute | solution.py:271
  76.5 6.6 %collective-permute-start.5 = (bf16[2,320,128]{2,1,0:T(8,128)(2,1)S(1)}, bf16[2,320,128]{2,1,0:T(8,128)(2,1)S(1)}, u32[]{:S(2)}, u32[]{:S(2)}) collective-permute-start(bf16[2,320,128]{2,1,0:T(8,128)(2,1)S(1)} %get-tuple-element.17), channel_id=1, source_target_pairs={{1,2},{2,1},{5,6},{6,5},{9,10},{10,9},{13,14},{14,13},{17,18},{18,... | collective-permute-start | bytes 491528 | tf_op jit(solution)/shard_map/ppermute | solution.py:271

commit v4 on v3

--- a/solution.py
+++ b/solution.py
@@ -22,77 +22,40 @@
 
 def part_kernel(segments, ext, disp, *refs):
     refs = list(refs)
-    flags, l_own, r_own, a_any, b_any = refs[:5]
-    zl, zr, ca_any, cb_any = refs[5:9] if ext else (None,) * 4
+    flags, l_own, r_own, a_ref, b_ref = refs[:5]
+    zl, zr, ca, cb = refs[5:9] if ext else (None,) * 4
     k1, k2 = refs[9:11] if ext else refs[5:7]
-    out_any, lrim, rrim, rrev, vf, vs, hf, hs, obuf, sems, osems = refs[-11:]
+    out_any, (rrev, vf, vs, hf, hs, obuf, osems) = refs[-9 if not ext else -8], refs[-7:]
     rows, cols, chans = l_own.shape
     pad = HALO if ext else 0
     lpad = disp + HALO if ext else 0
     scale = 1.0 / (chans ** 0.5)
-    odd = flags[0] == 1
-    if not ext:
-        out_any = refs[7]
-
-    def rim(side, main, corner):
-        dst = pl.ds(2 * side, 2)
-        out = [
-            (main.at[:, pl.ds(0, cols)], lrim.at[dst, pl.ds(pad, cols)], sems.at[side]),
-            (main.at[:, pl.ds(cols, cols)], rrim.at[dst, pl.ds(lpad, cols)], sems.at[side]),
-        ]
-        if ext:
-            wide = lpad + pad
-            out += [
-                (corner.at[:, pl.ds(0, lpad)], rrim.at[dst, pl.ds(0, lpad)], sems.at[side]),
-                (corner.at[:, pl.ds(lpad, pad)], lrim.at[dst, pl.ds(0, pad)], sems.at[side]),
-                (corner.at[:, pl.ds(wide, pad)], rrim.at[dst, pl.ds(lpad + cols, pad)], sems.at[side]),
-                (corner.at[:, pl.ds(wide + pad, pad)], lrim.at[dst, pl.ds(pad + cols, pad)], sems.at[side]),
-            ]
-        return out
-
-    @pl.when(odd)
-    def _():
-        for c in rim(0, a_any, ca_any) + rim(1, b_any, cb_any):
-            pltpu.make_async_copy(*c).start()
-
-    @pl.when(jnp.logical_not(odd))
-    def _():
-        for c in rim(0, b_any, cb_any) + rim(1, a_any, ca_any):
-            pltpu.make_async_copy(*c).start()
-
-    waited = set()
-
-    def wait_rows(row):
-        side = 0 if row < 2 else 1 if row >= rows + 2 else None
-        if side is not None and side not in waited:
-            waited.add(side)
-            for c in rim(side, a_any, ca_any):
-                pltpu.make_async_copy(*c).wait()
-
-    def pieces(row, lo, n, right):
-        if row < 2 or row >= rows + 2:
-            at = row if row < 2 else row - rows
-            ref, off = (rrim, lpad) if right else (lrim, pad)
-            return [ref[at, lo + off:lo + off + n, :]]
-        row -= 2
+    odd = flags[0].astype(F32)
+
+    def pieces(row, lo, n, right, own, left_edge, right_edge):
         out = []
         if lo < 0:
             m = min(n, -lo)
-            at = lo + lpad if right else lo + lpad + pad
-            out.append(zl[row, at:at + m, :])
+            at = left_edge[1] + lo + lpad if right else left_edge[1] + lpad + pad + lo
+            out.append(left_edge[0][row, at:at + m, :])
             lo, n = lo + m, n - m
         if n and lo < cols:
             m = min(n, cols - lo)
-            out.append((r_own if right else l_own)[row, lo:lo + m, :])
+            out.append(own[0][row, own[1] + lo:own[1] + lo + m, :])
             lo, n = lo + m, n - m
         if n:
-            at = lo - cols + (0 if right else pad)
-            out.append(zr[row, at:at + n, :])
-        return out
+            at = right_edge[1] + lo - cols + (0 if right else pad)
+            out.append(right_edge[0][row, at:at + n, :])
+        return out[0] if len(out) == 1 else jnp.concatenate(out, axis=0)
 
     def columns(row, lo, n, right):
-        parts = pieces(row, lo, n, right)
-        return parts[0] if len(parts) == 1 else jnp.concatenate(parts, axis=0)
+        if 2 <= row < rows + 2:
+            return pieces(row - 2, lo, n, right, (r_own if right else l_own, 0), (zl, 0), (zr, 0))
+        at, share = (row, odd) if row < 2 else (row - rows - 2, 1.0 - odd)
+        start = cols if right else 0
+        one = pieces(at, lo, n, right, (a_ref, start), (ca, 0), (ca, lpad + pad))
+        two = pieces(at, lo, n, right, (b_ref, start), (cb, 0), (cb, lpad + pad))
+        return (one.astype(F32) * share + two.astype(F32) * (1.0 - share)).astype(BF)
 
     mirror = 7 - lax.broadcasted_iota(jnp.int32, (8, 128), 0)
 
@@ -111,8 +74,6 @@
                 rrev[s, row + q, span - 128 * t - n:span - 128 * t, :] = res[:, chans * q:chans * (q + 1)]
 
         if row < rows + 4:
-            wait_rows(row)
-            wait_rows(row + 1)
             for s, seg in enumerate(segments):
                 for t in range(-(-(seg.vol + disp) // 128)):
                     unit(s, seg, t)
@@ -236,15 +197,12 @@
     pad = HALO if ext else 0
     span = max(128 * -(-s.vol // 128) + disp for s in segments)
     scratch = [
-        pltpu.VMEM((4, cols + 2 * pad, chans), BF),
-        pltpu.VMEM((4, cols + 2 * pad + (disp if ext else 0), chans), BF),
         pltpu.VMEM((len(segments), rows + 4, span, chans), BF),
         pltpu.VMEM((rows + 4, disp // 128, m_vol, 128), F32),
         pltpu.VMEM((rows + 4, m_hid, 3 * disp), BF),
         pltpu.VMEM((rows + 2, disp // 128, m_hid, 128), F32),
         pltpu.VMEM((rows + 2, m_out, 3 * disp), BF),
         pltpu.VMEM((rows, m_out, disp), BF),
-        pltpu.SemaphoreType.DMA((2,)),
         pltpu.SemaphoreType.DMA((rows, len(segments))),
     ]
     vmem, anywhere = pl.BlockSpec(memory_space=pltpu.VMEM), pl.BlockSpec(memory_space=pl.ANY)
@@ -253,7 +211,7 @@
     return pl.pallas_call(
         functools.partial(part_kernel, segments, ext, disp),
         out_shape=out_shape if ext else [out_shape, jax.ShapeDtypeStruct((16, 128), BF)],
-        in_specs=([smem, vmem, vmem, anywhere, anywhere] + ([vmem, vmem, anywhere, anywhere] if ext else [])
+        in_specs=([smem] + [vmem] * (8 if ext else 4)
                   + [vmem, vmem] + ([anywhere] if ext else [])),
         out_specs=anywhere if ext else [anywhere, anywhere],
         scratch_shapes=scratch,
@@ -279,47 +237,51 @@
         c.wait()
 
 
-def pack_columns(l_any, r_any, zl, sems):
+def pack_kernel(flags, l_any, r_any, zl, a, b, zr, zl_buf, a_buf, b_buf, zr_buf, in_sems, out_sems):
     rows, cols, _ = l_any.shape
     wide = zl.shape[1] - HALO
-    copies = [(r_any.at[q, pl.ds(cols - wide, wide)], zl.at[q, pl.ds(0, wide)]) for q in range(rows)]
-    copies.append((l_any.at[:, pl.ds(cols - HALO, HALO)], zl.at[:, pl.ds(wide, HALO)]))
-    copy_all(copies, sems)
-
-
-def pack_rims(flags, l_any, r_any, a, b, zr, sems):
-    cols = l_any.shape[1]
-    copies = []
-    for msg, at in ((b, flags[6]), (a, flags[5])):
-        copies.append((l_any.at[pl.ds(at, 2)], msg.at[:, pl.ds(0, cols)]))
-        copies.append((r_any.at[pl.ds(at, 2)], msg.at[:, pl.ds(cols, cols)]))
-    copies.append((r_any.at[:, pl.ds(0, HALO)], zr.at[:, pl.ds(0, HALO)]))
-    copies.append((l_any.at[:, pl.ds(0, HALO)], zr.at[:, pl.ds(HALO, HALO)]))
-    copy_all(copies, sems)
+    half = rows // 2
+    fills = {
+        0: [(r_any.at[pl.ds(0, half), pl.ds(cols - wide, wide)], zl_buf.at[pl.ds(0, half), pl.ds(0, wide)]),
+                 (r_any.at[pl.ds(half, rows - half), pl.ds(cols - wide, wide)],
+                  zl_buf.at[pl.ds(half, rows - half), pl.ds(0, wide)]),
+                 (l_any.at[:, pl.ds(cols - HALO, HALO)], zl_buf.at[:, pl.ds(wide, HALO)])],
+        3: [(r_any.at[:, pl.ds(0, HALO)], zr_buf.at[:, pl.ds(0, HALO)]),
+                 (l_any.at[:, pl.ds(0, HALO)], zr_buf.at[:, pl.ds(HALO, HALO)])],
+    }
+    for i, buf, at in ((1, b_buf, flags[6]), (2, a_buf, flags[5])):
+        fills[i] = [(l_any.at[pl.ds(at, 2)], buf.at[:, pl.ds(0, cols)]),
+                      (r_any.at[pl.ds(at, 2)], buf.at[:, pl.ds(cols, cols)])]
+    order = ((zl_buf, zl), (b_buf, b), (a_buf, a), (zr_buf, zr))
+    started = []
+    for i, (buf, _) in enumerate(order):
+        started.append([pltpu.make_async_copy(src, dst, in_sems.at[i, j]) for j, (src, dst) in enumerate(fills[i])])
+        for c in started[-1]:
+            c.start()
+    sends = []
+    for i, (buf, msg) in enumerate(order):
+        for c in started[i]:
+            c.wait()
+        sends.append(pltpu.make_async_copy(buf, msg, out_sems.at[i]))
+        sends[-1].start()
+    for c in sends:
+        c.wait()
 
 
 def pack(flags, left, right, disp):
     rows, cols, chans = left.shape
     anywhere = pl.BlockSpec(memory_space=pl.ANY)
-    zl = pl.pallas_call(
-        pack_columns,
-        out_shape=jax.ShapeDtypeStruct((rows, disp + 2 * HALO, chans), BF),
-        in_specs=[pl.BlockSpec(memory_space=pl.ANY)] * 2,
-        out_specs=anywhere,
-        scratch_shapes=[pltpu.SemaphoreType.DMA((rows + 1,))],
+    shapes = [(rows, disp + 2 * HALO, chans), (2, 2 * cols, chans), (2, 2 * cols, chans), (rows, 2 * HALO, chans)]
+    return pl.pallas_call(
+        pack_kernel,
+        out_shape=[jax.ShapeDtypeStruct(s, BF) for s in shapes],
+        in_specs=[pl.BlockSpec(memory_space=pltpu.SMEM), anywhere, anywhere],
+        out_specs=[anywhere] * 4,
+        scratch_shapes=[pltpu.VMEM(s, BF) for s in shapes]
+        + [pltpu.SemaphoreType.DMA((4, 3)), pltpu.SemaphoreType.DMA((4,))],
         compiler_params=pltpu.CompilerParams(vmem_limit_bytes=PACK << 20),
         cost_estimate=pl.CostEstimate(flops=0, bytes_accessed=1 << 10, transcendentals=0),
-    )(left, right)
-    shapes = [(2, 2 * cols, chans), (2, 2 * cols, chans), (rows, 2 * HALO, chans)]
-    return [zl] + list(pl.pallas_call(
-        pack_rims,
-        out_shape=[jax.ShapeDtypeStruct(s, BF) for s in shapes],
-        in_specs=[pl.BlockSpec(memory_space=pltpu.SMEM)] + [pl.BlockSpec(memory_space=pl.ANY)] * 2,
-        out_specs=[anywhere] * 3,
-        scratch_shapes=[pltpu.SemaphoreType.DMA((6,))],
-        compiler_params=pltpu.CompilerParams(vmem_limit_bytes=PACK << 20),
-        cost_estimate=pl.CostEstimate(flops=0, bytes_accessed=1 << 10, transcendentals=0),
-    )(flags, left, right))
+    )(flags, left, right)
 
 
 def pack_corners_kernel(flags, zl, zr, _, ca, cb, sems):

time: 96.1 us -> 45.4 us (0.47)
  Pallas kernels: 77.1 us -> 23.2 us
  waiting for transfers between devices: 4.28 us -> 5.57 us
  local copies, waits for them, and re-layouts: 1.95 us -> 3.12 us
    pallas_call x2 -> x1, Pallas kernels: 54.8 us -> 3.14 us  [pack(): pl.pallas_call(pack_kernel, out_shape=[jax.ShapeDtypeStruct(s, BF) for s...]
    pallas_call x2, Pallas kernels: 21.6 us -> 19.2 us  [part_call(): pl.pallas_call(functools.partial(part_kernel, segments, ext, disp), out_s...]
    ppermute x4, waiting for transfers between devices: 3.71 us -> 5.56 us  [pair_permute(): return lax.ppermute(x, axis, perm)]
    unnamed x12 -> x10, local copies, waits for them, and re-layouts: 1.28 us -> 2.55 us
  transfers between devices with their start and end apart: 6 -> 6, of which waited for: 2 -> 2; matrix products, arithmetic and copies ran while one was open for 0% -> 0% of each run, Pallas kernels for 29% -> 18%
where the time goes in v4:
time: 45.4 us; the launch traced here: 45.1 us
  Pallas kernels  23.2 us (51%)
  starting transfers between devices  13 us (29%)
  waiting for transfers between devices  5.57 us (12%)
  local copies, waits for them, and re-layouts  3.12 us (7%)
    pallas_call x2, Pallas kernels, part_call(): pl.pallas_call(functools.partial(part_kernel, segments, ext, disp), out_s...  19.2 us
    ppermute x4, starting transfers between devices, pair_permute(): return lax.ppermute(x, axis, perm)  8.48 us
    ppermute x4, waiting for transfers between devices, pair_permute(): return lax.ppermute(x, axis, perm)  5.56 us
    ppermute x1, starting transfers between devices, local(): zl = lax.ppermute(zl_msg, 'col', [(i, i + 1) for i in range(n_col - 1)])  3.24 us
    pallas_call x1, Pallas kernels, pack(): pl.pallas_call(pack_kernel, out_shape=[jax.ShapeDtypeStruct(s, BF) for s...  3.14 us
    unnamed x10, local copies, waits for them, and re-layouts  2.55 us
    ppermute x1, starting transfers between devices, local(): zr = lax.ppermute(zr_msg, 'col', [(i + 1, i) for i in range(n_col - 1)])  1.29 us
  transfers between devices with their start and end apart: 6, of which 2 were waited for; matrix products, arithmetic and copies ran while one was open for 0% of the time, Pallas kernels for 18%

profile of v4, /device:TPU:1, one launch (start us, length us, event | category | flops | bytes accessed | tf_op | source)
XLA Modules:
  0.0 45.1 jit_solution(10035191460417074111)
XLA Ops:
  0.0 0.0 copy-start.1
  0.0 0.6 %stack.47.flags.refs_0_ = s32[7]{0:T(128)} concatenate(s32[1]{0:T(128)} %bitcast, s32[1]{0:T(128)} %bitcast.1, s32[1]{0:T(128)} %bitcast.2, s32[1]{0:T(128)} %bitcast.3, s32[1]{0:T(128)} %bitcast.4, s32[1]{0:T(128)} %bitcast.5, s32[1]{0:T(128)} %bitcast.6), dimensions={0} | concatenate | bytes 56 | tf_op jit(solution)/shard_map/stack | solution.py:318
  0.6 3.1 %shard_map.46 = (bf16[8,288,128]{2,1,0:T(8,128)(2,1)}, bf16[2,1024,128]{2,1,0:T(8,128)(2,1)}, bf16[2,1024,128]{2,1,0:T(8,128)(2,1)}, bf16[8,32,128]{2,1,0:T(8,128)(2,1)}) custom-call(s32[7]{0:T(128)} %stack.47.flags.refs_0_, bf16[8,512,128]{2,1,0:T(8,128)(2,1)} %refs_1_.3, bf16[8,512,128]{2,1,0:T(8,128)(2,1)} %refs_2_.3), custom_call_target="tpu_custom_call" | custom-call | bytes 1024 | tf_op jit(solution)/shard_map/pallas_call | solution.py:275
  3.7 0.3 collective-permute-start
  4.0 4.5 %collective-permute-start.1 = (bf16[2,1024,128]{2,1,0:T(8,128)(2,1)}, bf16[2,1024,128]{2,1,0:T(8,128)(2,1)S(1)}, u32[]{:S(2)}, u32[]{:S(2)}) collective-permute-start(bf16[2,1024,128]{2,1,0:T(8,128)(2,1)} %get-tuple-element.14), channel_id=1, source_target_pairs={{1,2},{2,1},{5,6},{6,5},{9,10},{10,9},{13,14},{14,13},{17,18},{18,... | collective-permute-start | bytes 1572872 | tf_op jit(solution)/shard_map/ppermute | solution.py:229
  8.4 3.2 %collective-permute-start.2 = (bf16[8,288,128]{2,1,0:T(8,128)(2,1)}, bf16[8,288,128]{2,1,0:T(8,128)(2,1)S(1)}, u32[]{:S(2)}, u32[]{:S(2)}) collective-permute-start(bf16[8,288,128]{2,1,0:T(8,128)(2,1)} %get-tuple-element.15), channel_id=1, source_target_pairs={{0,4},{4,8},{8,12},{1,5},{5,9},{9,13},{2,6},{6,10},{10,14},{3,7},{... | collective-permute-start | bytes 1769480 | tf_op jit(solution)/shard_map/ppermute | solution.py:323
  11.7 1.3 %collective-permute-start.3 = (bf16[8,32,128]{2,1,0:T(8,128)(2,1)}, bf16[8,32,128]{2,1,0:T(8,128)(2,1)S(1)}, u32[]{:S(2)}, u32[]{:S(2)}) collective-permute-start(bf16[8,32,128]{2,1,0:T(8,128)(2,1)} %get-tuple-element.16), channel_id=1, source_target_pairs={{4,0},{8,4},{12,8},{5,1},{9,5},{13,9},{6,2},{10,6},{14,10},{7,3},{... | collective-permute-start | bytes 196616 | tf_op jit(solution)/shard_map/ppermute | solution.py:326
  13.0 0.0 collective-permute-done.refs_3_
  13.0 2.6 %collective-permute-done.1.refs_4_ = bf16[2,1024,128]{2,1,0:T(8,128)(2,1)S(1)} collective-permute-done((bf16[2,1024,128]{2,1,0:T(8,128)(2,1)}, bf16[2,1024,128]{2,1,0:T(8,128)(2,1)S(1)}, u32[]{:S(2)}, u32[]{:S(2)}) %collective-permute-start.1) | collective-permute-done | bytes 524320 | tf_op jit(solution)/shard_map/ppermute | solution.py:229
  15.6 0.0 copy-done.1
  15.6 0.0 copy-done
  15.6 0.0 copy-done.2
  15.6 0.0 copy-start.3
  15.7 1.3 %copy-done.3 = bf16[3,3,256,256]{3,2,1,0:T(8,128)(2,1)S(1)} copy-done((bf16[3,3,256,256]{3,2,1,0:T(8,128)(2,1)S(1)}, bf16[3,3,256,256]{3,2,1,0:T(8,128)(2,1)}, u32[]{:S(2)}) %copy-start.3) | copy-done | bytes 1179672
  16.9 1.3 %copy-done.4 = bf16[3,3,256,256]{3,2,1,0:T(8,128)(2,1)S(1)} copy-done((bf16[3,3,256,256]{3,2,1,0:T(8,128)(2,1)S(1)}, bf16[3,3,256,256]{3,2,1,0:T(8,128)(2,1)}, u32[]{:S(2)}) %copy-start.4) | copy-done | bytes 1179672
  18.2 8.1 %shard_map.47 = (bf16[8,512,256]{2,1,0:T(8,128)(2,1)}, bf16[16,128]{1,0:T(8,128)(2,1)S(1)}) custom-call(s32[7]{0:T(128)S(1)} %copy-done.2, bf16[8,512,128]{2,1,0:T(8,128)(2,1)S(1)} %copy-done, bf16[8,512,128]{2,1,0:T(8,128)(2,1)S(1)} %copy-done.1, bf16[2,1024,128]{2,1,0:T(8,128)(2,1)S(1)} %collective-permute-done.refs_3_, ...), custom_call_target="tpu_custom_call" | custom-call | flops 4945084416 | bytes 6291456 | tf_op jit(solution)/shard_map/pallas_call | solution.py:211
  26.3 0.0 collective-permute-done.3.zr.refs_6_
  26.3 0.0 collective-permute-done.2.zl.refs_5_
  26.3 0.8 %shard_map.48 = (bf16[2,320,128]{2,1,0:T(8,128)(2,1)S(1)}, bf16[2,320,128]{2,1,0:T(8,128)(2,1)S(1)}) custom-call(s32[7]{0:T(128)S(1)} %copy-done.2, bf16[8,288,128]{2,1,0:T(8,128)(2,1)S(1)} %collective-permute-done.2.zl.refs_5_, bf16[8,32,128]{2,1,0:T(8,128)(2,1)S(1)} %collective-permute-done.3.zr.refs_6_, bf16[16,128]{1,0:T(8,128)(2,1)S(1)} %get-tuple-element.17._), custom_call_target="tpu_custom_call" | custom-call | bytes 1024 | tf_op jit(solution)/shard_map/pallas_call | solution.py:299
  27.1 0.1 collective-permute-start.4
  27.2 3.7 %collective-permute-start.5 = (bf16[2,320,128]{2,1,0:T(8,128)(2,1)S(1)}, bf16[2,320,128]{2,1,0:T(8,128)(2,1)S(1)}, u32[]{:S(2)}, u32[]{:S(2)}) collective-permute-start(bf16[2,320,128]{2,1,0:T(8,128)(2,1)S(1)} %get-tuple-element.19), channel_id=1, source_target_pairs={{1,2},{2,1},{5,6},{6,5},{9,10},{10,9},{13,14},{14,13},{17,18},{18,... | collective-permute-start | bytes 491528 | tf_op jit(solution)/shard_map/ppermute | solution.py:229
  30.9 0.0 collective-permute-done.4.refs_7_
  30.9 2.9 %collective-permute-done.5.refs_8_ = bf16[2,320,128]{2,1,0:T(8,128)(2,1)S(1)} collective-permute-done((bf16[2,320,128]{2,1,0:T(8,128)(2,1)S(1)}, bf16[2,320,128]{2,1,0:T(8,128)(2,1)S(1)}, u32[]{:S(2)}, u32[]{:S(2)}) %collective-permute-start.5) | collective-permute-done | bytes 163872 | tf_op jit(solution)/shard_map/ppermute | solution.py:229
  33.9 11.1 %shard_map.49 = bf16[8,512,256]{2,1,0:T(8,128)(2,1)} custom-call(s32[7]{0:T(128)S(1)} %copy-done.2, bf16[8,512,128]{2,1,0:T(8,128)(2,1)S(1)} %copy-done, bf16[8,512,128]{2,1,0:T(8,128)(2,1)S(1)} %copy-done.1, bf16[2,1024,128]{2,1,0:T(8,128)(2,1)S(1)} %collective-permute-done.refs_3_, ...), custom_call_target="tpu_custom_call", output_to_operand_aliasing={{}: (11, {})} | custom-call | flops 6492782592 | bytes 6291456 | tf_op jit(solution)/shard_map/pallas_call | solution.py:211
  (3 shorter events, 0.0 us)
Async XLA Ops:
  0.0 15.6 %copy-start.1 = (bf16[8,512,128]{2,1,0:T(8,128)(2,1)S(1)}, bf16[8,512,128]{2,1,0:T(8,128)(2,1)}, u32[]{:S(2)}) copy-start(bf16[8,512,128]{2,1,0:T(8,128)(2,1)} %refs_2_.3) | copy-start | bytes 3145732
  0.0 15.6 %copy-start = (bf16[8,512,128]{2,1,0:T(8,128)(2,1)S(1)}, bf16[8,512,128]{2,1,0:T(8,128)(2,1)}, u32[]{:S(2)}) copy-start(bf16[8,512,128]{2,1,0:T(8,128)(2,1)} %refs_1_.3) | copy-start | bytes 3145732
  0.6 15.1 %copy-start.2 = (s32[7]{0:T(128)S(1)}, s32[7]{0:T(128)}, u32[]{:S(2)}) copy-start(s32[7]{0:T(128)} %stack.47.flags.refs_0_) | copy-start | bytes 88
  3.7 9.3 %collective-permute-start = (bf16[2,1024,128]{2,1,0:T(8,128)(2,1)}, bf16[2,1024,128]{2,1,0:T(8,128)(2,1)S(1)}, u32[]{:S(2)}, u32[]{:S(2)}) collective-permute-start(bf16[2,1024,128]{2,1,0:T(8,128)(2,1)} %get-tuple-element.13), channel_id=1, source_target_pairs={{0,1},{1,0},{2,3},{3,2},{4,5},{5,4},{6,7},{7,6},{8,9},{9,8},{10,11... | collective-permute-start | bytes 1572872 | tf_op jit(solution)/shard_map/ppermute | solution.py:229
  4.0 11.7 %collective-permute-start.1 = (bf16[2,1024,128]{2,1,0:T(8,128)(2,1)}, bf16[2,1024,128]{2,1,0:T(8,128)(2,1)S(1)}, u32[]{:S(2)}, u32[]{:S(2)}) collective-permute-start(bf16[2,1024,128]{2,1,0:T(8,128)(2,1)} %get-tuple-element.14), channel_id=1, source_target_pairs={{1,2},{2,1},{5,6},{6,5},{9,10},{10,9},{13,14},{14,13},{17,18},{18,... | collective-permute-start | bytes 1572872 | tf_op jit(solution)/shard_map/ppermute | solution.py:229
  8.4 17.9 %collective-permute-start.2 = (bf16[8,288,128]{2,1,0:T(8,128)(2,1)}, bf16[8,288,128]{2,1,0:T(8,128)(2,1)S(1)}, u32[]{:S(2)}, u32[]{:S(2)}) collective-permute-start(bf16[8,288,128]{2,1,0:T(8,128)(2,1)} %get-tuple-element.15), channel_id=1, source_target_pairs={{0,4},{4,8},{8,12},{1,5},{5,9},{9,13},{2,6},{6,10},{10,14},{3,7},{... | collective-permute-start | bytes 1769480 | tf_op jit(solution)/shard_map/ppermute | solution.py:323
  11.7 14.6 %collective-permute-start.3 = (bf16[8,32,128]{2,1,0:T(8,128)(2,1)}, bf16[8,32,128]{2,1,0:T(8,128)(2,1)S(1)}, u32[]{:S(2)}, u32[]{:S(2)}) collective-permute-start(bf16[8,32,128]{2,1,0:T(8,128)(2,1)} %get-tuple-element.16), channel_id=1, source_target_pairs={{4,0},{8,4},{12,8},{5,1},{9,5},{13,9},{6,2},{10,6},{14,10},{7,3},{... | collective-permute-start | bytes 196616 | tf_op jit(solution)/shard_map/ppermute | solution.py:326
  15.6 1.3 %copy-start.3 = (bf16[3,3,256,256]{3,2,1,0:T(8,128)(2,1)S(1)}, bf16[3,3,256,256]{3,2,1,0:T(8,128)(2,1)}, u32[]{:S(2)}) copy-start(bf16[3,3,256,256]{3,2,1,0:T(8,128)(2,1)} %param.6) | copy-start | bytes 3538948
  16.9 1.3 %copy-start.4 = (bf16[3,3,256,256]{3,2,1,0:T(8,128)(2,1)S(1)}, bf16[3,3,256,256]{3,2,1,0:T(8,128)(2,1)}, u32[]{:S(2)}) copy-start(bf16[3,3,256,256]{3,2,1,0:T(8,128)(2,1)} %param.7) | copy-start | bytes 3538948
  27.1 3.8 %collective-permute-start.4 = (bf16[2,320,128]{2,1,0:T(8,128)(2,1)S(1)}, bf16[2,320,128]{2,1,0:T(8,128)(2,1)S(1)}, u32[]{:S(2)}, u32[]{:S(2)}) collective-permute-start(bf16[2,320,128]{2,1,0:T(8,128)(2,1)S(1)} %get-tuple-element.18), channel_id=1, source_target_pairs={{0,1},{1,0},{2,3},{3,2},{4,5},{5,4},{6,7},{7,6},{8,9},{9,8},{10,11... | collective-permute-start | bytes 491528 | tf_op jit(solution)/shard_map/ppermute | solution.py:229
  27.2 6.6 %collective-permute-start.5 = (bf16[2,320,128]{2,1,0:T(8,128)(2,1)S(1)}, bf16[2,320,128]{2,1,0:T(8,128)(2,1)S(1)}, u32[]{:S(2)}, u32[]{:S(2)}) collective-permute-start(bf16[2,320,128]{2,1,0:T(8,128)(2,1)S(1)} %get-tuple-element.19), channel_id=1, source_target_pairs={{1,2},{2,1},{5,6},{6,5},{9,10},{10,9},{13,14},{14,13},{17,18},{18,... | collective-permute-start | bytes 491528 | tf_op jit(solution)/shard_map/ppermute | solution.py:229

commit v5 on v4

--- a/solution.py
+++ b/solution.py
@@ -10,7 +10,7 @@
 BF = jnp.bfloat16
 F32 = jnp.float32
 HALO = 16
-PACK = 60
+PACK = 58
 
 
 class Segment:
@@ -280,7 +280,7 @@
         scratch_shapes=[pltpu.VMEM(s, BF) for s in shapes]
         + [pltpu.SemaphoreType.DMA((4, 3)), pltpu.SemaphoreType.DMA((4,))],
         compiler_params=pltpu.CompilerParams(vmem_limit_bytes=PACK << 20),
-        cost_estimate=pl.CostEstimate(flops=0, bytes_accessed=1 << 10, transcendentals=0),
+        cost_estimate=pl.CostEstimate(flops=8 << 30, bytes_accessed=1 << 10, transcendentals=0),
     )(flags, left, right)
 
 
@@ -303,7 +303,7 @@
         out_specs=[anywhere] * 2,
         scratch_shapes=[pltpu.SemaphoreType.DMA((4,))],
         compiler_params=pltpu.CompilerParams(vmem_limit_bytes=1 << 20),
-        cost_estimate=pl.CostEstimate(flops=0, bytes_accessed=1 << 10, transcendentals=0),
+        cost_estimate=pl.CostEstimate(flops=8 << 30, bytes_accessed=1 << 10, transcendentals=0),
     )(flags, zl, zr, after)
 
 

time: 45.4 us -> 43.1 us (0.949)
  local copies, waits for them, and re-layouts: 3.12 us -> 0.59 us
    unnamed x10, local copies, waits for them, and re-layouts: 2.55 us -> 0.02 us
  transfers between devices with their start and end apart: 6 -> 6, of which waited for: 2 -> 2; matrix products, arithmetic and copies ran while one was open for 0% -> 0% of each run, Pallas kernels for 18% -> 19%
where the time goes in v5:
time: 43.1 us; the launch traced here: 42.9 us
  Pallas kernels  23.6 us (55%)
  starting transfers between devices  12.9 us (30%)
  waiting for transfers between devices  5.57 us (13%)
  local copies, waits for them, and re-layouts  0.59 us (1%)
    pallas_call x2, Pallas kernels, part_call(): pl.pallas_call(functools.partial(part_kernel, segments, ext, disp), out_s...  19.2 us
    ppermute x4, starting transfers between devices, pair_permute(): return lax.ppermute(x, axis, perm)  8.35 us
    ppermute x4, waiting for transfers between devices, pair_permute(): return lax.ppermute(x, axis, perm)  5.57 us
    pallas_call x1, Pallas kernels, pack(): pl.pallas_call(pack_kernel, out_shape=[jax.ShapeDtypeStruct(s, BF) for s...  3.54 us
    ppermute x1, starting transfers between devices, local(): zl = lax.ppermute(zl_msg, 'col', [(i, i + 1) for i in range(n_col - 1)])  3.24 us
    ppermute x1, starting transfers between devices, local(): zr = lax.ppermute(zr_msg, 'col', [(i + 1, i) for i in range(n_col - 1)])  1.29 us
  transfers between devices with their start and end apart: 6, of which 2 were waited for; matrix products, arithmetic and copies ran while one was open for 0% of the time, Pallas kernels for 19%

profile of v5, /device:TPU:1, one launch (start us, length us, event | category | flops | bytes accessed | tf_op | source)
XLA Modules:
  0.0 42.9 jit_solution(12656890638617751789)
XLA Ops:
  0.0 0.6 %stack.47.flags.refs_0_ = s32[7]{0:T(128)} concatenate(s32[1]{0:T(128)} %bitcast, s32[1]{0:T(128)} %bitcast.1, s32[1]{0:T(128)} %bitcast.2, s32[1]{0:T(128)} %bitcast.3, s32[1]{0:T(128)} %bitcast.4, s32[1]{0:T(128)} %bitcast.5, s32[1]{0:T(128)} %bitcast.6), dimensions={0} | concatenate | bytes 56 | tf_op jit(solution)/shard_map/stack | solution.py:318
  0.6 0.0 copy-start
  0.6 0.0 copy-start.4
  0.6 3.5 %shard_map.46 = (bf16[8,288,128]{2,1,0:T(8,128)(2,1)}, bf16[2,1024,128]{2,1,0:T(8,128)(2,1)}, bf16[2,1024,128]{2,1,0:T(8,128)(2,1)}, bf16[8,32,128]{2,1,0:T(8,128)(2,1)}) custom-call(s32[7]{0:T(128)} %stack.47.flags.refs_0_, bf16[8,512,128]{2,1,0:T(8,128)(2,1)} %refs_1_.3, bf16[8,512,128]{2,1,0:T(8,128)(2,1)} %refs_2_.3), custom_call_target="tpu_custom_call" | custom-call | flops 8589934592 | bytes 1024 | tf_op jit(solution)/shard_map/pallas_call | solution.py:275
  4.1 0.1 collective-permute-start
  4.3 4.5 %collective-permute-start.1 = (bf16[2,1024,128]{2,1,0:T(8,128)(2,1)}, bf16[2,1024,128]{2,1,0:T(8,128)(2,1)S(1)}, u32[]{:S(2)}, u32[]{:S(2)}) collective-permute-start(bf16[2,1024,128]{2,1,0:T(8,128)(2,1)} %get-tuple-element.14), channel_id=1, source_target_pairs={{1,2},{2,1},{5,6},{6,5},{9,10},{10,9},{13,14},{14,13},{17,18},{18,... | collective-permute-start | bytes 1572872 | tf_op jit(solution)/shard_map/ppermute | solution.py:229
  8.7 3.2 %collective-permute-start.2 = (bf16[8,288,128]{2,1,0:T(8,128)(2,1)}, bf16[8,288,128]{2,1,0:T(8,128)(2,1)S(1)}, u32[]{:S(2)}, u32[]{:S(2)}) collective-permute-start(bf16[8,288,128]{2,1,0:T(8,128)(2,1)} %get-tuple-element.15), channel_id=1, source_target_pairs={{0,4},{4,8},{8,12},{1,5},{5,9},{9,13},{2,6},{6,10},{10,14},{3,7},{... | collective-permute-start | bytes 1769480 | tf_op jit(solution)/shard_map/ppermute | solution.py:323
  12.0 1.3 %collective-permute-start.3 = (bf16[8,32,128]{2,1,0:T(8,128)(2,1)}, bf16[8,32,128]{2,1,0:T(8,128)(2,1)S(1)}, u32[]{:S(2)}, u32[]{:S(2)}) collective-permute-start(bf16[8,32,128]{2,1,0:T(8,128)(2,1)} %get-tuple-element.16), channel_id=1, source_target_pairs={{4,0},{8,4},{12,8},{5,1},{9,5},{13,9},{6,2},{10,6},{14,10},{7,3},{... | collective-permute-start | bytes 196616 | tf_op jit(solution)/shard_map/ppermute | solution.py:326
  13.3 0.0 collective-permute-done.refs_3_
  13.3 2.6 %collective-permute-done.1.refs_4_ = bf16[2,1024,128]{2,1,0:T(8,128)(2,1)S(1)} collective-permute-done((bf16[2,1024,128]{2,1,0:T(8,128)(2,1)}, bf16[2,1024,128]{2,1,0:T(8,128)(2,1)S(1)}, u32[]{:S(2)}, u32[]{:S(2)}) %collective-permute-start.1) | collective-permute-done | bytes 524320 | tf_op jit(solution)/shard_map/ppermute | solution.py:229
  15.9 0.0 copy-done
  15.9 0.0 copy-done.1
  15.9 0.0 copy-done.2
  15.9 0.0 copy-done.3
  15.9 0.0 copy-done.4
  16.0 8.1 %shard_map.47 = (bf16[8,512,256]{2,1,0:T(8,128)(2,1)}, bf16[16,128]{1,0:T(8,128)(2,1)S(1)}) custom-call(s32[7]{0:T(128)S(1)} %copy-done, bf16[8,512,128]{2,1,0:T(8,128)(2,1)S(1)} %copy-done.3, bf16[8,512,128]{2,1,0:T(8,128)(2,1)S(1)} %copy-done.4, bf16[2,1024,128]{2,1,0:T(8,128)(2,1)S(1)} %collective-permute-done.refs_3_, ...), custom_call_target="tpu_custom_call" | custom-call | flops 4945084416 | bytes 6291456 | tf_op jit(solution)/shard_map/pallas_call | solution.py:211
  24.1 0.0 collective-permute-done.3.zr.refs_6_
  24.1 0.0 collective-permute-done.2.zl.refs_5_
  24.1 0.8 %shard_map.48 = (bf16[2,320,128]{2,1,0:T(8,128)(2,1)S(1)}, bf16[2,320,128]{2,1,0:T(8,128)(2,1)S(1)}) custom-call(s32[7]{0:T(128)S(1)} %copy-done, bf16[8,288,128]{2,1,0:T(8,128)(2,1)S(1)} %collective-permute-done.2.zl.refs_5_, bf16[8,32,128]{2,1,0:T(8,128)(2,1)S(1)} %collective-permute-done.3.zr.refs_6_, bf16[16,128]{1,0:T(8,128)(2,1)S(1)} %get-tuple-element.17._), custom_call_target="tpu_custom_call" | custom-call | flops 8589934592 | bytes 1024 | tf_op jit(solution)/shard_map/pallas_call | solution.py:299
  24.9 0.1 collective-permute-start.4
  25.0 3.7 %collective-permute-start.5 = (bf16[2,320,128]{2,1,0:T(8,128)(2,1)S(1)}, bf16[2,320,128]{2,1,0:T(8,128)(2,1)S(1)}, u32[]{:S(2)}, u32[]{:S(2)}) collective-permute-start(bf16[2,320,128]{2,1,0:T(8,128)(2,1)S(1)} %get-tuple-element.19), channel_id=1, source_target_pairs={{1,2},{2,1},{5,6},{6,5},{9,10},{10,9},{13,14},{14,13},{17,18},{18,... | collective-permute-start | bytes 491528 | tf_op jit(solution)/shard_map/ppermute | solution.py:229
  28.7 0.0 collective-permute-done.4.refs_7_
  28.7 2.9 %collective-permute-done.5.refs_8_ = bf16[2,320,128]{2,1,0:T(8,128)(2,1)S(1)} collective-permute-done((bf16[2,320,128]{2,1,0:T(8,128)(2,1)S(1)}, bf16[2,320,128]{2,1,0:T(8,128)(2,1)S(1)}, u32[]{:S(2)}, u32[]{:S(2)}) %collective-permute-start.5) | collective-permute-done | bytes 163872 | tf_op jit(solution)/shard_map/ppermute | solution.py:229
  31.6 11.1 %shard_map.49 = bf16[8,512,256]{2,1,0:T(8,128)(2,1)} custom-call(s32[7]{0:T(128)S(1)} %copy-done, bf16[8,512,128]{2,1,0:T(8,128)(2,1)S(1)} %copy-done.3, bf16[8,512,128]{2,1,0:T(8,128)(2,1)S(1)} %copy-done.4, bf16[2,1024,128]{2,1,0:T(8,128)(2,1)S(1)} %collective-permute-done.refs_3_, ...), custom_call_target="tpu_custom_call", output_to_operand_aliasing={{}: (11, {})} | custom-call | flops 6492782592 | bytes 6291456 | tf_op jit(solution)/shard_map/pallas_call | solution.py:211
  (3 shorter events, 0.0 us)
Async XLA Ops:
  0.6 15.4 %copy-start = (s32[7]{0:T(128)S(1)}, s32[7]{0:T(128)}, u32[]{:S(2)}) copy-start(s32[7]{0:T(128)} %stack.47.flags.refs_0_) | copy-start | bytes 88
  0.6 15.4 %copy-start.1 = (bf16[3,3,256,256]{3,2,1,0:T(8,128)(2,1)S(1)}, bf16[3,3,256,256]{3,2,1,0:T(8,128)(2,1)}, u32[]{:S(2)}) copy-start(bf16[3,3,256,256]{3,2,1,0:T(8,128)(2,1)} %param.6) | copy-start | bytes 3538948
  0.6 15.4 %copy-start.2 = (bf16[3,3,256,256]{3,2,1,0:T(8,128)(2,1)S(1)}, bf16[3,3,256,256]{3,2,1,0:T(8,128)(2,1)}, u32[]{:S(2)}) copy-start(bf16[3,3,256,256]{3,2,1,0:T(8,128)(2,1)} %param.7) | copy-start | bytes 3538948
  0.6 15.4 %copy-start.3 = (bf16[8,512,128]{2,1,0:T(8,128)(2,1)S(1)}, bf16[8,512,128]{2,1,0:T(8,128)(2,1)}, u32[]{:S(2)}) copy-start(bf16[8,512,128]{2,1,0:T(8,128)(2,1)} %refs_1_.3) | copy-start | bytes 3145732
  0.6 15.4 %copy-start.4 = (bf16[8,512,128]{2,1,0:T(8,128)(2,1)S(1)}, bf16[8,512,128]{2,1,0:T(8,128)(2,1)}, u32[]{:S(2)}) copy-start(bf16[8,512,128]{2,1,0:T(8,128)(2,1)} %refs_2_.3) | copy-start | bytes 3145732
  4.1 9.1 %collective-permute-start = (bf16[2,1024,128]{2,1,0:T(8,128)(2,1)}, bf16[2,1024,128]{2,1,0:T(8,128)(2,1)S(1)}, u32[]{:S(2)}, u32[]{:S(2)}) collective-permute-start(bf16[2,1024,128]{2,1,0:T(8,128)(2,1)} %get-tuple-element.13), channel_id=1, source_target_pairs={{0,1},{1,0},{2,3},{3,2},{4,5},{5,4},{6,7},{7,6},{8,9},{9,8},{10,11... | collective-permute-start | bytes 1572872 | tf_op jit(solution)/shard_map/ppermute | solution.py:229
  4.3 11.7 %collective-permute-start.1 = (bf16[2,1024,128]{2,1,0:T(8,128)(2,1)}, bf16[2,1024,128]{2,1,0:T(8,128)(2,1)S(1)}, u32[]{:S(2)}, u32[]{:S(2)}) collective-permute-start(bf16[2,1024,128]{2,1,0:T(8,128)(2,1)} %get-tuple-element.14), channel_id=1, source_target_pairs={{1,2},{2,1},{5,6},{6,5},{9,10},{10,9},{13,14},{14,13},{17,18},{18,... | collective-permute-start | bytes 1572872 | tf_op jit(solution)/shard_map/ppermute | solution.py:229
  8.7 15.4 %collective-permute-start.2 = (bf16[8,288,128]{2,1,0:T(8,128)(2,1)}, bf16[8,288,128]{2,1,0:T(8,128)(2,1)S(1)}, u32[]{:S(2)}, u32[]{:S(2)}) collective-permute-start(bf16[8,288,128]{2,1,0:T(8,128)(2,1)} %get-tuple-element.15), channel_id=1, source_target_pairs={{0,4},{4,8},{8,12},{1,5},{5,9},{9,13},{2,6},{6,10},{10,14},{3,7},{... | collective-permute-start | bytes 1769480 | tf_op jit(solution)/shard_map/ppermute | solution.py:323
  12.0 12.1 %collective-permute-start.3 = (bf16[8,32,128]{2,1,0:T(8,128)(2,1)}, bf16[8,32,128]{2,1,0:T(8,128)(2,1)S(1)}, u32[]{:S(2)}, u32[]{:S(2)}) collective-permute-start(bf16[8,32,128]{2,1,0:T(8,128)(2,1)} %get-tuple-element.16), channel_id=1, source_target_pairs={{4,0},{8,4},{12,8},{5,1},{9,5},{13,9},{6,2},{10,6},{14,10},{7,3},{... | collective-permute-start | bytes 196616 | tf_op jit(solution)/shard_map/ppermute | solution.py:326
  24.9 3.8 %collective-permute-start.4 = (bf16[2,320,128]{2,1,0:T(8,128)(2,1)S(1)}, bf16[2,320,128]{2,1,0:T(8,128)(2,1)S(1)}, u32[]{:S(2)}, u32[]{:S(2)}) collective-permute-start(bf16[2,320,128]{2,1,0:T(8,128)(2,1)S(1)} %get-tuple-element.18), channel_id=1, source_target_pairs={{0,1},{1,0},{2,3},{3,2},{4,5},{5,4},{6,7},{7,6},{8,9},{9,8},{10,11... | collective-permute-start | bytes 491528 | tf_op jit(solution)/shard_map/ppermute | solution.py:229
  25.0 6.6 %collective-permute-start.5 = (bf16[2,320,128]{2,1,0:T(8,128)(2,1)S(1)}, bf16[2,320,128]{2,1,0:T(8,128)(2,1)S(1)}, u32[]{:S(2)}, u32[]{:S(2)}) collective-permute-start(bf16[2,320,128]{2,1,0:T(8,128)(2,1)S(1)} %get-tuple-element.19), channel_id=1, source_target_pairs={{1,2},{2,1},{5,6},{6,5},{9,10},{10,9},{13,14},{14,13},{17,18},{18,... | collective-permute-start | bytes 491528 | tf_op jit(solution)/shard_map/ppermute | solution.py:229

commit v6 on v5

--- a/solution.py
+++ b/solution.py
@@ -25,7 +25,7 @@
     flags, l_own, r_own, a_ref, b_ref = refs[:5]
     zl, zr, ca, cb = refs[5:9] if ext else (None,) * 4
     k1, k2 = refs[9:11] if ext else refs[5:7]
-    out_any, (rrev, vf, vs, hf, hs, obuf, osems) = refs[-9 if not ext else -8], refs[-7:]
+    out_any, (rrev, vf, vs, hf, hs, obuf, osems) = refs[-8], refs[-7:]
     rows, cols, chans = l_own.shape
     pad = HALO if ext else 0
     lpad = disp + HALO if ext else 0
@@ -210,10 +210,10 @@
     flops = 2 * 9 * disp * disp * ((rows + 2) * m_hid + rows * m_out)
     return pl.pallas_call(
         functools.partial(part_kernel, segments, ext, disp),
-        out_shape=out_shape if ext else [out_shape, jax.ShapeDtypeStruct((16, 128), BF)],
+        out_shape=out_shape,
         in_specs=([smem] + [vmem] * (8 if ext else 4)
                   + [vmem, vmem] + ([anywhere] if ext else [])),
-        out_specs=anywhere if ext else [anywhere, anywhere],
+        out_specs=anywhere,
         scratch_shapes=scratch,
         input_output_aliases={len(operands) - 1: 0} if ext else {},
         compiler_params=pltpu.CompilerParams(vmem_limit_bytes=44 << 20),
@@ -284,7 +284,7 @@
     )(flags, left, right)
 
 
-def pack_corners_kernel(flags, zl, zr, _, ca, cb, sems):
+def pack_corners_kernel(flags, zl, zr, ca, cb, sems):
     wide = zl.shape[1]
     copies = []
     for msg, at in ((cb, flags[6]), (ca, flags[5])):
@@ -293,18 +293,18 @@
     copy_all(copies, sems)
 
 
-def pack_corners(flags, zl, zr, after):
+def pack_corners(flags, zl, zr):
     anywhere = pl.BlockSpec(memory_space=pl.ANY)
     shape = jax.ShapeDtypeStruct((2, zl.shape[1] + zr.shape[1], zl.shape[2]), BF)
     return pl.pallas_call(
         pack_corners_kernel,
         out_shape=[shape, shape],
-        in_specs=[pl.BlockSpec(memory_space=pltpu.SMEM)] + [anywhere] * 3,
+        in_specs=[pl.BlockSpec(memory_space=pltpu.SMEM)] + [anywhere] * 2,
         out_specs=[anywhere] * 2,
         scratch_shapes=[pltpu.SemaphoreType.DMA((4,))],
         compiler_params=pltpu.CompilerParams(vmem_limit_bytes=1 << 20),
         cost_estimate=pl.CostEstimate(flops=8 << 30, bytes_accessed=1 << 10, transcendentals=0),
-    )(flags, zl, zr, after)
+    )(flags, zl, zr)
 
 
 def local(left, right, conv_first, conv_second):
@@ -327,9 +327,9 @@
 
     out_shape = jax.ShapeDtypeStruct((rows, cols, disp), BF)
     mid = [Segment(disp, cols - disp - 2 * HALO)]
-    out, after = part_call(mid, False, disp, rows, cols, chans, out_shape, (flags, left, right, a, b, k1, k2))
-
-    ca_msg, cb_msg = pack_corners(flags, zl, zr, after)
+    out = part_call(mid, False, disp, rows, cols, chans, out_shape, (flags, left, right, a, b, k1, k2))
+
+    ca_msg, cb_msg = pack_corners(flags, zl, zr)
     cb = pair_permute(cb_msg, "row", 1)
     ca = pair_permute(ca_msg, "row", 0)
     rest = [Segment(-HALO, disp + HALO), Segment(cols - 2 * HALO, HALO)]

time: 43.1 us -> 45.1 us (1.046)
  starting transfers between devices: 12.9 us -> 14.3 us
  waiting for transfers between devices: 5.57 us -> 6.6 us
    ppermute x1, waiting for transfers between devices: 0.01 us -> 6.59 us  [local(): zl = lax.ppermute(zl_msg, 'col', [(i, i + 1) for i in range(n_col - 1)])]
    ppermute x4, waiting for transfers between devices: 5.57 us -> 0.01 us  [pair_permute(): return lax.ppermute(x, axis, perm)]
    ppermute x1, starting transfers between devices: 3.24 us -> 4.07 us  [local(): zl = lax.ppermute(zl_msg, 'col', [(i, i + 1) for i in range(n_col - 1)])]
    ppermute x4, starting transfers between devices: 8.35 us -> 8.97 us  [pair_permute(): return lax.ppermute(x, axis, perm)]
  transfers between devices with their start and end apart: 6 -> 6, of which waited for: 2 -> 1; matrix products, arithmetic and copies ran while one was open for 0% -> 0% of each run, Pallas kernels for 19% -> 20%
where the time goes in v6:
time: 45.1 us; the launch traced here: 44.9 us
  Pallas kernels  23.2 us (51%)
  starting transfers between devices  14.3 us (32%)
  waiting for transfers between devices  6.6 us (15%)
  local copies, waits for them, and re-layouts  0.63 us (1%)
    pallas_call x2, Pallas kernels, part_call(): pl.pallas_call(functools.partial(part_kernel, segments, ext, disp), out_s...  19.2 us
    ppermute x4, starting transfers between devices, pair_permute(): return lax.ppermute(x, axis, perm)  8.97 us
    ppermute x1, waiting for transfers between devices, local(): zl = lax.ppermute(zl_msg, 'col', [(i, i + 1) for i in range(n_col - 1)])  6.59 us
    ppermute x1, starting transfers between devices, local(): zl = lax.ppermute(zl_msg, 'col', [(i, i + 1) for i in range(n_col - 1)])  4.07 us
    pallas_call x1, Pallas kernels, pack(): pl.pallas_call(pack_kernel, out_shape=[jax.ShapeDtypeStruct(s, BF) for s...  3.15 us
    ppermute x1, starting transfers between devices, local(): zr = lax.ppermute(zr_msg, 'col', [(i + 1, i) for i in range(n_col - 1)])  1.29 us
  transfers between devices with their start and end apart: 6, of which 1 were waited for; matrix products, arithmetic and copies ran while one was open for 0% of the time, Pallas kernels for 20%

profile of v6, /device:TPU:1, one launch (start us, length us, event | category | flops | bytes accessed | tf_op | source)
XLA Modules:
  0.0 44.9 jit_solution(7072113594376356750)
XLA Ops:
  0.0 0.6 %stack.47.flags.refs_0_ = s32[7]{0:T(128)} concatenate(s32[1]{0:T(128)} %bitcast, s32[1]{0:T(128)} %bitcast.1, s32[1]{0:T(128)} %bitcast.2, s32[1]{0:T(128)} %bitcast.3, s32[1]{0:T(128)} %bitcast.4, s32[1]{0:T(128)} %bitcast.5, s32[1]{0:T(128)} %bitcast.6), dimensions={0} | concatenate | bytes 56 | tf_op jit(solution)/shard_map/stack | solution.py:318
  0.6 0.0 copy-start
  0.6 3.1 %shard_map.46 = (bf16[8,288,128]{2,1,0:T(8,128)(2,1)}, bf16[2,1024,128]{2,1,0:T(8,128)(2,1)}, bf16[2,1024,128]{2,1,0:T(8,128)(2,1)}, bf16[8,32,128]{2,1,0:T(8,128)(2,1)}) custom-call(s32[7]{0:T(128)} %stack.47.flags.refs_0_, bf16[8,512,128]{2,1,0:T(8,128)(2,1)} %refs_1_.3, bf16[8,512,128]{2,1,0:T(8,128)(2,1)} %refs_2_.3), custom_call_target="tpu_custom_call" | custom-call | flops 8589934592 | bytes 1024 | tf_op jit(solution)/shard_map/pallas_call | solution.py:275
  3.8 4.1 %collective-permute-start.2 = (bf16[8,288,128]{2,1,0:T(8,128)(2,1)}, bf16[8,288,128]{2,1,0:T(8,128)(2,1)S(1)}, u32[]{:S(2)}, u32[]{:S(2)}) collective-permute-start(bf16[8,288,128]{2,1,0:T(8,128)(2,1)} %get-tuple-element.13), channel_id=1, source_target_pairs={{0,4},{4,8},{8,12},{1,5},{5,9},{9,13},{2,6},{6,10},{10,14},{3,7},{... | collective-permute-start | bytes 1769480 | tf_op jit(solution)/shard_map/ppermute | solution.py:323
  7.8 1.3 %collective-permute-start.3 = (bf16[8,32,128]{2,1,0:T(8,128)(2,1)}, bf16[8,32,128]{2,1,0:T(8,128)(2,1)S(1)}, u32[]{:S(2)}, u32[]{:S(2)}) collective-permute-start(bf16[8,32,128]{2,1,0:T(8,128)(2,1)} %get-tuple-element.14), channel_id=1, source_target_pairs={{4,0},{8,4},{12,8},{5,1},{9,5},{13,9},{6,2},{10,6},{14,10},{7,3},{... | collective-permute-start | bytes 196616 | tf_op jit(solution)/shard_map/ppermute | solution.py:326
  9.1 1.0 %collective-permute-start = (bf16[2,1024,128]{2,1,0:T(8,128)(2,1)}, bf16[2,1024,128]{2,1,0:T(8,128)(2,1)S(1)}, u32[]{:S(2)}, u32[]{:S(2)}) collective-permute-start(bf16[2,1024,128]{2,1,0:T(8,128)(2,1)} %get-tuple-element.11), channel_id=1, source_target_pairs={{0,1},{1,0},{2,3},{3,2},{4,5},{5,4},{6,7},{7,6},{8,9},{9,8},{10,11... | collective-permute-start | bytes 1572872 | tf_op jit(solution)/shard_map/ppermute | solution.py:229
  10.2 0.0 copy-start.1
  10.2 3.3 %collective-permute-start.1 = (bf16[2,1024,128]{2,1,0:T(8,128)(2,1)}, bf16[2,1024,128]{2,1,0:T(8,128)(2,1)S(1)}, u32[]{:S(2)}, u32[]{:S(2)}) collective-permute-start(bf16[2,1024,128]{2,1,0:T(8,128)(2,1)} %get-tuple-element.12), channel_id=1, source_target_pairs={{1,2},{2,1},{5,6},{6,5},{9,10},{10,9},{13,14},{14,13},{17,18},{18,... | collective-permute-start | bytes 1572872 | tf_op jit(solution)/shard_map/ppermute | solution.py:229
  13.5 0.0 collective-permute-done.3.zr.refs_6_
  13.5 6.6 %collective-permute-done.2.zl.refs_5_ = bf16[8,288,128]{2,1,0:T(8,128)(2,1)S(1)} collective-permute-done((bf16[8,288,128]{2,1,0:T(8,128)(2,1)}, bf16[8,288,128]{2,1,0:T(8,128)(2,1)S(1)}, u32[]{:S(2)}, u32[]{:S(2)}) %collective-permute-start.2) | collective-permute-done | bytes 589856 | tf_op jit(solution)/shard_map/ppermute | solution.py:323
  20.1 0.0 copy-done
  20.1 0.8 %shard_map.47 = (bf16[2,320,128]{2,1,0:T(8,128)(2,1)S(1)}, bf16[2,320,128]{2,1,0:T(8,128)(2,1)S(1)}) custom-call(s32[7]{0:T(128)S(1)} %copy-done, bf16[8,288,128]{2,1,0:T(8,128)(2,1)S(1)} %collective-permute-done.2.zl.refs_5_, bf16[8,32,128]{2,1,0:T(8,128)(2,1)S(1)} %collective-permute-done.3.zr.refs_6_), custom_call_target="tpu_custom_call" | custom-call | flops 8589934592 | bytes 1024 | tf_op jit(solution)/shard_map/pallas_call | solution.py:299
  20.9 1.6 %collective-permute-start.4 = (bf16[2,320,128]{2,1,0:T(8,128)(2,1)S(1)}, bf16[2,320,128]{2,1,0:T(8,128)(2,1)S(1)}, u32[]{:S(2)}, u32[]{:S(2)}) collective-permute-start(bf16[2,320,128]{2,1,0:T(8,128)(2,1)S(1)} %get-tuple-element.15), channel_id=1, source_target_pairs={{0,1},{1,0},{2,3},{3,2},{4,5},{5,4},{6,7},{7,6},{8,9},{9,8},{10,11... | collective-permute-start | bytes 491528 | tf_op jit(solution)/shard_map/ppermute | solution.py:229
  22.5 3.0 %collective-permute-start.5 = (bf16[2,320,128]{2,1,0:T(8,128)(2,1)S(1)}, bf16[2,320,128]{2,1,0:T(8,128)(2,1)S(1)}, u32[]{:S(2)}, u32[]{:S(2)}) collective-permute-start(bf16[2,320,128]{2,1,0:T(8,128)(2,1)S(1)} %get-tuple-element.16), channel_id=1, source_target_pairs={{1,2},{2,1},{5,6},{6,5},{9,10},{10,9},{13,14},{14,13},{17,18},{18,... | collective-permute-start | bytes 491528 | tf_op jit(solution)/shard_map/ppermute | solution.py:229
  25.6 0.0 collective-permute-done.refs_3_
  25.6 0.0 collective-permute-done.1.refs_4_
  25.6 0.0 copy-done.1
  25.6 0.0 copy-done.2
  25.6 0.0 copy-done.3
  25.6 0.0 copy-done.4
  25.6 8.1 %shard_map.48.refs_11_ = bf16[8,512,256]{2,1,0:T(8,128)(2,1)} custom-call(s32[7]{0:T(128)S(1)} %copy-done, bf16[8,512,128]{2,1,0:T(8,128)(2,1)S(1)} %copy-done.3, bf16[8,512,128]{2,1,0:T(8,128)(2,1)S(1)} %copy-done.4, bf16[2,1024,128]{2,1,0:T(8,128)(2,1)S(1)} %collective-permute-done.refs_3_, bf16[2,1024,128]{2,1,0:T(8,128)(2,1)S(1)} %collective-permute-done.1.refs_4_, ...), custom_call_target="tpu_custom_call" | custom-call | flops 4945084416 | bytes 6291456 | tf_op jit(solution)/shard_map/pallas_call | solution.py:211
  33.7 0.0 collective-permute-done.4.refs_7_
  33.7 0.0 collective-permute-done.5.refs_8_
  33.7 11.1 %shard_map.49 = bf16[8,512,256]{2,1,0:T(8,128)(2,1)} custom-call(s32[7]{0:T(128)S(1)} %copy-done, bf16[8,512,128]{2,1,0:T(8,128)(2,1)S(1)} %copy-done.3, bf16[8,512,128]{2,1,0:T(8,128)(2,1)S(1)} %copy-done.4, bf16[2,1024,128]{2,1,0:T(8,128)(2,1)S(1)} %collective-permute-done.refs_3_, ...), custom_call_target="tpu_custom_call", output_to_operand_aliasing={{}: (11, {})} | custom-call | flops 6492782592 | bytes 6291456 | tf_op jit(solution)/shard_map/pallas_call | solution.py:211
  (3 shorter events, 0.0 us)
Async XLA Ops:
  0.6 19.5 %copy-start = (s32[7]{0:T(128)S(1)}, s32[7]{0:T(128)}, u32[]{:S(2)}) copy-start(s32[7]{0:T(128)} %stack.47.flags.refs_0_) | copy-start | bytes 88
  3.8 16.3 %collective-permute-start.2 = (bf16[8,288,128]{2,1,0:T(8,128)(2,1)}, bf16[8,288,128]{2,1,0:T(8,128)(2,1)S(1)}, u32[]{:S(2)}, u32[]{:S(2)}) collective-permute-start(bf16[8,288,128]{2,1,0:T(8,128)(2,1)} %get-tuple-element.13), channel_id=1, source_target_pairs={{0,4},{4,8},{8,12},{1,5},{5,9},{9,13},{2,6},{6,10},{10,14},{3,7},{... | collective-permute-start | bytes 1769480 | tf_op jit(solution)/shard_map/ppermute | solution.py:323
  7.8 5.7 %collective-permute-start.3 = (bf16[8,32,128]{2,1,0:T(8,128)(2,1)}, bf16[8,32,128]{2,1,0:T(8,128)(2,1)S(1)}, u32[]{:S(2)}, u32[]{:S(2)}) collective-permute-start(bf16[8,32,128]{2,1,0:T(8,128)(2,1)} %get-tuple-element.14), channel_id=1, source_target_pairs={{4,0},{8,4},{12,8},{5,1},{9,5},{13,9},{6,2},{10,6},{14,10},{7,3},{... | collective-permute-start | bytes 196616 | tf_op jit(solution)/shard_map/ppermute | solution.py:326
  9.1 16.4 %collective-permute-start = (bf16[2,1024,128]{2,1,0:T(8,128)(2,1)}, bf16[2,1024,128]{2,1,0:T(8,128)(2,1)S(1)}, u32[]{:S(2)}, u32[]{:S(2)}) collective-permute-start(bf16[2,1024,128]{2,1,0:T(8,128)(2,1)} %get-tuple-element.11), channel_id=1, source_target_pairs={{0,1},{1,0},{2,3},{3,2},{4,5},{5,4},{6,7},{7,6},{8,9},{9,8},{10,11... | collective-permute-start | bytes 1572872 | tf_op jit(solution)/shard_map/ppermute | solution.py:229
  10.2 15.4 %copy-start.1 = (bf16[3,3,256,256]{3,2,1,0:T(8,128)(2,1)S(1)}, bf16[3,3,256,256]{3,2,1,0:T(8,128)(2,1)}, u32[]{:S(2)}) copy-start(bf16[3,3,256,256]{3,2,1,0:T(8,128)(2,1)} %param.6) | copy-start | bytes 3538948
  10.2 15.4 %copy-start.2 = (bf16[3,3,256,256]{3,2,1,0:T(8,128)(2,1)S(1)}, bf16[3,3,256,256]{3,2,1,0:T(8,128)(2,1)}, u32[]{:S(2)}) copy-start(bf16[3,3,256,256]{3,2,1,0:T(8,128)(2,1)} %param.7) | copy-start | bytes 3538948
  10.2 15.4 %copy-start.3 = (bf16[8,512,128]{2,1,0:T(8,128)(2,1)S(1)}, bf16[8,512,128]{2,1,0:T(8,128)(2,1)}, u32[]{:S(2)}) copy-start(bf16[8,512,128]{2,1,0:T(8,128)(2,1)} %refs_1_.3) | copy-start | bytes 3145732
  10.2 15.4 %copy-start.4 = (bf16[8,512,128]{2,1,0:T(8,128)(2,1)S(1)}, bf16[8,512,128]{2,1,0:T(8,128)(2,1)}, u32[]{:S(2)}) copy-start(bf16[8,512,128]{2,1,0:T(8,128)(2,1)} %refs_2_.3) | copy-start | bytes 3145732
  10.2 15.4 %collective-permute-start.1 = (bf16[2,1024,128]{2,1,0:T(8,128)(2,1)}, bf16[2,1024,128]{2,1,0:T(8,128)(2,1)S(1)}, u32[]{:S(2)}, u32[]{:S(2)}) collective-permute-start(bf16[2,1024,128]{2,1,0:T(8,128)(2,1)} %get-tuple-element.12), channel_id=1, source_target_pairs={{1,2},{2,1},{5,6},{6,5},{9,10},{10,9},{13,14},{14,13},{17,18},{18,... | collective-permute-start | bytes 1572872 | tf_op jit(solution)/shard_map/ppermute | solution.py:229
  20.9 12.8 %collective-permute-start.4 = (bf16[2,320,128]{2,1,0:T(8,128)(2,1)S(1)}, bf16[2,320,128]{2,1,0:T(8,128)(2,1)S(1)}, u32[]{:S(2)}, u32[]{:S(2)}) collective-permute-start(bf16[2,320,128]{2,1,0:T(8,128)(2,1)S(1)} %get-tuple-element.15), channel_id=1, source_target_pairs={{0,1},{1,0},{2,3},{3,2},{4,5},{5,4},{6,7},{7,6},{8,9},{9,8},{10,11... | collective-permute-start | bytes 491528 | tf_op jit(solution)/shard_map/ppermute | solution.py:229
  22.5 11.2 %collective-permute-start.5 = (bf16[2,320,128]{2,1,0:T(8,128)(2,1)S(1)}, bf16[2,320,128]{2,1,0:T(8,128)(2,1)S(1)}, u32[]{:S(2)}, u32[]{:S(2)}) collective-permute-start(bf16[2,320,128]{2,1,0:T(8,128)(2,1)S(1)} %get-tuple-element.16), channel_id=1, source_target_pairs={{1,2},{2,1},{5,6},{6,5},{9,10},{10,9},{13,14},{14,13},{17,18},{18,... | collective-permute-start | bytes 491528 | tf_op jit(solution)/shard_map/ppermute | solution.py:229

commit v7 on v5

--- a/solution.py
+++ b/solution.py
@@ -22,7 +22,7 @@
 
 def part_kernel(segments, ext, disp, *refs):
     refs = list(refs)
-    flags, l_own, r_own, a_ref, b_ref = refs[:5]
+    flags, l_own, r_own, b_ref, a_ref = refs[:5]
     zl, zr, ca, cb = refs[5:9] if ext else (None,) * 4
     k1, k2 = refs[9:11] if ext else refs[5:7]
     out_any, (rrev, vf, vs, hf, hs, obuf, osems) = refs[-9 if not ext else -8], refs[-7:]
@@ -327,14 +327,14 @@
 
     out_shape = jax.ShapeDtypeStruct((rows, cols, disp), BF)
     mid = [Segment(disp, cols - disp - 2 * HALO)]
-    out, after = part_call(mid, False, disp, rows, cols, chans, out_shape, (flags, left, right, a, b, k1, k2))
+    out, after = part_call(mid, False, disp, rows, cols, chans, out_shape, (flags, left, right, b, a, k1, k2))
 
     ca_msg, cb_msg = pack_corners(flags, zl, zr, after)
     cb = pair_permute(cb_msg, "row", 1)
     ca = pair_permute(ca_msg, "row", 0)
     rest = [Segment(-HALO, disp + HALO), Segment(cols - 2 * HALO, HALO)]
     return part_call(rest, True, disp, rows, cols, chans, out_shape,
-                     (flags, left, right, a, b, zl, zr, ca, cb, k1, k2, out))
+                     (flags, left, right, b, a, zl, zr, ca, cb, k1, k2, out))
 
 
 def solution(mesh):

time: 43.1 us -> 44.8 us (1.039)
  waiting for transfers between devices: 5.57 us -> 7.5 us
    ppermute x4, waiting for transfers between devices: 5.57 us -> 6.96 us  [pair_permute(): return lax.ppermute(x, axis, perm)]
    ppermute x1, waiting for transfers between devices: 0.01 us -> 0.53 us  [local(): zl = lax.ppermute(zl_msg, 'col', [(i, i + 1) for i in range(n_col - 1)])]
  transfers between devices with their start and end apart: 6 -> 6, of which waited for: 2 -> 3; matrix products, arithmetic and copies ran while one was open for 0% -> 0% of each run, Pallas kernels for 19% -> 18%
where the time goes in v7:
time: 44.8 us; the launch traced here: 44.6 us
  Pallas kernels  23.6 us (53%)
  starting transfers between devices  12.6 us (28%)
  waiting for transfers between devices  7.5 us (17%)
  local copies, waits for them, and re-layouts  0.59 us (1%)
    pallas_call x2, Pallas kernels, part_call(): pl.pallas_call(functools.partial(part_kernel, segments, ext, disp), out_s...  19.2 us
    ppermute x4, starting transfers between devices, pair_permute(): return lax.ppermute(x, axis, perm)  8.07 us
    ppermute x4, waiting for transfers between devices, pair_permute(): return lax.ppermute(x, axis, perm)  6.96 us
    pallas_call x1, Pallas kernels, pack(): pl.pallas_call(pack_kernel, out_shape=[jax.ShapeDtypeStruct(s, BF) for s...  3.54 us
    ppermute x1, starting transfers between devices, local(): zl = lax.ppermute(zl_msg, 'col', [(i, i + 1) for i in range(n_col - 1)])  3.24 us
    ppermute x1, starting transfers between devices, local(): zr = lax.ppermute(zr_msg, 'col', [(i + 1, i) for i in range(n_col - 1)])  1.29 us
  transfers between devices with their start and end apart: 6, of which 3 were waited for; matrix products, arithmetic and copies ran while one was open for 0% of the time, Pallas kernels for 18%

profile of v7, /device:TPU:1, one launch (start us, length us, event | category | flops | bytes accessed | tf_op | source)
XLA Modules:
  0.0 44.6 jit_solution(11814880951467194498)
XLA Ops:
  0.0 0.6 %stack.47.flags.refs_0_ = s32[7]{0:T(128)} concatenate(s32[1]{0:T(128)} %bitcast, s32[1]{0:T(128)} %bitcast.1, s32[1]{0:T(128)} %bitcast.2, s32[1]{0:T(128)} %bitcast.3, s32[1]{0:T(128)} %bitcast.4, s32[1]{0:T(128)} %bitcast.5, s32[1]{0:T(128)} %bitcast.6), dimensions={0} | concatenate | bytes 56 | tf_op jit(solution)/shard_map/stack | solution.py:318
  0.6 0.0 copy-start
  0.6 0.0 copy-start.4
  0.6 3.5 %shard_map.46 = (bf16[8,288,128]{2,1,0:T(8,128)(2,1)}, bf16[2,1024,128]{2,1,0:T(8,128)(2,1)}, bf16[2,1024,128]{2,1,0:T(8,128)(2,1)}, bf16[8,32,128]{2,1,0:T(8,128)(2,1)}) custom-call(s32[7]{0:T(128)} %stack.47.flags.refs_0_, bf16[8,512,128]{2,1,0:T(8,128)(2,1)} %refs_1_.3, bf16[8,512,128]{2,1,0:T(8,128)(2,1)} %refs_2_.3), custom_call_target="tpu_custom_call" | custom-call | flops 8589934592 | bytes 1024 | tf_op jit(solution)/shard_map/pallas_call | solution.py:275
  4.1 4.5 %collective-permute-start = (bf16[2,1024,128]{2,1,0:T(8,128)(2,1)}, bf16[2,1024,128]{2,1,0:T(8,128)(2,1)S(1)}, u32[]{:S(2)}, u32[]{:S(2)}) collective-permute-start(bf16[2,1024,128]{2,1,0:T(8,128)(2,1)} %get-tuple-element.13), channel_id=1, source_target_pairs={{1,2},{2,1},{5,6},{6,5},{9,10},{10,9},{13,14},{14,13},{17,18},{18,... | collective-permute-start | bytes 1572872 | tf_op jit(solution)/shard_map/ppermute | solution.py:229
  8.7 0.1 collective-permute-start.1
  8.7 3.2 %collective-permute-start.2 = (bf16[8,288,128]{2,1,0:T(8,128)(2,1)}, bf16[8,288,128]{2,1,0:T(8,128)(2,1)S(1)}, u32[]{:S(2)}, u32[]{:S(2)}) collective-permute-start(bf16[8,288,128]{2,1,0:T(8,128)(2,1)} %get-tuple-element.15), channel_id=1, source_target_pairs={{0,4},{4,8},{8,12},{1,5},{5,9},{9,13},{2,6},{6,10},{10,14},{3,7},{... | collective-permute-start | bytes 1769480 | tf_op jit(solution)/shard_map/ppermute | solution.py:323
  12.0 1.3 %collective-permute-start.3 = (bf16[8,32,128]{2,1,0:T(8,128)(2,1)}, bf16[8,32,128]{2,1,0:T(8,128)(2,1)S(1)}, u32[]{:S(2)}, u32[]{:S(2)}) collective-permute-start(bf16[8,32,128]{2,1,0:T(8,128)(2,1)} %get-tuple-element.16), channel_id=1, source_target_pairs={{4,0},{8,4},{12,8},{5,1},{9,5},{13,9},{6,2},{10,6},{14,10},{7,3},{... | collective-permute-start | bytes 196616 | tf_op jit(solution)/shard_map/ppermute | solution.py:326
  13.3 2.4 %collective-permute-done.refs_3_ = bf16[2,1024,128]{2,1,0:T(8,128)(2,1)S(1)} collective-permute-done((bf16[2,1024,128]{2,1,0:T(8,128)(2,1)}, bf16[2,1024,128]{2,1,0:T(8,128)(2,1)S(1)}, u32[]{:S(2)}, u32[]{:S(2)}) %collective-permute-start) | collective-permute-done | bytes 524320 | tf_op jit(solution)/shard_map/ppermute | solution.py:229
  15.7 0.0 collective-permute-done.1.refs_4_
  15.7 0.0 copy-done
  15.7 0.0 copy-done.1
  15.7 0.0 copy-done.2
  15.7 0.0 copy-done.3
  15.7 0.0 copy-done.4
  15.8 8.1 %shard_map.47 = (bf16[8,512,256]{2,1,0:T(8,128)(2,1)}, bf16[16,128]{1,0:T(8,128)(2,1)S(1)}) custom-call(s32[7]{0:T(128)S(1)} %copy-done, bf16[8,512,128]{2,1,0:T(8,128)(2,1)S(1)} %copy-done.3, bf16[8,512,128]{2,1,0:T(8,128)(2,1)S(1)} %copy-done.4, bf16[2,1024,128]{2,1,0:T(8,128)(2,1)S(1)} %collective-permute-done.refs_3_, ...), custom_call_target="tpu_custom_call" | custom-call | flops 4945084416 | bytes 6291456 | tf_op jit(solution)/shard_map/pallas_call | solution.py:211
  23.9 0.0 collective-permute-done.3.zr.refs_6_
  23.9 0.5 %collective-permute-done.2.zl.refs_5_ = bf16[8,288,128]{2,1,0:T(8,128)(2,1)S(1)} collective-permute-done((bf16[8,288,128]{2,1,0:T(8,128)(2,1)}, bf16[8,288,128]{2,1,0:T(8,128)(2,1)S(1)}, u32[]{:S(2)}, u32[]{:S(2)}) %collective-permute-start.2) | collective-permute-done | bytes 589856 | tf_op jit(solution)/shard_map/ppermute | solution.py:323
  24.5 0.8 %shard_map.48 = (bf16[2,320,128]{2,1,0:T(8,128)(2,1)S(1)}, bf16[2,320,128]{2,1,0:T(8,128)(2,1)S(1)}) custom-call(s32[7]{0:T(128)S(1)} %copy-done, bf16[8,288,128]{2,1,0:T(8,128)(2,1)S(1)} %collective-permute-done.2.zl.refs_5_, bf16[8,32,128]{2,1,0:T(8,128)(2,1)S(1)} %collective-permute-done.3.zr.refs_6_, bf16[16,128]{1,0:T(8,128)(2,1)S(1)} %get-tuple-element.17._), custom_call_target="tpu_custom_call" | custom-call | flops 8589934592 | bytes 1024 | tf_op jit(solution)/shard_map/pallas_call | solution.py:299
  25.3 1.4 %collective-permute-start.4 = (bf16[2,320,128]{2,1,0:T(8,128)(2,1)S(1)}, bf16[2,320,128]{2,1,0:T(8,128)(2,1)S(1)}, u32[]{:S(2)}, u32[]{:S(2)}) collective-permute-start(bf16[2,320,128]{2,1,0:T(8,128)(2,1)S(1)} %get-tuple-element.18), channel_id=1, source_target_pairs={{0,1},{1,0},{2,3},{3,2},{4,5},{5,4},{6,7},{7,6},{8,9},{9,8},{10,11... | collective-permute-start | bytes 491528 | tf_op jit(solution)/shard_map/ppermute | solution.py:229
  26.7 2.1 %collective-permute-start.5 = (bf16[2,320,128]{2,1,0:T(8,128)(2,1)S(1)}, bf16[2,320,128]{2,1,0:T(8,128)(2,1)S(1)}, u32[]{:S(2)}, u32[]{:S(2)}) collective-permute-start(bf16[2,320,128]{2,1,0:T(8,128)(2,1)S(1)} %get-tuple-element.19), channel_id=1, source_target_pairs={{1,2},{2,1},{5,6},{6,5},{9,10},{10,9},{13,14},{14,13},{17,18},{18,... | collective-permute-start | bytes 491528 | tf_op jit(solution)/shard_map/ppermute | solution.py:229
  28.8 0.0 collective-permute-done.4.refs_7_
  28.8 4.5 %collective-permute-done.5.refs_8_ = bf16[2,320,128]{2,1,0:T(8,128)(2,1)S(1)} collective-permute-done((bf16[2,320,128]{2,1,0:T(8,128)(2,1)S(1)}, bf16[2,320,128]{2,1,0:T(8,128)(2,1)S(1)}, u32[]{:S(2)}, u32[]{:S(2)}) %collective-permute-start.5) | collective-permute-done | bytes 163872 | tf_op jit(solution)/shard_map/ppermute | solution.py:229
  33.3 11.1 %shard_map.49 = bf16[8,512,256]{2,1,0:T(8,128)(2,1)} custom-call(s32[7]{0:T(128)S(1)} %copy-done, bf16[8,512,128]{2,1,0:T(8,128)(2,1)S(1)} %copy-done.3, bf16[8,512,128]{2,1,0:T(8,128)(2,1)S(1)} %copy-done.4, bf16[2,1024,128]{2,1,0:T(8,128)(2,1)S(1)} %collective-permute-done.refs_3_, ...), custom_call_target="tpu_custom_call", output_to_operand_aliasing={{}: (11, {})} | custom-call | flops 6492782592 | bytes 6291456 | tf_op jit(solution)/shard_map/pallas_call | solution.py:211
  (3 shorter events, 0.0 us)
Async XLA Ops:
  0.6 15.2 %copy-start = (s32[7]{0:T(128)S(1)}, s32[7]{0:T(128)}, u32[]{:S(2)}) copy-start(s32[7]{0:T(128)} %stack.47.flags.refs_0_) | copy-start | bytes 88
  0.6 15.2 %copy-start.1 = (bf16[3,3,256,256]{3,2,1,0:T(8,128)(2,1)S(1)}, bf16[3,3,256,256]{3,2,1,0:T(8,128)(2,1)}, u32[]{:S(2)}) copy-start(bf16[3,3,256,256]{3,2,1,0:T(8,128)(2,1)} %param.6) | copy-start | bytes 3538948
  0.6 15.2 %copy-start.2 = (bf16[3,3,256,256]{3,2,1,0:T(8,128)(2,1)S(1)}, bf16[3,3,256,256]{3,2,1,0:T(8,128)(2,1)}, u32[]{:S(2)}) copy-start(bf16[3,3,256,256]{3,2,1,0:T(8,128)(2,1)} %param.7) | copy-start | bytes 3538948
  0.6 15.2 %copy-start.3 = (bf16[8,512,128]{2,1,0:T(8,128)(2,1)S(1)}, bf16[8,512,128]{2,1,0:T(8,128)(2,1)}, u32[]{:S(2)}) copy-start(bf16[8,512,128]{2,1,0:T(8,128)(2,1)} %refs_1_.3) | copy-start | bytes 3145732
  0.6 15.2 %copy-start.4 = (bf16[8,512,128]{2,1,0:T(8,128)(2,1)S(1)}, bf16[8,512,128]{2,1,0:T(8,128)(2,1)}, u32[]{:S(2)}) copy-start(bf16[8,512,128]{2,1,0:T(8,128)(2,1)} %refs_2_.3) | copy-start | bytes 3145732
  4.1 11.6 %collective-permute-start = (bf16[2,1024,128]{2,1,0:T(8,128)(2,1)}, bf16[2,1024,128]{2,1,0:T(8,128)(2,1)S(1)}, u32[]{:S(2)}, u32[]{:S(2)}) collective-permute-start(bf16[2,1024,128]{2,1,0:T(8,128)(2,1)} %get-tuple-element.13), channel_id=1, source_target_pairs={{1,2},{2,1},{5,6},{6,5},{9,10},{10,9},{13,14},{14,13},{17,18},{18,... | collective-permute-start | bytes 1572872 | tf_op jit(solution)/shard_map/ppermute | solution.py:229
  8.7 7.1 %collective-permute-start.1 = (bf16[2,1024,128]{2,1,0:T(8,128)(2,1)}, bf16[2,1024,128]{2,1,0:T(8,128)(2,1)S(1)}, u32[]{:S(2)}, u32[]{:S(2)}) collective-permute-start(bf16[2,1024,128]{2,1,0:T(8,128)(2,1)} %get-tuple-element.14), channel_id=1, source_target_pairs={{0,1},{1,0},{2,3},{3,2},{4,5},{5,4},{6,7},{7,6},{8,9},{9,8},{10,11... | collective-permute-start | bytes 1572872 | tf_op jit(solution)/shard_map/ppermute | solution.py:229
  8.7 15.7 %collective-permute-start.2 = (bf16[8,288,128]{2,1,0:T(8,128)(2,1)}, bf16[8,288,128]{2,1,0:T(8,128)(2,1)S(1)}, u32[]{:S(2)}, u32[]{:S(2)}) collective-permute-start(bf16[8,288,128]{2,1,0:T(8,128)(2,1)} %get-tuple-element.15), channel_id=1, source_target_pairs={{0,4},{4,8},{8,12},{1,5},{5,9},{9,13},{2,6},{6,10},{10,14},{3,7},{... | collective-permute-start | bytes 1769480 | tf_op jit(solution)/shard_map/ppermute | solution.py:323
  12.0 11.9 %collective-permute-start.3 = (bf16[8,32,128]{2,1,0:T(8,128)(2,1)}, bf16[8,32,128]{2,1,0:T(8,128)(2,1)S(1)}, u32[]{:S(2)}, u32[]{:S(2)}) collective-permute-start(bf16[8,32,128]{2,1,0:T(8,128)(2,1)} %get-tuple-element.16), channel_id=1, source_target_pairs={{4,0},{8,4},{12,8},{5,1},{9,5},{13,9},{6,2},{10,6},{14,10},{7,3},{... | collective-permute-start | bytes 196616 | tf_op jit(solution)/shard_map/ppermute | solution.py:326
  25.3 3.5 %collective-permute-start.4 = (bf16[2,320,128]{2,1,0:T(8,128)(2,1)S(1)}, bf16[2,320,128]{2,1,0:T(8,128)(2,1)S(1)}, u32[]{:S(2)}, u32[]{:S(2)}) collective-permute-start(bf16[2,320,128]{2,1,0:T(8,128)(2,1)S(1)} %get-tuple-element.18), channel_id=1, source_target_pairs={{0,1},{1,0},{2,3},{3,2},{4,5},{5,4},{6,7},{7,6},{8,9},{9,8},{10,11... | collective-permute-start | bytes 491528 | tf_op jit(solution)/shard_map/ppermute | solution.py:229
  26.7 6.6 %collective-permute-start.5 = (bf16[2,320,128]{2,1,0:T(8,128)(2,1)S(1)}, bf16[2,320,128]{2,1,0:T(8,128)(2,1)S(1)}, u32[]{:S(2)}, u32[]{:S(2)}) collective-permute-start(bf16[2,320,128]{2,1,0:T(8,128)(2,1)S(1)} %get-tuple-element.19), channel_id=1, source_target_pairs={{1,2},{2,1},{5,6},{6,5},{9,10},{10,9},{13,14},{14,13},{17,18},{18,... | collective-permute-start | bytes 491528 | tf_op jit(solution)/shard_map/ppermute | solution.py:229
